TPU v7x, 512 devices: a whole 4x8x8 slice. The times are simulated.
512 devices in a mesh: tm: 16 (over y, core), space: 32 (over x, z).
Axes of the slice: x: 4, y: 8, z: 8, core: 2. Of those that a mesh axis runs over, the one named last changes fastest.
Arguments:
- initial_state: float32 [3, 256, 32, 128], P(None, 'space'), may hold values from -4 to 4
- guess: float32 [16, 3, 256, 32, 128], P('tm', None, 'space'), may hold values from -4 to 4
- soil_kind_index: int32 [256, 32, 128], P('space'), may hold values from 0 to 3
Outputs:
- corrected: float32 [16, 3, 256, 32, 128], P('tm', None, 'space')
- relaxed: float32 [16, 3, 256, 32, 128], P('tm', None, 'space')
All inputs are finite; a program needn't handle non-finite values.
Results may differ from a plain program's by a relative error of at most 0.00002.
Values sent between devices are 32-bit elements; how exact they have to be, the bound alone decides.
No kernel may reach another device: no remote copies, remote signals or barrier semaphores. Data moves between devices by JAX's collectives and lax.ppermute only.
A program may use at most 64 MiB of HBM per device.

v0:
```python
import jax
import jax.numpy as jnp
from jax import lax
from jax.sharding import PartitionSpec as P

RATIO = 8


KAPPA = (0.05, 0.08, 0.12, 0.15)
PORE_DIFF = (0.1, 0.04, 0.15, 0.07)
ENERGY = (0.5, 1.0, 1.5, 2.0)
FLUIDITY = (0.2, 0.35, 0.15, 0.3)
STRENGTH = (1.0, 0.6, 1.4, 0.8)
FRICTION_WARMING = 0.3
DRAINAGE = 0.5
DILATANCY = 0.4
TIME_STEP = 0.02


def with_halo(shard, sides, width):
    for axis, dim in sides:
        size, length = (lax.axis_size(axis), shard.shape[dim])
        up = [(i, (i + 1) % size) for i in range(size - 1)]
        down = [(j, i) for i, j in up]
        last = lax.slice_in_dim(shard, length - width, length, axis=dim)
        initial = lax.slice_in_dim(shard, 0, width, axis=dim)
        before = lax.ppermute(last, axis, up)
        after = lax.ppermute(initial, axis, down)
        shard = jnp.concatenate([before, shard, after], axis=dim)
    return shard


def from_behind(shard, axis, by):
    length = lax.axis_size(axis)
    pairs = [(i, i + by) for i in range(length) if 0 <= i + by < length]
    return lax.ppermute(shard, axis, pairs)


def lookup(soil_kind_index, table):
    looked = jnp.full(soil_kind_index.shape, table[0], jnp.float32)
    for entry in range(1, len(table)):
        looked = jnp.where(soil_kind_index == entry, jnp.float32(table[entry]), looked)
    return looked


def march_solution(
    heat_level_map,
    irreversible_deformation,
    water_stress,
    heat_level_curvature,
    water_stress_curvature,
    soil_kind_index,
    forward_euler_update,
):
    heat_diffusion_map = lookup(soil_kind_index, KAPPA)
    pore_map = lookup(soil_kind_index, PORE_DIFF)
    warmth_content = lookup(soil_kind_index, ENERGY)
    fluidity = lookup(soil_kind_index, FLUIDITY)
    strength = lookup(soil_kind_index, STRENGTH)
    activation_multiplier = jnp.exp(warmth_content * (1.0 - 1.0 / (1.5 + jnp.tanh(heat_level_map))))
    yielding_velocity = (
        fluidity * activation_multiplier * jax.nn.softplus(strength - 0.5 * water_stress)
    )
    next_heat_level = heat_level_map + forward_euler_update * (
        heat_diffusion_map * heat_level_curvature + FRICTION_WARMING * yielding_velocity
    )
    next_irreversible_deformation = (
        irreversible_deformation + forward_euler_update * yielding_velocity
    )
    next_water_stress = water_stress + forward_euler_update * (
        pore_map * water_stress_curvature - DRAINAGE * water_stress - DILATANCY * yielding_velocity
    )
    return (next_heat_level, next_irreversible_deformation, next_water_stress)


def box_sum(field, along):
    margins = [(0, 0)] * field.ndim
    margins[along] = (1, 1)
    padded = jnp.pad(field, margins)
    length = field.shape[along]
    return (
        lax.slice_in_dim(padded, 0, length, axis=along)
        + lax.slice_in_dim(padded, 1, length + 1, axis=along)
        + lax.slice_in_dim(padded, 2, length + 2, axis=along)
    )


def x_sum(padded):
    return padded[:, :, :-2] + padded[:, :, 1:-1] + padded[:, :, 2:]


def step_once(fields, soil_kind_index, forward_euler_update):
    diffusing = jnp.stack([fields[:, 0], fields[:, 2]], 1)
    padded = with_halo(diffusing, (("space", 2),), 1)
    boxed = box_sum(box_sum(x_sum(padded), 3), 4)
    lapl = boxed - 27.0 * diffusing
    new = march_solution(
        fields[:, 0],
        fields[:, 1],
        fields[:, 2],
        lapl[:, 0],
        lapl[:, 1],
        soil_kind_index,
        forward_euler_update,
    )
    return jnp.stack(new, 1)


def on_device(initial_state, guess, soil_kind_index):
    position = lax.axis_index("tm")
    is_first = position == 0
    coarse_dt = RATIO * TIME_STEP

    def advance(fields):
        return lax.fori_loop(
            0, RATIO, lambda turn, current: step_once(current, soil_kind_index, TIME_STEP), fields
        )

    prior = from_behind(guess, "tm", 1)
    head = jnp.where(is_first, initial_state[None], prior)
    starts = jnp.concatenate([head, guess[:-1]], 0)
    relaxed = advance(starts)
    prior_two = from_behind(relaxed, "tm", 1)
    head_two = jnp.where(is_first, initial_state[None], prior_two)
    second = jnp.concatenate([head_two, relaxed[:-1]], 0)
    propagated = advance(second)
    defect = propagated - step_once(second, soil_kind_index, coarse_dt)

    def chain(current, term):
        following = step_once(current, soil_kind_index, coarse_dt) + term[None]
        return (following, following[0])

    def relay_turn(turn, current):
        incoming = from_behind(current, "tm", 1)
        start = jnp.where(is_first, initial_state[None], incoming)
        unused, chained = lax.scan(chain, start, defect)
        return chained

    corrected = lax.fori_loop(0, lax.axis_size("tm"), relay_turn, jnp.zeros_like(guess))
    return (corrected, relaxed)


def solution(mesh):
    placed = (
        P(None, "space", None, None),
        P("tm", None, "space", None, None),
        P("space", None, None),
    )
    return jax.shard_map(
        on_device,
        mesh=mesh,
        in_specs=placed,
        out_specs=(P("tm", None, "space", None, None), P("tm", None, "space", None, None)),
        check_vma=False,
    )
```

profile of v0, /device:TPU:36, one launch (start us, length us, event | category | flops | bytes accessed | tf_op | source)
XLA Modules:
  0.0 549.2 jit_solution(16510008736023079563)
XLA Ops:
  2.6 8.6 %collective-permute-done.7 = f32[1,3,8,32,128]{4,3,2,1,0:T(8,128)S(1)} collective-permute-done((f32[1,3,8,32,128]{4,3,2,1,0:T(8,128)}, f32[1,3,8,32,128]{4,3,2,1,0:T(8,128)S(1)}, u32[]{:S(2)}, u32[]{:S(2)}) %collective-permute-start.7) | collective-permute-done | bytes 393248 | tf_op jit(solution)/shard_map/ppermute | solution.py:36
  12.2 93.9 %while.42 = (s32[]{:T(128)}, f32[1,3,8,32,128]{4,3,2,1,0:T(8,128)S(1)}, s32[8,32,128]{2,1,0:T(8,128)S(1)}, s32[]{:T(128)}) while((s32[]{:T(128)}, f32[1,3,8,32,128]{4,3,2,1,0:T(8,128)S(1)}, s32[8,32,128]{2,1,0:T(8,128)S(1)}, s32[]{:T(128)}) %tuple.139), condition=%wide.region_1.2_spmd, body=%wide.region_0.1_spmd.sunk | while | flops 2637826 | bytes 5570693 | solution.py:115
  12.3 11.1 %collective-permute-start = (f32[1,2,1,32,128]{4,3,2,1,0:T(8,128)S(1)}, f32[1,2,1,32,128]{4,3,2,1,0:T(8,128)S(1)}, u32[]{:S(2)}, u32[]{:S(2)}) collective-permute-start(f32[1,2,1,32,128]{4,3,2,1,0:T(8,128)S(1)} %get-tuple-element.369), channel_id=1, source_target_pairs={{1,0},{2,1},{3,2},{4,3},{5,4},{6,5},{7,6},{8,7},{9,8},{10,9},{11,1... | collective-permute-start | bytes 98312 | tf_op jit(solution)/shard_map/while/body/eval_jaxpr/ppermute | solution.py:28
  25.3 6.0 %collective-permute-done.1 = f32[1,2,1,32,128]{4,3,2,1,0:T(8,128)S(1)} collective-permute-done((f32[1,2,1,32,128]{4,3,2,1,0:T(8,128)S(1)}, f32[1,2,1,32,128]{4,3,2,1,0:T(8,128)S(1)}, u32[]{:S(2)}, u32[]{:S(2)}) %collective-permute-start.1) | collective-permute-done | bytes 32800 | tf_op jit(solution)/shard_map/while/body/eval_jaxpr/ppermute | solution.py:27
  48.5 4.0 collective-permute-done.1
  69.6 4.0 collective-permute-done.1
  80.2 4.0 collective-permute-done.1
  101.4 4.0 collective-permute-done.1
  108.0 8.4 %collective-permute-done.8 = f32[1,3,8,32,128]{4,3,2,1,0:T(8,128)S(1)} collective-permute-done((f32[1,3,8,32,128]{4,3,2,1,0:T(8,128)S(1)}, f32[1,3,8,32,128]{4,3,2,1,0:T(8,128)S(1)}, u32[]{:S(2)}, u32[]{:S(2)}) %collective-permute-start.8) | collective-permute-done | bytes 393248 | tf_op jit(solution)/shard_map/ppermute | solution.py:36
  127.0 84.9 %while.43 = (s32[]{:T(128)}, f32[1,3,8,32,128]{4,3,2,1,0:T(8,128)S(1)}, s32[8,32,128]{2,1,0:T(8,128)S(1)}, s32[]{:T(128)}) while((s32[]{:T(128)}, f32[1,3,8,32,128]{4,3,2,1,0:T(8,128)S(1)}, s32[8,32,128]{2,1,0:T(8,128)S(1)}, s32[]{:T(128)}) %tuple.140), condition=%wide.region_3.4_spmd, body=%wide.region_2.3_spmd.sunk | while | flops 2637826 | bytes 5570693 | solution.py:115
  154.1 4.0 collective-permute-done.3
  164.9 4.0 collective-permute-done.3
  175.5 4.0 collective-permute-done.3
  196.7 4.0 collective-permute-done.3
  212.0 336.4 %while.44 = (s32[]{:T(128)}, f32[1,3,8,32,128]{4,3,2,1,0:T(8,128)S(1)}, pred[]{:T(512)}, f32[3,8,32,128]{3,2,1,0:T(8,128)S(1)}, s32[8,32,128]{2,1,0:T(8,128)S(1)...) while((s32[]{:T(128)}, f32[1,3,8,32,128]{4,3,2,1,0:T(8,128)S(1)}, pred[]{:T(512)}, ...), condition=%wide.region_5.6_spmd.clone, body=%wide.region_4.5_spmd.clone.sunk | while | flops 2932739 | bytes 9502936 | solution.py:139
  214.0 8.4 %collective-permute-done.4 = f32[1,3,8,32,128]{4,3,2,1,0:T(8,128)S(1)} collective-permute-done((f32[1,3,8,32,128]{4,3,2,1,0:T(8,128)S(1)}, f32[1,3,8,32,128]{4,3,2,1,0:T(8,128)S(1)}, u32[]{:S(2)}, u32[]{:S(2)}) %collective-permute-start.4) | collective-permute-done | bytes 393248 | tf_op jit(solution)/shard_map/while/body/eval_jaxpr/ppermute | solution.py:36
  228.4 4.0 collective-permute-done.6
  235.0 8.4 %collective-permute-done.4 = f32[1,3,8,32,128]{4,3,2,1,0:T(8,128)S(1)} collective-permute-done((f32[1,3,8,32,128]{4,3,2,1,0:T(8,128)S(1)}, f32[1,3,8,32,128]{4,3,2,1,0:T(8,128)S(1)}, u32[]{:S(2)}, u32[]{:S(2)}) %collective-permute-start.4) | collective-permute-done | bytes 393248 | tf_op jit(solution)/shard_map/while/body/eval_jaxpr/ppermute | solution.py:36
  256.1 8.4 %collective-permute-done.4 = f32[1,3,8,32,128]{4,3,2,1,0:T(8,128)S(1)} collective-permute-done((f32[1,3,8,32,128]{4,3,2,1,0:T(8,128)S(1)}, f32[1,3,8,32,128]{4,3,2,1,0:T(8,128)S(1)}, u32[]{:S(2)}, u32[]{:S(2)}) %collective-permute-start.4) | collective-permute-done | bytes 393248 | tf_op jit(solution)/shard_map/while/body/eval_jaxpr/ppermute | solution.py:36
  277.1 8.4 %collective-permute-done.4 = f32[1,3,8,32,128]{4,3,2,1,0:T(8,128)S(1)} collective-permute-done((f32[1,3,8,32,128]{4,3,2,1,0:T(8,128)S(1)}, f32[1,3,8,32,128]{4,3,2,1,0:T(8,128)S(1)}, u32[]{:S(2)}, u32[]{:S(2)}) %collective-permute-start.4) | collective-permute-done | bytes 393248 | tf_op jit(solution)/shard_map/while/body/eval_jaxpr/ppermute | solution.py:36
  298.1 8.4 %collective-permute-done.4 = f32[1,3,8,32,128]{4,3,2,1,0:T(8,128)S(1)} collective-permute-done((f32[1,3,8,32,128]{4,3,2,1,0:T(8,128)S(1)}, f32[1,3,8,32,128]{4,3,2,1,0:T(8,128)S(1)}, u32[]{:S(2)}, u32[]{:S(2)}) %collective-permute-start.4) | collective-permute-done | bytes 393248 | tf_op jit(solution)/shard_map/while/body/eval_jaxpr/ppermute | solution.py:36
  319.1 8.4 %collective-permute-done.4 = f32[1,3,8,32,128]{4,3,2,1,0:T(8,128)S(1)} collective-permute-done((f32[1,3,8,32,128]{4,3,2,1,0:T(8,128)S(1)}, f32[1,3,8,32,128]{4,3,2,1,0:T(8,128)S(1)}, u32[]{:S(2)}, u32[]{:S(2)}) %collective-permute-start.4) | collective-permute-done | bytes 393248 | tf_op jit(solution)/shard_map/while/body/eval_jaxpr/ppermute | solution.py:36
  340.2 8.4 %collective-permute-done.4 = f32[1,3,8,32,128]{4,3,2,1,0:T(8,128)S(1)} collective-permute-done((f32[1,3,8,32,128]{4,3,2,1,0:T(8,128)S(1)}, f32[1,3,8,32,128]{4,3,2,1,0:T(8,128)S(1)}, u32[]{:S(2)}, u32[]{:S(2)}) %collective-permute-start.4) | collective-permute-done | bytes 393248 | tf_op jit(solution)/shard_map/while/body/eval_jaxpr/ppermute | solution.py:36
  361.2 8.4 %collective-permute-done.4 = f32[1,3,8,32,128]{4,3,2,1,0:T(8,128)S(1)} collective-permute-done((f32[1,3,8,32,128]{4,3,2,1,0:T(8,128)S(1)}, f32[1,3,8,32,128]{4,3,2,1,0:T(8,128)S(1)}, u32[]{:S(2)}, u32[]{:S(2)}) %collective-permute-start.4) | collective-permute-done | bytes 393248 | tf_op jit(solution)/shard_map/while/body/eval_jaxpr/ppermute | solution.py:36
  382.2 8.4 %collective-permute-done.4 = f32[1,3,8,32,128]{4,3,2,1,0:T(8,128)S(1)} collective-permute-done((f32[1,3,8,32,128]{4,3,2,1,0:T(8,128)S(1)}, f32[1,3,8,32,128]{4,3,2,1,0:T(8,128)S(1)}, u32[]{:S(2)}, u32[]{:S(2)}) %collective-permute-start.4) | collective-permute-done | bytes 393248 | tf_op jit(solution)/shard_map/while/body/eval_jaxpr/ppermute | solution.py:36
  403.2 8.4 %collective-permute-done.4 = f32[1,3,8,32,128]{4,3,2,1,0:T(8,128)S(1)} collective-permute-done((f32[1,3,8,32,128]{4,3,2,1,0:T(8,128)S(1)}, f32[1,3,8,32,128]{4,3,2,1,0:T(8,128)S(1)}, u32[]{:S(2)}, u32[]{:S(2)}) %collective-permute-start.4) | collective-permute-done | bytes 393248 | tf_op jit(solution)/shard_map/while/body/eval_jaxpr/ppermute | solution.py:36
  424.3 8.4 %collective-permute-done.4 = f32[1,3,8,32,128]{4,3,2,1,0:T(8,128)S(1)} collective-permute-done((f32[1,3,8,32,128]{4,3,2,1,0:T(8,128)S(1)}, f32[1,3,8,32,128]{4,3,2,1,0:T(8,128)S(1)}, u32[]{:S(2)}, u32[]{:S(2)}) %collective-permute-start.4) | collective-permute-done | bytes 393248 | tf_op jit(solution)/shard_map/while/body/eval_jaxpr/ppermute | solution.py:36
  445.3 8.4 %collective-permute-done.4 = f32[1,3,8,32,128]{4,3,2,1,0:T(8,128)S(1)} collective-permute-done((f32[1,3,8,32,128]{4,3,2,1,0:T(8,128)S(1)}, f32[1,3,8,32,128]{4,3,2,1,0:T(8,128)S(1)}, u32[]{:S(2)}, u32[]{:S(2)}) %collective-permute-start.4) | collective-permute-done | bytes 393248 | tf_op jit(solution)/shard_map/while/body/eval_jaxpr/ppermute | solution.py:36
  466.3 8.4 %collective-permute-done.4 = f32[1,3,8,32,128]{4,3,2,1,0:T(8,128)S(1)} collective-permute-done((f32[1,3,8,32,128]{4,3,2,1,0:T(8,128)S(1)}, f32[1,3,8,32,128]{4,3,2,1,0:T(8,128)S(1)}, u32[]{:S(2)}, u32[]{:S(2)}) %collective-permute-start.4) | collective-permute-done | bytes 393248 | tf_op jit(solution)/shard_map/while/body/eval_jaxpr/ppermute | solution.py:36
  487.3 8.4 %collective-permute-done.4 = f32[1,3,8,32,128]{4,3,2,1,0:T(8,128)S(1)} collective-permute-done((f32[1,3,8,32,128]{4,3,2,1,0:T(8,128)S(1)}, f32[1,3,8,32,128]{4,3,2,1,0:T(8,128)S(1)}, u32[]{:S(2)}, u32[]{:S(2)}) %collective-permute-start.4) | collective-permute-done | bytes 393248 | tf_op jit(solution)/shard_map/while/body/eval_jaxpr/ppermute | solution.py:36
  508.4 8.4 %collective-permute-done.4 = f32[1,3,8,32,128]{4,3,2,1,0:T(8,128)S(1)} collective-permute-done((f32[1,3,8,32,128]{4,3,2,1,0:T(8,128)S(1)}, f32[1,3,8,32,128]{4,3,2,1,0:T(8,128)S(1)}, u32[]{:S(2)}, u32[]{:S(2)}) %collective-permute-start.4) | collective-permute-done | bytes 393248 | tf_op jit(solution)/shard_map/while/body/eval_jaxpr/ppermute | solution.py:36
  529.4 8.4 %collective-permute-done.4 = f32[1,3,8,32,128]{4,3,2,1,0:T(8,128)S(1)} collective-permute-done((f32[1,3,8,32,128]{4,3,2,1,0:T(8,128)S(1)}, f32[1,3,8,32,128]{4,3,2,1,0:T(8,128)S(1)}, u32[]{:S(2)}, u32[]{:S(2)}) %collective-permute-start.4) | collective-permute-done | bytes 393248 | tf_op jit(solution)/shard_map/while/body/eval_jaxpr/ppermute | solution.py:36
  (446 shorter events, 341.4 us)
Async XLA Ops:
  0.6 10.5 %collective-permute-start.7 = (f32[1,3,8,32,128]{4,3,2,1,0:T(8,128)}, f32[1,3,8,32,128]{4,3,2,1,0:T(8,128)S(1)}, u32[]{:S(2)}, u32[]{:S(2)}) collective-permute-start(f32[1,3,8,32,128]{4,3,2,1,0:T(8,128)} %param.10), channel_id=1, source_target_pairs={{0,32},{32,64},{64,96},{96,128},{128,160},{160,192},{192,224},{224... | collective-permute-start | bytes 1179656 | tf_op jit(solution)/shard_map/ppermute | solution.py:36
  12.3 13.0 %collective-permute-start = (f32[1,2,1,32,128]{4,3,2,1,0:T(8,128)S(1)}, f32[1,2,1,32,128]{4,3,2,1,0:T(8,128)S(1)}, u32[]{:S(2)}, u32[]{:S(2)}) collective-permute-start(f32[1,2,1,32,128]{4,3,2,1,0:T(8,128)S(1)} %get-tuple-element.369), channel_id=1, source_target_pairs={{1,0},{2,1},{3,2},{4,3},{5,4},{6,5},{7,6},{8,7},{9,8},{10,9},{11,1... | collective-permute-start | bytes 98312 | tf_op jit(solution)/shard_map/while/body/eval_jaxpr/ppermute | solution.py:28
  23.3 7.9 %collective-permute-start.1 = (f32[1,2,1,32,128]{4,3,2,1,0:T(8,128)S(1)}, f32[1,2,1,32,128]{4,3,2,1,0:T(8,128)S(1)}, u32[]{:S(2)}, u32[]{:S(2)}) collective-permute-start(f32[1,2,1,32,128]{4,3,2,1,0:T(8,128)S(1)} %get-tuple-element.370), channel_id=1, source_target_pairs={{0,1},{1,2},{2,3},{3,4},{4,5},{5,6},{6,7},{7,8},{8,9},{9,10},{10,1... | collective-permute-start | bytes 98312 | tf_op jit(solution)/shard_map/while/body/eval_jaxpr/ppermute | solution.py:27
  33.9 7.9 %collective-permute-start.1 = (f32[1,2,1,32,128]{4,3,2,1,0:T(8,128)S(1)}, f32[1,2,1,32,128]{4,3,2,1,0:T(8,128)S(1)}, u32[]{:S(2)}, u32[]{:S(2)}) collective-permute-start(f32[1,2,1,32,128]{4,3,2,1,0:T(8,128)S(1)} %get-tuple-element.370), channel_id=1, source_target_pairs={{0,1},{1,2},{2,3},{3,4},{4,5},{5,6},{6,7},{7,8},{8,9},{9,10},{10,1... | collective-permute-start | bytes 98312 | tf_op jit(solution)/shard_map/while/body/eval_jaxpr/ppermute | solution.py:27
  44.5 7.9 %collective-permute-start.1 = (f32[1,2,1,32,128]{4,3,2,1,0:T(8,128)S(1)}, f32[1,2,1,32,128]{4,3,2,1,0:T(8,128)S(1)}, u32[]{:S(2)}, u32[]{:S(2)}) collective-permute-start(f32[1,2,1,32,128]{4,3,2,1,0:T(8,128)S(1)} %get-tuple-element.370), channel_id=1, source_target_pairs={{0,1},{1,2},{2,3},{3,4},{4,5},{5,6},{6,7},{7,8},{8,9},{9,10},{10,1... | collective-permute-start | bytes 98312 | tf_op jit(solution)/shard_map/while/body/eval_jaxpr/ppermute | solution.py:27
  65.7 7.9 %collective-permute-start.1 = (f32[1,2,1,32,128]{4,3,2,1,0:T(8,128)S(1)}, f32[1,2,1,32,128]{4,3,2,1,0:T(8,128)S(1)}, u32[]{:S(2)}, u32[]{:S(2)}) collective-permute-start(f32[1,2,1,32,128]{4,3,2,1,0:T(8,128)S(1)} %get-tuple-element.370), channel_id=1, source_target_pairs={{0,1},{1,2},{2,3},{3,4},{4,5},{5,6},{6,7},{7,8},{8,9},{9,10},{10,1... | collective-permute-start | bytes 98312 | tf_op jit(solution)/shard_map/while/body/eval_jaxpr/ppermute | solution.py:27
  76.3 7.9 %collective-permute-start.1 = (f32[1,2,1,32,128]{4,3,2,1,0:T(8,128)S(1)}, f32[1,2,1,32,128]{4,3,2,1,0:T(8,128)S(1)}, u32[]{:S(2)}, u32[]{:S(2)}) collective-permute-start(f32[1,2,1,32,128]{4,3,2,1,0:T(8,128)S(1)} %get-tuple-element.370), channel_id=1, source_target_pairs={{0,1},{1,2},{2,3},{3,4},{4,5},{5,6},{6,7},{7,8},{8,9},{9,10},{10,1... | collective-permute-start | bytes 98312 | tf_op jit(solution)/shard_map/while/body/eval_jaxpr/ppermute | solution.py:27
  97.5 7.9 %collective-permute-start.1 = (f32[1,2,1,32,128]{4,3,2,1,0:T(8,128)S(1)}, f32[1,2,1,32,128]{4,3,2,1,0:T(8,128)S(1)}, u32[]{:S(2)}, u32[]{:S(2)}) collective-permute-start(f32[1,2,1,32,128]{4,3,2,1,0:T(8,128)S(1)} %get-tuple-element.370), channel_id=1, source_target_pairs={{0,1},{1,2},{2,3},{3,4},{4,5},{5,6},{6,7},{7,8},{8,9},{9,10},{10,1... | collective-permute-start | bytes 98312 | tf_op jit(solution)/shard_map/while/body/eval_jaxpr/ppermute | solution.py:27
  106.1 10.3 %collective-permute-start.8 = (f32[1,3,8,32,128]{4,3,2,1,0:T(8,128)S(1)}, f32[1,3,8,32,128]{4,3,2,1,0:T(8,128)S(1)}, u32[]{:S(2)}, u32[]{:S(2)}) collective-permute-start(f32[1,3,8,32,128]{4,3,2,1,0:T(8,128)S(1)} %get-tuple-element.175), channel_id=1, source_target_pairs={{0,32},{32,64},{64,96},{96,128},{128,160},{160,192},{192,224},{224... | collective-permute-start | bytes 1179656 | tf_op jit(solution)/shard_map/ppermute | solution.py:36
  118.5 7.9 %collective-permute-start.9 = (f32[1,2,1,32,128]{4,3,2,1,0:T(8,128)S(1)}, f32[1,2,1,32,128]{4,3,2,1,0:T(8,128)S(1)}, u32[]{:S(2)}, u32[]{:S(2)}) collective-permute-start(f32[1,2,1,32,128]{4,3,2,1,0:T(8,128)S(1)} %get-tuple-element.266), channel_id=1, source_target_pairs={{0,1},{1,2},{2,3},{3,4},{4,5},{5,6},{6,7},{7,8},{8,9},{9,10},{10,1... | collective-permute-start | bytes 98312 | tf_op jit(solution)/shard_map/ppermute | solution.py:27
  139.6 7.9 %collective-permute-start.3 = (f32[1,2,1,32,128]{4,3,2,1,0:T(8,128)S(1)}, f32[1,2,1,32,128]{4,3,2,1,0:T(8,128)S(1)}, u32[]{:S(2)}, u32[]{:S(2)}) collective-permute-start(f32[1,2,1,32,128]{4,3,2,1,0:T(8,128)S(1)} %get-tuple-element.384), channel_id=1, source_target_pairs={{0,1},{1,2},{2,3},{3,4},{4,5},{5,6},{6,7},{7,8},{8,9},{9,10},{10,1... | collective-permute-start | bytes 98312 | tf_op jit(solution)/shard_map/while/body/eval_jaxpr/ppermute | solution.py:27
  150.2 7.9 %collective-permute-start.3 = (f32[1,2,1,32,128]{4,3,2,1,0:T(8,128)S(1)}, f32[1,2,1,32,128]{4,3,2,1,0:T(8,128)S(1)}, u32[]{:S(2)}, u32[]{:S(2)}) collective-permute-start(f32[1,2,1,32,128]{4,3,2,1,0:T(8,128)S(1)} %get-tuple-element.384), channel_id=1, source_target_pairs={{0,1},{1,2},{2,3},{3,4},{4,5},{5,6},{6,7},{7,8},{8,9},{9,10},{10,1... | collective-permute-start | bytes 98312 | tf_op jit(solution)/shard_map/while/body/eval_jaxpr/ppermute | solution.py:27
  160.8 8.1 %collective-permute-start.3 = (f32[1,2,1,32,128]{4,3,2,1,0:T(8,128)S(1)}, f32[1,2,1,32,128]{4,3,2,1,0:T(8,128)S(1)}, u32[]{:S(2)}, u32[]{:S(2)}) collective-permute-start(f32[1,2,1,32,128]{4,3,2,1,0:T(8,128)S(1)} %get-tuple-element.384), channel_id=1, source_target_pairs={{0,1},{1,2},{2,3},{3,4},{4,5},{5,6},{6,7},{7,8},{8,9},{9,10},{10,1... | collective-permute-start | bytes 98312 | tf_op jit(solution)/shard_map/while/body/eval_jaxpr/ppermute | solution.py:27
  171.6 7.9 %collective-permute-start.3 = (f32[1,2,1,32,128]{4,3,2,1,0:T(8,128)S(1)}, f32[1,2,1,32,128]{4,3,2,1,0:T(8,128)S(1)}, u32[]{:S(2)}, u32[]{:S(2)}) collective-permute-start(f32[1,2,1,32,128]{4,3,2,1,0:T(8,128)S(1)} %get-tuple-element.384), channel_id=1, source_target_pairs={{0,1},{1,2},{2,3},{3,4},{4,5},{5,6},{6,7},{7,8},{8,9},{9,10},{10,1... | collective-permute-start | bytes 98312 | tf_op jit(solution)/shard_map/while/body/eval_jaxpr/ppermute | solution.py:27
  192.8 7.9 %collective-permute-start.3 = (f32[1,2,1,32,128]{4,3,2,1,0:T(8,128)S(1)}, f32[1,2,1,32,128]{4,3,2,1,0:T(8,128)S(1)}, u32[]{:S(2)}, u32[]{:S(2)}) collective-permute-start(f32[1,2,1,32,128]{4,3,2,1,0:T(8,128)S(1)} %get-tuple-element.384), channel_id=1, source_target_pairs={{0,1},{1,2},{2,3},{3,4},{4,5},{5,6},{6,7},{7,8},{8,9},{9,10},{10,1... | collective-permute-start | bytes 98312 | tf_op jit(solution)/shard_map/while/body/eval_jaxpr/ppermute | solution.py:27
  212.1 10.3 %collective-permute-start.4 = (f32[1,3,8,32,128]{4,3,2,1,0:T(8,128)S(1)}, f32[1,3,8,32,128]{4,3,2,1,0:T(8,128)S(1)}, u32[]{:S(2)}, u32[]{:S(2)}) collective-permute-start(f32[1,3,8,32,128]{4,3,2,1,0:T(8,128)S(1)} %broadcast_select_fusion.2), channel_id=1, source_target_pairs={{0,32},{32,64},{64,96},{96,128},{128,160},{160,192},{192,224},{224... | collective-permute-start | bytes 1179656 | tf_op jit(solution)/shard_map/while/body/eval_jaxpr/ppermute | solution.py:36
  224.4 7.9 %collective-permute-start.6 = (f32[1,2,1,32,128]{4,3,2,1,0:T(8,128)S(1)}, f32[1,2,1,32,128]{4,3,2,1,0:T(8,128)S(1)}, u32[]{:S(2)}, u32[]{:S(2)}) collective-permute-start(f32[1,2,1,32,128]{4,3,2,1,0:T(8,128)S(1)} %get-tuple-element.401), channel_id=1, source_target_pairs={{0,1},{1,2},{2,3},{3,4},{4,5},{5,6},{6,7},{7,8},{8,9},{9,10},{10,1... | collective-permute-start | bytes 98312 | tf_op jit(solution)/shard_map/while/body/eval_jaxpr/while/body/eval_jaxpr/ppermute | solution.py:27
  233.1 10.3 %collective-permute-start.4 = (f32[1,3,8,32,128]{4,3,2,1,0:T(8,128)S(1)}, f32[1,3,8,32,128]{4,3,2,1,0:T(8,128)S(1)}, u32[]{:S(2)}, u32[]{:S(2)}) collective-permute-start(f32[1,3,8,32,128]{4,3,2,1,0:T(8,128)S(1)} %broadcast_select_fusion.2), channel_id=1, source_target_pairs={{0,32},{32,64},{64,96},{96,128},{128,160},{160,192},{192,224},{224... | collective-permute-start | bytes 1179656 | tf_op jit(solution)/shard_map/while/body/eval_jaxpr/ppermute | solution.py:36
  254.1 10.3 %collective-permute-start.4 = (f32[1,3,8,32,128]{4,3,2,1,0:T(8,128)S(1)}, f32[1,3,8,32,128]{4,3,2,1,0:T(8,128)S(1)}, u32[]{:S(2)}, u32[]{:S(2)}) collective-permute-start(f32[1,3,8,32,128]{4,3,2,1,0:T(8,128)S(1)} %broadcast_select_fusion.2), channel_id=1, source_target_pairs={{0,32},{32,64},{64,96},{96,128},{128,160},{160,192},{192,224},{224... | collective-permute-start | bytes 1179656 | tf_op jit(solution)/shard_map/while/body/eval_jaxpr/ppermute | solution.py:36
  275.2 10.3 %collective-permute-start.4 = (f32[1,3,8,32,128]{4,3,2,1,0:T(8,128)S(1)}, f32[1,3,8,32,128]{4,3,2,1,0:T(8,128)S(1)}, u32[]{:S(2)}, u32[]{:S(2)}) collective-permute-start(f32[1,3,8,32,128]{4,3,2,1,0:T(8,128)S(1)} %broadcast_select_fusion.2), channel_id=1, source_target_pairs={{0,32},{32,64},{64,96},{96,128},{128,160},{160,192},{192,224},{224... | collective-permute-start | bytes 1179656 | tf_op jit(solution)/shard_map/while/body/eval_jaxpr/ppermute | solution.py:36
  296.2 10.3 %collective-permute-start.4 = (f32[1,3,8,32,128]{4,3,2,1,0:T(8,128)S(1)}, f32[1,3,8,32,128]{4,3,2,1,0:T(8,128)S(1)}, u32[]{:S(2)}, u32[]{:S(2)}) collective-permute-start(f32[1,3,8,32,128]{4,3,2,1,0:T(8,128)S(1)} %broadcast_select_fusion.2), channel_id=1, source_target_pairs={{0,32},{32,64},{64,96},{96,128},{128,160},{160,192},{192,224},{224... | collective-permute-start | bytes 1179656 | tf_op jit(solution)/shard_map/while/body/eval_jaxpr/ppermute | solution.py:36
  317.2 10.3 %collective-permute-start.4 = (f32[1,3,8,32,128]{4,3,2,1,0:T(8,128)S(1)}, f32[1,3,8,32,128]{4,3,2,1,0:T(8,128)S(1)}, u32[]{:S(2)}, u32[]{:S(2)}) collective-permute-start(f32[1,3,8,32,128]{4,3,2,1,0:T(8,128)S(1)} %broadcast_select_fusion.2), channel_id=1, source_target_pairs={{0,32},{32,64},{64,96},{96,128},{128,160},{160,192},{192,224},{224... | collective-permute-start | bytes 1179656 | tf_op jit(solution)/shard_map/while/body/eval_jaxpr/ppermute | solution.py:36
  338.2 10.3 %collective-permute-start.4 = (f32[1,3,8,32,128]{4,3,2,1,0:T(8,128)S(1)}, f32[1,3,8,32,128]{4,3,2,1,0:T(8,128)S(1)}, u32[]{:S(2)}, u32[]{:S(2)}) collective-permute-start(f32[1,3,8,32,128]{4,3,2,1,0:T(8,128)S(1)} %broadcast_select_fusion.2), channel_id=1, source_target_pairs={{0,32},{32,64},{64,96},{96,128},{128,160},{160,192},{192,224},{224... | collective-permute-start | bytes 1179656 | tf_op jit(solution)/shard_map/while/body/eval_jaxpr/ppermute | solution.py:36
  359.3 10.3 %collective-permute-start.4 = (f32[1,3,8,32,128]{4,3,2,1,0:T(8,128)S(1)}, f32[1,3,8,32,128]{4,3,2,1,0:T(8,128)S(1)}, u32[]{:S(2)}, u32[]{:S(2)}) collective-permute-start(f32[1,3,8,32,128]{4,3,2,1,0:T(8,128)S(1)} %broadcast_select_fusion.2), channel_id=1, source_target_pairs={{0,32},{32,64},{64,96},{96,128},{128,160},{160,192},{192,224},{224... | collective-permute-start | bytes 1179656 | tf_op jit(solution)/shard_map/while/body/eval_jaxpr/ppermute | solution.py:36
  380.3 10.3 %collective-permute-start.4 = (f32[1,3,8,32,128]{4,3,2,1,0:T(8,128)S(1)}, f32[1,3,8,32,128]{4,3,2,1,0:T(8,128)S(1)}, u32[]{:S(2)}, u32[]{:S(2)}) collective-permute-start(f32[1,3,8,32,128]{4,3,2,1,0:T(8,128)S(1)} %broadcast_select_fusion.2), channel_id=1, source_target_pairs={{0,32},{32,64},{64,96},{96,128},{128,160},{160,192},{192,224},{224... | collective-permute-start | bytes 1179656 | tf_op jit(solution)/shard_map/while/body/eval_jaxpr/ppermute | solution.py:36
  401.3 10.3 %collective-permute-start.4 = (f32[1,3,8,32,128]{4,3,2,1,0:T(8,128)S(1)}, f32[1,3,8,32,128]{4,3,2,1,0:T(8,128)S(1)}, u32[]{:S(2)}, u32[]{:S(2)}) collective-permute-start(f32[1,3,8,32,128]{4,3,2,1,0:T(8,128)S(1)} %broadcast_select_fusion.2), channel_id=1, source_target_pairs={{0,32},{32,64},{64,96},{96,128},{128,160},{160,192},{192,224},{224... | collective-permute-start | bytes 1179656 | tf_op jit(solution)/shard_map/while/body/eval_jaxpr/ppermute | solution.py:36
  422.3 10.3 %collective-permute-start.4 = (f32[1,3,8,32,128]{4,3,2,1,0:T(8,128)S(1)}, f32[1,3,8,32,128]{4,3,2,1,0:T(8,128)S(1)}, u32[]{:S(2)}, u32[]{:S(2)}) collective-permute-start(f32[1,3,8,32,128]{4,3,2,1,0:T(8,128)S(1)} %broadcast_select_fusion.2), channel_id=1, source_target_pairs={{0,32},{32,64},{64,96},{96,128},{128,160},{160,192},{192,224},{224... | collective-permute-start | bytes 1179656 | tf_op jit(solution)/shard_map/while/body/eval_jaxpr/ppermute | solution.py:36
  443.4 10.3 %collective-permute-start.4 = (f32[1,3,8,32,128]{4,3,2,1,0:T(8,128)S(1)}, f32[1,3,8,32,128]{4,3,2,1,0:T(8,128)S(1)}, u32[]{:S(2)}, u32[]{:S(2)}) collective-permute-start(f32[1,3,8,32,128]{4,3,2,1,0:T(8,128)S(1)} %broadcast_select_fusion.2), channel_id=1, source_target_pairs={{0,32},{32,64},{64,96},{96,128},{128,160},{160,192},{192,224},{224... | collective-permute-start | bytes 1179656 | tf_op jit(solution)/shard_map/while/body/eval_jaxpr/ppermute | solution.py:36
  464.4 10.3 %collective-permute-start.4 = (f32[1,3,8,32,128]{4,3,2,1,0:T(8,128)S(1)}, f32[1,3,8,32,128]{4,3,2,1,0:T(8,128)S(1)}, u32[]{:S(2)}, u32[]{:S(2)}) collective-permute-start(f32[1,3,8,32,128]{4,3,2,1,0:T(8,128)S(1)} %broadcast_select_fusion.2), channel_id=1, source_target_pairs={{0,32},{32,64},{64,96},{96,128},{128,160},{160,192},{192,224},{224... | collective-permute-start | bytes 1179656 | tf_op jit(solution)/shard_map/while/body/eval_jaxpr/ppermute | solution.py:36
  485.4 10.3 %collective-permute-start.4 = (f32[1,3,8,32,128]{4,3,2,1,0:T(8,128)S(1)}, f32[1,3,8,32,128]{4,3,2,1,0:T(8,128)S(1)}, u32[]{:S(2)}, u32[]{:S(2)}) collective-permute-start(f32[1,3,8,32,128]{4,3,2,1,0:T(8,128)S(1)} %broadcast_select_fusion.2), channel_id=1, source_target_pairs={{0,32},{32,64},{64,96},{96,128},{128,160},{160,192},{192,224},{224... | collective-permute-start | bytes 1179656 | tf_op jit(solution)/shard_map/while/body/eval_jaxpr/ppermute | solution.py:36
  506.4 10.3 %collective-permute-start.4 = (f32[1,3,8,32,128]{4,3,2,1,0:T(8,128)S(1)}, f32[1,3,8,32,128]{4,3,2,1,0:T(8,128)S(1)}, u32[]{:S(2)}, u32[]{:S(2)}) collective-permute-start(f32[1,3,8,32,128]{4,3,2,1,0:T(8,128)S(1)} %broadcast_select_fusion.2), channel_id=1, source_target_pairs={{0,32},{32,64},{64,96},{96,128},{128,160},{160,192},{192,224},{224... | collective-permute-start | bytes 1179656 | tf_op jit(solution)/shard_map/while/body/eval_jaxpr/ppermute | solution.py:36
  527.5 10.3 %collective-permute-start.4 = (f32[1,3,8,32,128]{4,3,2,1,0:T(8,128)S(1)}, f32[1,3,8,32,128]{4,3,2,1,0:T(8,128)S(1)}, u32[]{:S(2)}, u32[]{:S(2)}) collective-permute-start(f32[1,3,8,32,128]{4,3,2,1,0:T(8,128)S(1)} %broadcast_select_fusion.2), channel_id=1, source_target_pairs={{0,32},{32,64},{64,96},{96,128},{128,160},{160,192},{192,224},{224... | collective-permute-start | bytes 1179656 | tf_op jit(solution)/shard_map/while/body/eval_jaxpr/ppermute | solution.py:36
  (56 other events, 471.0 us)
where the time goes:
time: 552 us; the launch traced here: 549 us
  waiting for transfers between devices  285 us (52%)
  starting transfers between devices  235 us (43%)
  other arithmetic  24.9 us (5%)
    ppermute x18, waiting for transfers between devices, from_behind(): return lax.ppermute(shard, axis, pairs)  151 us
    ppermute x33, waiting for transfers between devices, with_halo(): before = lax.ppermute(last, axis, up)  133 us
    ppermute x33, starting transfers between devices, with_halo(): before = lax.ppermute(last, axis, up)  127 us
    ppermute x33, starting transfers between devices, with_halo(): after = lax.ppermute(initial, axis, down)  72.5 us
    ppermute x18, starting transfers between devices, from_behind(): return lax.ppermute(shard, axis, pairs)  34.6 us
  transfers between devices with their start and end apart: 84, of which 52 were waited for; matrix products, arithmetic and copies ran while one was open for 0% of the time, Pallas kernels for 0%

commit v1 on v0

v1 whole, which is shorter than its diff:
```python
import functools
import math

import jax
import jax.numpy as jnp
from jax import lax
from jax.experimental import pallas as pl
from jax.experimental.pallas import tpu as pltpu
from jax.sharding import PartitionSpec as P

RATIO = 8
KAPPA = (0.05, 0.08, 0.12, 0.15)
PORE_DIFF = (0.1, 0.04, 0.15, 0.07)
ENERGY = (0.5, 1.0, 1.5, 2.0)
FLUIDITY = (0.2, 0.35, 0.15, 0.3)
STRENGTH = (1.0, 0.6, 1.4, 0.8)
FRICTION_WARMING = 0.3
DRAINAGE = 0.5
DILATANCY = 0.4
TIME_STEP = 0.02
LOG2E = math.log2(math.e)
LN2 = math.log(2.0)

TILE = 8
EXT = 3 * TILE
STEPS_AHEAD = 7
VMEM = functools.partial(pl.BlockSpec, memory_space=pltpu.VMEM)
SMEM = functools.partial(pl.BlockSpec, memory_space=pltpu.SMEM)
F32 = jnp.float32


def load_rows(ref, *at):
    return [ref[(*at, pl.ds(r, 8, stride=4), slice(None))] for r in range(4)]


def store_rows(ref, rows, *at):
    for r in range(4):
        ref[(*at, pl.ds(r, 8, stride=4), slice(None))] = rows[r]


def load4(ref, *at):
    *lead, layer = at
    return [ref[(*lead, layer * 4 + r)] for r in range(4)]


def store4(ref, rows, *at):
    *lead, layer = at
    for r in range(4):
        ref[(*lead, layer * 4 + r)] = rows[r]


def edges():
    lane = lax.broadcasted_iota(jnp.int32, (8, 128), 1)
    sub = lax.broadcasted_iota(jnp.int32, (8, 128), 0)
    return lane == 0, lane == 127, sub == 0, sub == 7


def curvature(below, here, above, ends):
    lane0, lane127, sub0, sub7 = ends
    s = [a + b + c for a, b, c in zip(below, here, above)]
    first, second = s[0] + s[1], s[2] + s[3]
    before = jnp.where(sub0, 0.0, pltpu.roll(s[3], 1, 0))
    after = jnp.where(sub7, 0.0, pltpu.roll(s[0], 7, 0))
    columns = [before + first, first + s[2], s[1] + second, second + after]
    out = []
    for c, v in zip(columns, here):
        left = jnp.where(lane0, 0.0, pltpu.roll(c, 1, 1))
        right = jnp.where(lane127, 0.0, pltpu.roll(c, 127, 1))
        out.append((c + left + right) - 27.0 * v)
    return out


def increments(load, tabs, at, ends):
    here_t, here_w = load(0, 0), load(1, 0)
    curve_t = curvature(load(0, -1), here_t, load(0, 1), ends)
    curve_w = curvature(load(1, -1), here_w, load(1, 1), ends)
    hk, hc, c0, c1, s = (load4(tabs, i, at) for i in range(5))
    inc_t, inc_p, inc_w = [], [], []
    for r in range(4):
        warm = 1.0 / (1.5 + jnp.tanh(here_t[r]))
        x = s[r] - 0.5 * here_w[r]
        soft = jnp.maximum(x, 0.0) + LN2 * jnp.log2(1.0 + jnp.exp2(-LOG2E * jnp.abs(x)))
        flow = jnp.exp2(c0[r] - c1[r] * warm) * soft
        inc_t.append(hk[r] * curve_t[r] + FRICTION_WARMING * flow)
        inc_p.append(flow)
        inc_w.append(hc[r] * curve_w[r] - (DRAINAGE * TIME_STEP) * here_w[r] - DILATANCY * flow)
    return here_t, here_w, inc_t, inc_p, inc_w


def plus(a, b):
    return [x + y for x, y in zip(a, b)]


def make_tables(flag, soils, tabs):
    for part, load in enumerate(soils):
        def one(i, _):
            kinds = load(i)
            out = [[] for _ in range(5)]
            for kind in kinds:
                def pick(table):
                    got = jnp.full((8, 128), table[0], F32)
                    for entry in range(1, 4):
                        got = jnp.where(kind == float(entry), F32(table[entry]), got)
                    return got
                rows = [
                    pick([TIME_STEP * v for v in KAPPA]),
                    pick([TIME_STEP * v for v in PORE_DIFF]),
                    pick([LOG2E * e + math.log2(TIME_STEP * f) for e, f in zip(ENERGY, FLUIDITY)]),
                    pick([LOG2E * e for e in ENERGY]),
                    pick(STRENGTH),
                ]
                if part != 1:
                    inside = flag[0 if part == 0 else 1]
                    rows[0], rows[1], rows[3] = rows[0] * inside, rows[1] * inside, rows[3] * inside
                    rows[2] = rows[2] - 1000.0 * (1.0 - inside)
                for o, v in zip(out, rows):
                    o.append(v)
            for k in range(5):
                store4(tabs, out[k], k, part * TILE + i)
            return 0
        lax.fori_loop(0, TILE, one, 0)


def fine_steps(bufs, tabs, ps, finish, ends, first_extra=None):
    for t in range(RATIO):
        src, dst = bufs[t % 2], bufs[(t + 1) % 2]

        def one(l, _, t=t, src=src, dst=dst, tile=False):
            load = lambda f, d: load4(src, f, l + d)
            here_t, here_w, inc_t, inc_p, inc_w = increments(load, tabs, l, ends)
            new_t, new_w = plus(here_t, inc_t), plus(here_w, inc_w)
            if tile:
                i = l - TILE
                if t == 0:
                    store4(ps, inc_p, i)
                    if first_extra is not None:
                        first_extra(i, here_t, here_w, inc_t, inc_p, inc_w)
                else:
                    store4(ps, plus(load4(ps, i), inc_p), i)
            if t == RATIO - 1:
                finish(l - TILE, new_t, new_w)
            else:
                store4(dst, new_t, 0, l)
                store4(dst, new_w, 1, l)
            return 0

        if t < RATIO - 1:
            lax.fori_loop(1 + t, TILE, one, 0)
        lax.fori_loop(TILE, 2 * TILE, functools.partial(one, tile=True), 0)
        if t < RATIO - 1:
            lax.fori_loop(2 * TILE, EXT - 1 - t, one, 0)


def gather_ext(buf, left, centre, right, fields):
    def one(i, _):
        for f, (a, b, c) in enumerate(fields):
            store4(buf, load_rows(left, a, i), f, i)
            store4(buf, load_rows(centre, b, i), f, TILE + i)
            store4(buf, load_rows(right, c, i), f, 2 * TILE + i)
        return 0
    lax.fori_loop(0, TILE, one, 0)


def relax_kernel(flag, centre, pressure, left, right, soil, out, tabs, a, b, ps):
    ends = edges()
    make_tables(
        flag,
        (
            lambda i: load_rows(left, 2, i),
            lambda i: [k.astype(F32) for k in load_rows(soil, i)],
            lambda i: load_rows(right, 2, i),
        ),
        tabs,
    )
    gather_ext(a, left, centre, right, ((0, 0, 0), (1, 1, 1)))

    def finish(i, theta, w):
        store_rows(out, theta, 0, i)
        store_rows(out, w, 2, i)

    fine_steps((a, b), tabs, ps, finish, ends)

    def strain(i, _):
        store_rows(out, plus(load_rows(pressure, i), load4(ps, i)), 1, i)
        return 0
    lax.fori_loop(0, TILE, strain, 0)


def defect_kernel(flag, centre, left, right, tabs, out, out_p, a, b, ps, coarse):
    ends = edges()
    gather_ext(a, left, centre, right, ((0, 0, 0), (1, 2, 1)))
    later = 1.0 - flag[2]

    def first_extra(i, here_t, here_w, inc_t, inc_p, inc_w):
        store4(coarse, [later * (v + RATIO * d) for v, d in zip(here_t, inc_t)], 0, i)
        store4(coarse, [(later * RATIO) * d for d in inc_p], 1, i)
        store4(coarse, [later * (v + RATIO * d) for v, d in zip(here_w, inc_w)], 2, i)

    def finish(i, theta, w):
        store_rows(out, [v - g for v, g in zip(theta, load4(coarse, 0, i))], 0, i)
        store_rows(out, [v - g for v, g in zip(w, load4(coarse, 2, i))], 1, i)

    fine_steps((a, b), tabs, ps, finish, ends, first_extra)

    def strain(i, _):
        rows = zip(load_rows(centre, 1, i), load4(ps, i), load4(coarse, 1, i))
        store_rows(out_p, [flag[2] * p + (s - g) for p, s, g in rows], i)
        return 0
    lax.fori_loop(0, TILE, strain, 0)


def coarse_kernel(halo, state, tabs, left, centre, right, strain, held, out, out_p, out_held):
    ends = edges()
    new = halo - 1

    def one(o, _, kind=None):
        i = o + 1
        at = TILE - halo + i
        load = lambda f, d: load_rows(state, f, i + d)
        here_t, here_w, inc_t, inc_p, inc_w = increments(load, tabs, at, ends)
        if kind == 0:
            d, j = left, o + STEPS_AHEAD - new
        elif kind == 1:
            d, j = centre, o - new
            store_rows(out_p, [p + RATIO * v for p, v in zip(load_rows(strain, j), inc_p)], j)
            store_rows(out_held, plus(load_rows(held, 0, j), here_t), 0, j)
            store_rows(out_held, plus(load_rows(held, 1, j), here_w), 1, j)
        else:
            d, j = right, o - new - TILE
        store_rows(out, [(v + RATIO * x) + e for v, x, e in zip(here_t, inc_t, load_rows(d, 0, j))], 0, o)
        store_rows(out, [(v + RATIO * x) + e for v, x, e in zip(here_w, inc_w, load_rows(d, 1, j))], 1, o)
        return 0

    if new:
        lax.fori_loop(0, new, functools.partial(one, kind=0), 0)
    lax.fori_loop(new, new + TILE, functools.partial(one, kind=1), 0)
    if new:
        lax.fori_loop(new + TILE, 2 * new + TILE, functools.partial(one, kind=2), 0)


def call(kernel, outs, scratch, n_in, smem_first=True, **kw):
    specs = [VMEM() for _ in range(n_in)]
    if smem_first:
        specs[0] = SMEM()
    return pl.pallas_call(
        kernel,
        out_shape=[jax.ShapeDtypeStruct(s, F32) for s in outs],
        in_specs=specs,
        out_specs=[VMEM() for _ in outs],
        scratch_shapes=[pltpu.VMEM(s, F32) for s in scratch],
        compiler_params=pltpu.CompilerParams(vmem_limit_bytes=24 * 2**20),
        **kw,
    )


LAYER = (32, 128)
REGS = (8, 128)


def on_device(nt, ns, initial_state, guess, soil):
    t, s = lax.axis_index("tm"), lax.axis_index("space")
    flag = jnp.stack([s > 0, s < ns - 1, t == 0]).astype(F32)
    both = ("tm", "space")

    def shifted(x, dt, ds, only=None):
        pairs = []
        for a in range(nt) if only is None else only:
            for b in range(ns):
                if 0 <= b + ds < ns:
                    pairs.append((a * ns + b, (a + dt) % nt * ns + b + ds))
        return lax.ppermute(x, both, pairs)

    mine = jnp.where(t == nt - 1, initial_state, guess[0])
    heat_stress = jnp.stack([mine[0], mine[2]])
    packed = jnp.concatenate([heat_stress, soil.astype(F32)[None]])
    from_left = shifted(packed, 1, 1)
    from_right = shifted(packed, 1, -1)
    centre = shifted(heat_stress, 1, 0)
    pressure = shifted(mine[1], 1, 0)
    relaxed, tabs = call(
        relax_kernel,
        [(3, TILE, *LAYER), (5, EXT * 4, *REGS)],
        [(2, EXT * 4, *REGS), (2, EXT * 4, *REGS), (TILE * 4, *REGS)],
        6,
    )(flag, centre, pressure, from_left, from_right, soil)

    heat_stress = jnp.stack([relaxed[0], relaxed[2]])
    from_left = shifted(heat_stress, 0, 1)
    from_right = shifted(heat_stress, 0, -1)
    defect, strain = call(
        defect_kernel,
        [(2, TILE, *LAYER), (TILE, *LAYER)],
        [(2, EXT * 4, *REGS), (2, EXT * 4, *REGS), (TILE * 4, *REGS), (3, TILE * 4, *REGS)],
        5,
    )(flag, relaxed, from_left, from_right, tabs)

    ahead = STEPS_AHEAD
    left = shifted(defect[:, TILE - ahead:], 0, 1)
    right = shifted(defect[:, :ahead], 0, -1)
    zero = jnp.zeros((), F32)
    held = jnp.where(t == 0, jnp.stack([relaxed[0], relaxed[2]]), zero)
    held_p = jnp.where(t == 0, relaxed[1], zero)

    state = jnp.concatenate([left, defect, right], axis=1)
    total = strain
    for k in range(1, nt):
        since = (k - 1) % ahead
        if since == 0 and 1 < k < nt - 1:
            tile = state
            state = jnp.concatenate(
                [
                    shifted(tile[:, TILE - ahead:], 1, 1, [k - 1]),
                    shifted(tile, 1, 0, [k - 1]),
                    shifted(tile[:, :ahead], 1, -1, [k - 1]),
                ],
                axis=1,
            )
        else:
            state = shifted(state, 1, 0, [k - 1])
        halo = ahead - since
        got = shifted(total, 1, 0, [k - 1])
        held_p = held_p + got
        if k == nt - 1:
            held = held + state
            break
        out, grown, held = call(
            functools.partial(coarse_kernel, halo),
            [(2, TILE + 2 * halo - 2, *LAYER), (TILE, *LAYER), (2, TILE, *LAYER)],
            [],
            7,
            smem_first=False,
            input_output_aliases={6: 2},
        )(state, tabs, left, defect, right, strain, held)
        total = got + grown
        state = out
    corrected = jnp.stack([held[0], held_p, held[1]])
    return corrected[None], relaxed[None]


def solution(mesh):
    placed = (
        P(None, "space", None, None),
        P("tm", None, "space", None, None),
        P("space", None, None),
    )
    return jax.shard_map(
        functools.partial(on_device, mesh.shape["tm"], mesh.shape["space"]),
        mesh=mesh,
        in_specs=placed,
        out_specs=(P("tm", None, "space", None, None), P("tm", None, "space", None, None)),
        check_vma=False,
    )
```

time: 552 us -> 196 us (0.36)
  the two profiles are of different devices: /device:TPU:36 before, /device:TPU:127 now
where the time goes in v1:
time: 196 us; the launch traced here: 195 us
  waiting for transfers between devices  100 us (51%)
  Pallas kernels  44.9 us (23%)
  starting transfers between devices  42.7 us (22%)
  other arithmetic  3.73 us (2%)
  local copies, waits for them, and re-layouts  2.12 us (1%)
    ppermute x40, waiting for transfers between devices, shifted(): return lax.ppermute(x, both, pairs)  100 us
    ppermute x40, starting transfers between devices, shifted(): return lax.ppermute(x, both, pairs)  42.7 us
    pallas_call x14, Pallas kernels, on_device(): call(functools.partial(coarse_kernel, halo), [(2, TILE + 2 * halo - 2, *L...  19.3 us
    pallas_call x1, Pallas kernels, on_device(): call(relax_kernel, [(3, TILE, *LAYER), (5, EXT * 4, *REGS)], [(2, EXT * 4...  13.4 us
    pallas_call x1, Pallas kernels, on_device(): call(defect_kernel, [(2, TILE, *LAYER), (TILE, *LAYER)], [(2, EXT * 4, *R...  12.2 us
  transfers between devices with their start and end apart: 40, of which 8 were waited for; matrix products, arithmetic and copies ran while one was open for 1% of the time, Pallas kernels for 3%

profile of v1, /device:TPU:127, one launch (start us, length us, event | category | flops | bytes accessed | tf_op | source)
XLA Modules:
  0.0 195.1 jit_solution(8692113822089872023)
XLA Ops:
  0.6 1.2 bitcast_select_fusion
  2.0 3.6 %collective-permute-start.2 = (f32[3,8,32,128]{3,2,1,0:T(8,128)S(1)}, f32[3,8,32,128]{3,2,1,0:T(8,128)S(1)}, u32[]{:S(2)}, u32[]{:S(2)}) collective-permute-start(f32[3,8,32,128]{3,2,1,0:T(8,128)S(1)} %pad_maximum_fusion.2), channel_id=1, source_target_pairs={{0,33},{1,34},{2,35},{3,36},{4,37},{5,38},{6,39},{7,40},{8,41},{9,... | collective-permute-start | bytes 1179656 | tf_op jit(solution)/shard_map/ppermute | solution.py:271
  5.6 1.9 collective-permute-start.3
  9.4 9.5 %collective-permute-done.1.pressure = f32[8,32,128]{2,1,0:T(8,128)S(1)} collective-permute-done((f32[8,32,128]{2,1,0:T(8,128)S(1)}, f32[8,32,128]{2,1,0:T(8,128)S(1)}, u32[]{:S(2)}, u32[]{:S(2)}) %collective-permute-start.1) | collective-permute-done | bytes 131104 | tf_op jit(solution)/shard_map/ppermute | solution.py:271
  18.8 1.4 collective-permute-done.3.right
  20.2 13.4 %shard_map.50 = (f32[3,8,32,128]{3,2,1,0:T(8,128)}, f32[5,96,8,128]{3,2,1,0:T(8,128)S(1)}) custom-call(f32[3]{0:T(128)S(1)} %add_convert_fusion.flag, f32[2,8,32,128]{3,2,1,0:T(8,128)S(1)} %collective-permute-done.centre, f32[8,32,128]{2,1,0:T(8,128)S(1)} %collective-permute-done.1.pressure, f32[3,8,32,128]{3,2,1,0:T(8,128)S(1)} %collective-permute-done.2.left, ...), custom_call_target="tpu_custom_call" | custom-call | tf_op jit(solution)/shard_map/pallas_call | solution.py:280
  33.6 1.0 fusion.15
  34.6 5.2 %collective-permute-start.4 = (f32[2,8,32,128]{3,2,1,0:T(8,128)S(1)}, f32[2,8,32,128]{3,2,1,0:T(8,128)S(1)}, u32[]{:S(2)}, u32[]{:S(2)}) collective-permute-start(f32[2,8,32,128]{3,2,1,0:T(8,128)S(1)} %get-tuple-element.104), channel_id=1, source_target_pairs={{0,1},{1,2},{2,3},{3,4},{4,5},{5,6},{6,7},{7,8},{8,9},{9,10},{10,1... | collective-permute-start | bytes 786440 | tf_op jit(solution)/shard_map/ppermute | solution.py:271
  39.9 1.9 collective-permute-start.5
  41.8 3.2 %collective-permute-done.4.left = f32[2,8,32,128]{3,2,1,0:T(8,128)S(1)} collective-permute-done((f32[2,8,32,128]{3,2,1,0:T(8,128)S(1)}, f32[2,8,32,128]{3,2,1,0:T(8,128)S(1)}, u32[]{:S(2)}, u32[]{:S(2)}) %collective-permute-start.4) | collective-permute-done | bytes 262176 | tf_op jit(solution)/shard_map/ppermute | solution.py:271
  45.0 3.3 %collective-permute-done.5.right = f32[2,8,32,128]{3,2,1,0:T(8,128)S(1)} collective-permute-done((f32[2,8,32,128]{3,2,1,0:T(8,128)S(1)}, f32[2,8,32,128]{3,2,1,0:T(8,128)S(1)}, u32[]{:S(2)}, u32[]{:S(2)}) %collective-permute-start.5) | collective-permute-done | bytes 262176 | tf_op jit(solution)/shard_map/ppermute | solution.py:271
  48.3 1.0 copy-done
  49.3 12.2 %shard_map.51 = (f32[2,8,32,128]{3,2,1,0:T(8,128)S(1)}, f32[8,32,128]{2,1,0:T(8,128)S(1)}) custom-call(f32[3]{0:T(128)S(1)} %add_convert_fusion.flag, f32[3,8,32,128]{3,2,1,0:T(8,128)S(1)} %copy-done, f32[2,8,32,128]{3,2,1,0:T(8,128)S(1)} %collective-permute-done.4.left, f32[2,8,32,128]{3,2,1,0:T(8,128)S(1)} %collective-permute-done.5.right, ...), custom_call_target="tpu_custom_call" | custom-call | tf_op jit(solution)/shard_map/pallas_call | solution.py:290
  61.6 3.1 %collective-permute-start.7 = (f32[2,7,32,128]{3,2,1,0:T(8,128)S(1)}, f32[2,7,32,128]{3,2,1,0:T(8,128)S(1)}, u32[]{:S(2)}, u32[]{:S(2)}) collective-permute-start(f32[2,7,32,128]{3,2,1,0:T(8,128)S(1)} %get-tuple-element.106), channel_id=1, source_target_pairs={{1,0},{2,1},{3,2},{4,3},{5,4},{6,5},{7,6},{8,7},{9,8},{10,9},{11,1... | collective-permute-start | bytes 688136 | tf_op jit(solution)/shard_map/ppermute | solution.py:271
  64.7 2.2 %collective-permute-start.6 = (f32[2,7,32,128]{3,2,1,0:T(8,128)S(1)}, f32[2,7,32,128]{3,2,1,0:T(8,128)S(1)}, u32[]{:S(2)}, u32[]{:S(2)}) collective-permute-start(f32[2,7,32,128]{3,2,1,0:T(8,128)S(1)} %get-tuple-element.105), channel_id=1, source_target_pairs={{0,1},{1,2},{2,3},{3,4},{4,5},{5,6},{6,7},{7,8},{8,9},{9,10},{10,1... | collective-permute-start | bytes 688136 | tf_op jit(solution)/shard_map/ppermute | solution.py:271
  66.9 1.5 collective-permute-done.7.right
  68.4 6.0 %collective-permute-done.6.left = f32[2,7,32,128]{3,2,1,0:T(8,128)S(1)} collective-permute-done((f32[2,7,32,128]{3,2,1,0:T(8,128)S(1)}, f32[2,7,32,128]{3,2,1,0:T(8,128)S(1)}, u32[]{:S(2)}, u32[]{:S(2)}) %collective-permute-start.6) | collective-permute-done | bytes 229408 | tf_op jit(solution)/shard_map/ppermute | solution.py:271
  75.1 2.0 %shard_map.52 = (f32[2,20,32,128]{3,2,1,0:T(8,128)S(1)}, f32[8,32,128]{2,1,0:T(8,128)S(1)}, f32[2,8,32,128]{3,2,1,0:T(8,128)S(1)}) custom-call(f32[2,22,32,128]{3,2,1,0:T(8,128)S(1)} %collective-permute-done.8.state, f32[5,96,8,128]{3,2,1,0:T(8,128)S(1)} %get-tuple-element.49.tabs, ...), custom_call_target="tpu_custom_call", output_to_operand_aliasing={{2}: (6, {})} | custom-call | tf_op jit(solution)/shard_map/pallas_call | solution.py:326
  77.8 1.8 shard_map.53
  80.3 1.6 shard_map.54
  82.6 1.4 shard_map.55
  84.7 1.2 shard_map.56
  91.2 2.0 %shard_map.59 = (f32[2,20,32,128]{3,2,1,0:T(8,128)S(1)}, f32[8,32,128]{2,1,0:T(8,128)S(1)}, f32[2,8,32,128]{3,2,1,0:T(8,128)S(1)}) custom-call(f32[2,22,32,128]{3,2,1,0:T(8,128)S(1)} %pad_maximum_fusion.1.state, f32[5,96,8,128]{3,2,1,0:T(8,128)S(1)} %get-tuple-element.49.tabs, ...), custom_call_target="tpu_custom_call", output_to_operand_aliasing={{2}: (6, {})} | custom-call | tf_op jit(solution)/shard_map/pallas_call | solution.py:326
  93.9 1.8 shard_map.60
  97.8 1.6 shard_map.61
  103.0 1.4 shard_map.62
  107.2 1.2 shard_map.63
  111.3 1.0 shard_map.64
  115.2 1.3 collective-permute-start.39
  116.5 1.3 collective-permute-start.24
  117.8 75.0 %collective-permute-done.39 = f32[8,32,128]{2,1,0:T(8,128)S(1)} collective-permute-done((f32[8,32,128]{2,1,0:T(8,128)S(1)}, f32[8,32,128]{2,1,0:T(8,128)S(1)}, u32[]{:S(2)}, u32[]{:S(2)}) %collective-permute-start.39) | collective-permute-done | bytes 131104 | tf_op jit(solution)/shard_map/ppermute | solution.py:271
  192.8 1.1 fusion.14
  (98 shorter events, 26.6 us)
Async XLA Ops:
  2.0 16.9 %collective-permute-start.2 = (f32[3,8,32,128]{3,2,1,0:T(8,128)S(1)}, f32[3,8,32,128]{3,2,1,0:T(8,128)S(1)}, u32[]{:S(2)}, u32[]{:S(2)}) collective-permute-start(f32[3,8,32,128]{3,2,1,0:T(8,128)S(1)} %pad_maximum_fusion.2), channel_id=1, source_target_pairs={{0,33},{1,34},{2,35},{3,36},{4,37},{5,38},{6,39},{7,40},{8,41},{9,... | collective-permute-start | bytes 1179656 | tf_op jit(solution)/shard_map/ppermute | solution.py:271
  5.6 14.6 %collective-permute-start.3 = (f32[3,8,32,128]{3,2,1,0:T(8,128)S(1)}, f32[3,8,32,128]{3,2,1,0:T(8,128)S(1)}, u32[]{:S(2)}, u32[]{:S(2)}) collective-permute-start(f32[3,8,32,128]{3,2,1,0:T(8,128)S(1)} %pad_maximum_fusion.2), channel_id=1, source_target_pairs={{1,32},{2,33},{3,34},{4,35},{5,36},{6,37},{7,38},{8,39},{9,40},{10... | collective-permute-start | bytes 1179656 | tf_op jit(solution)/shard_map/ppermute | solution.py:271
  7.6 11.3 %collective-permute-start = (f32[2,8,32,128]{3,2,1,0:T(8,128)S(1)}, f32[2,8,32,128]{3,2,1,0:T(8,128)S(1)}, u32[]{:S(2)}, u32[]{:S(2)}) collective-permute-start(f32[2,8,32,128]{3,2,1,0:T(8,128)S(1)} %pad_maximum_fusion.3), channel_id=1, source_target_pairs={{0,32},{1,33},{2,34},{3,35},{4,36},{5,37},{6,38},{7,39},{8,40},{9,... | collective-permute-start | bytes 786440 | tf_op jit(solution)/shard_map/ppermute | solution.py:271
  8.5 10.3 %collective-permute-start.1 = (f32[8,32,128]{2,1,0:T(8,128)S(1)}, f32[8,32,128]{2,1,0:T(8,128)S(1)}, u32[]{:S(2)}, u32[]{:S(2)}) collective-permute-start(f32[8,32,128]{2,1,0:T(8,128)S(1)} %get-tuple-element.96), channel_id=1, source_target_pairs={{0,32},{1,33},{2,34},{3,35},{4,36},{5,37},{6,38},{7,39},{8,40},{9,... | collective-permute-start | bytes 393224 | tf_op jit(solution)/shard_map/ppermute | solution.py:271
  34.6 10.3 %collective-permute-start.4 = (f32[2,8,32,128]{3,2,1,0:T(8,128)S(1)}, f32[2,8,32,128]{3,2,1,0:T(8,128)S(1)}, u32[]{:S(2)}, u32[]{:S(2)}) collective-permute-start(f32[2,8,32,128]{3,2,1,0:T(8,128)S(1)} %get-tuple-element.104), channel_id=1, source_target_pairs={{0,1},{1,2},{2,3},{3,4},{4,5},{5,6},{6,7},{7,8},{8,9},{9,10},{10,1... | collective-permute-start | bytes 786440 | tf_op jit(solution)/shard_map/ppermute | solution.py:271
  39.9 8.4 %collective-permute-start.5 = (f32[2,8,32,128]{3,2,1,0:T(8,128)S(1)}, f32[2,8,32,128]{3,2,1,0:T(8,128)S(1)}, u32[]{:S(2)}, u32[]{:S(2)}) collective-permute-start(f32[2,8,32,128]{3,2,1,0:T(8,128)S(1)} %get-tuple-element.104), channel_id=1, source_target_pairs={{1,0},{2,1},{3,2},{4,3},{5,4},{6,5},{7,6},{8,7},{9,8},{10,9},{11,1... | collective-permute-start | bytes 786440 | tf_op jit(solution)/shard_map/ppermute | solution.py:271
  61.6 6.8 %collective-permute-start.7 = (f32[2,7,32,128]{3,2,1,0:T(8,128)S(1)}, f32[2,7,32,128]{3,2,1,0:T(8,128)S(1)}, u32[]{:S(2)}, u32[]{:S(2)}) collective-permute-start(f32[2,7,32,128]{3,2,1,0:T(8,128)S(1)} %get-tuple-element.106), channel_id=1, source_target_pairs={{1,0},{2,1},{3,2},{4,3},{5,4},{6,5},{7,6},{8,7},{9,8},{10,9},{11,1... | collective-permute-start | bytes 688136 | tf_op jit(solution)/shard_map/ppermute | solution.py:271
  64.7 9.6 %collective-permute-start.6 = (f32[2,7,32,128]{3,2,1,0:T(8,128)S(1)}, f32[2,7,32,128]{3,2,1,0:T(8,128)S(1)}, u32[]{:S(2)}, u32[]{:S(2)}) collective-permute-start(f32[2,7,32,128]{3,2,1,0:T(8,128)S(1)} %get-tuple-element.105), channel_id=1, source_target_pairs={{0,1},{1,2},{2,3},{3,4},{4,5},{5,6},{6,7},{7,8},{8,9},{9,10},{10,1... | collective-permute-start | bytes 688136 | tf_op jit(solution)/shard_map/ppermute | solution.py:271
  74.4 0.7 collective-permute-start.8
  77.1 0.7 collective-permute-start.9
  79.6 0.7 collective-permute-start.10
  81.9 0.7 collective-permute-start.11
  84.0 0.7 collective-permute-start.12
  85.9 0.7 collective-permute-start.13
  87.6 0.7 collective-permute-start.14
  89.1 2.1 %collective-permute-start.16 = (f32[2,8,32,128]{3,2,1,0:T(8,128)S(1)}, f32[2,8,32,128]{3,2,1,0:T(8,128)S(1)}, u32[]{:S(2)}, u32[]{:S(2)}) collective-permute-start(f32[2,8,32,128]{3,2,1,0:T(8,128)S(1)} %get-tuple-element.64), channel_id=1, source_target_pairs={{224,256},{225,257},{226,258},{227,259},{228,260},{229,261},{230,2... | collective-permute-start | bytes 786440 | tf_op jit(solution)/shard_map/ppermute | solution.py:271
  89.8 1.4 collective-permute-start.17
  90.5 0.7 collective-permute-start.15
  93.2 0.7 collective-permute-start.18
  95.7 2.1 %collective-permute-start.19 = (f32[2,18,32,128]{3,2,1,0:T(8,128)S(1)}, f32[2,18,32,128]{3,2,1,0:T(8,128)S(1)}, u32[]{:S(2)}, u32[]{:S(2)}) collective-permute-start(f32[2,18,32,128]{3,2,1,0:T(8,128)S(1)} %get-tuple-element.68), channel_id=1, source_target_pairs={{288,320},{289,321},{290,322},{291,323},{292,324},{293,325},{294,3... | collective-permute-start | bytes 1769480 | tf_op jit(solution)/shard_map/ppermute | solution.py:271
  96.4 0.7 collective-permute-start.25
  97.1 3.0 %collective-permute-start.26 = (f32[8,32,128]{2,1,0:T(8,128)S(1)}, f32[8,32,128]{2,1,0:T(8,128)S(1)}, u32[]{:S(2)}, u32[]{:S(2)}) collective-permute-start(f32[8,32,128]{2,1,0:T(8,128)S(1)} %add.92), channel_id=1, source_target_pairs={{32,64},{33,65},{34,66},{35,67},{36,68},{37,69},{38,70},{39,71},{4... | collective-permute-start | bytes 393224 | tf_op jit(solution)/shard_map/ppermute | solution.py:271
  99.4 3.6 %collective-permute-start.20 = (f32[2,16,32,128]{3,2,1,0:T(8,128)S(1)}, f32[2,16,32,128]{3,2,1,0:T(8,128)S(1)}, u32[]{:S(2)}, u32[]{:S(2)}) collective-permute-start(f32[2,16,32,128]{3,2,1,0:T(8,128)S(1)} %get-tuple-element.70), channel_id=1, source_target_pairs={{320,352},{321,353},{322,354},{323,355},{324,356},{325,357},{326,3... | collective-permute-start | bytes 1572872 | tf_op jit(solution)/shard_map/ppermute | solution.py:271
  102.3 2.8 %collective-permute-start.30 = (f32[8,32,128]{2,1,0:T(8,128)S(1)}, f32[8,32,128]{2,1,0:T(8,128)S(1)}, u32[]{:S(2)}, u32[]{:S(2)}) collective-permute-start(f32[8,32,128]{2,1,0:T(8,128)S(1)} %add.100), channel_id=1, source_target_pairs={{160,192},{161,193},{162,194},{163,195},{164,196},{165,197},{166,1... | collective-permute-start | bytes 393224 | tf_op jit(solution)/shard_map/ppermute | solution.py:271
  104.4 2.8 %collective-permute-start.21 = (f32[2,14,32,128]{3,2,1,0:T(8,128)S(1)}, f32[2,14,32,128]{3,2,1,0:T(8,128)S(1)}, u32[]{:S(2)}, u32[]{:S(2)}) collective-permute-start(f32[2,14,32,128]{3,2,1,0:T(8,128)S(1)} %get-tuple-element.72), channel_id=1, source_target_pairs={{352,384},{353,385},{354,386},{355,387},{356,388},{357,389},{358,3... | collective-permute-start | bytes 1376264 | tf_op jit(solution)/shard_map/ppermute | solution.py:271
  106.5 2.6 %collective-permute-start.33 = (f32[8,32,128]{2,1,0:T(8,128)S(1)}, f32[8,32,128]{2,1,0:T(8,128)S(1)}, u32[]{:S(2)}, u32[]{:S(2)}) collective-permute-start(f32[8,32,128]{2,1,0:T(8,128)S(1)} %add.106), channel_id=1, source_target_pairs={{256,288},{257,289},{258,290},{259,291},{260,292},{261,293},{262,2... | collective-permute-start | bytes 393224 | tf_op jit(solution)/shard_map/ppermute | solution.py:271
  108.4 2.8 %collective-permute-start.22 = (f32[2,12,32,128]{3,2,1,0:T(8,128)S(1)}, f32[2,12,32,128]{3,2,1,0:T(8,128)S(1)}, u32[]{:S(2)}, u32[]{:S(2)}) collective-permute-start(f32[2,12,32,128]{3,2,1,0:T(8,128)S(1)} %get-tuple-element.74), channel_id=1, source_target_pairs={{384,416},{385,417},{386,418},{387,419},{388,420},{389,421},{390,4... | collective-permute-start | bytes 1179656 | tf_op jit(solution)/shard_map/ppermute | solution.py:271
  110.6 2.4 %collective-permute-start.36 = (f32[8,32,128]{2,1,0:T(8,128)S(1)}, f32[8,32,128]{2,1,0:T(8,128)S(1)}, u32[]{:S(2)}, u32[]{:S(2)}) collective-permute-start(f32[8,32,128]{2,1,0:T(8,128)S(1)} %add.112), channel_id=1, source_target_pairs={{352,384},{353,385},{354,386},{355,387},{356,388},{357,389},{358,3... | collective-permute-start | bytes 393224 | tf_op jit(solution)/shard_map/ppermute | solution.py:271
  112.2 2.1 %collective-permute-start.23 = (f32[2,10,32,128]{3,2,1,0:T(8,128)S(1)}, f32[2,10,32,128]{3,2,1,0:T(8,128)S(1)}, u32[]{:S(2)}, u32[]{:S(2)}) collective-permute-start(f32[2,10,32,128]{3,2,1,0:T(8,128)S(1)} %get-tuple-element.76), channel_id=1, source_target_pairs={{416,448},{417,449},{418,450},{419,451},{420,452},{421,453},{422,4... | collective-permute-start | bytes 983048 | tf_op jit(solution)/shard_map/ppermute | solution.py:271
  113.7 1.5 collective-permute-start.38
  115.2 77.6 %collective-permute-start.39 = (f32[8,32,128]{2,1,0:T(8,128)S(1)}, f32[8,32,128]{2,1,0:T(8,128)S(1)}, u32[]{:S(2)}, u32[]{:S(2)}) collective-permute-start(f32[8,32,128]{2,1,0:T(8,128)S(1)} %add.118), channel_id=1, source_target_pairs={{448,480},{449,481},{450,482},{451,483},{452,484},{453,485},{454,4... | collective-permute-start | bytes 393224 | tf_op jit(solution)/shard_map/ppermute | solution.py:271
  116.5 77.7 %collective-permute-start.24 = (f32[2,8,32,128]{3,2,1,0:T(8,128)S(1)}, f32[2,8,32,128]{3,2,1,0:T(8,128)S(1)}, u32[]{:S(2)}, u32[]{:S(2)}) collective-permute-start(f32[2,8,32,128]{3,2,1,0:T(8,128)S(1)} %get-tuple-element.79), channel_id=1, source_target_pairs={{448,480},{449,481},{450,482},{451,483},{452,484},{453,485},{454,4... | collective-permute-start | bytes 786440 | tf_op jit(solution)/shard_map/ppermute | solution.py:271
  (10 other events, 7.7 us)

commit v2 on v1

--- a/solution.py
+++ b/solution.py
@@ -23,7 +23,17 @@
 
 TILE = 8
 EXT = 3 * TILE
-STEPS_AHEAD = 7
+
+BLOCKS = ((1, range(2, 3)), (3, range(3, 8)), (9, range(8, 13)), (15, range(13, 16)))
+PHASE_END = {k: 7 if k < 8 else 15 for k in range(1, 16)}
+ROUNDS = (
+    ((15, 13, 13), (9, 10, 10), (3, 4, 4), (1, 2, 2)),
+    ((15, 14, 14), (9, 11, 11), (3, 5, 5)),
+    ((9, 12, 12), (3, 6, 6)),
+    ((9, 8, 8), (3, 7, 7)),
+)
+KEPT = ((1, 1), (3, 3), (9, 9), (15, 15))
+AROUND = 7
 VMEM = functools.partial(pl.BlockSpec, memory_space=pltpu.VMEM)
 SMEM = functools.partial(pl.BlockSpec, memory_space=pltpu.SMEM)
 F32 = jnp.float32
@@ -47,6 +57,12 @@
     *lead, layer = at
     for r in range(4):
         ref[(*lead, layer * 4 + r)] = rows[r]
+
+
+def loop(low, high, body):
+    for start in range(low, high, TILE):
+        for layer in range(start, min(start + TILE, high)):
+            body(layer, 0)
 
 
 def edges():
@@ -145,10 +161,10 @@
             return 0
 
         if t < RATIO - 1:
-            lax.fori_loop(1 + t, TILE, one, 0)
-        lax.fori_loop(TILE, 2 * TILE, functools.partial(one, tile=True), 0)
+            loop(1 + t, TILE, one)
+        loop(TILE, 2 * TILE, functools.partial(one, tile=True))
         if t < RATIO - 1:
-            lax.fori_loop(2 * TILE, EXT - 1 - t, one, 0)
+            loop(2 * TILE, EXT - 1 - t, one)
 
 
 def gather_ext(buf, left, centre, right, fields):
@@ -209,33 +225,27 @@
     lax.fori_loop(0, TILE, strain, 0)
 
 
-def coarse_kernel(halo, state, tabs, left, centre, right, strain, held, out, out_p, out_held):
+def coarse_kernel(halo, state, tabs, defect, out):
     ends = edges()
     new = halo - 1
-
-    def one(o, _, kind=None):
+    wide, narrow = TILE + 2 * halo, TILE + 2 * new
+
+    def one(o, _, tile=False):
         i = o + 1
-        at = TILE - halo + i
-        load = lambda f, d: load_rows(state, f, i + d)
-        here_t, here_w, inc_t, inc_p, inc_w = increments(load, tabs, at, ends)
-        if kind == 0:
-            d, j = left, o + STEPS_AHEAD - new
-        elif kind == 1:
-            d, j = centre, o - new
-            store_rows(out_p, [p + RATIO * v for p, v in zip(load_rows(strain, j), inc_p)], j)
-            store_rows(out_held, plus(load_rows(held, 0, j), here_t), 0, j)
-            store_rows(out_held, plus(load_rows(held, 1, j), here_w), 1, j)
-        else:
-            d, j = right, o - new - TILE
-        store_rows(out, [(v + RATIO * x) + e for v, x, e in zip(here_t, inc_t, load_rows(d, 0, j))], 0, o)
-        store_rows(out, [(v + RATIO * x) + e for v, x, e in zip(here_w, inc_w, load_rows(d, 1, j))], 1, o)
+        load = lambda f, d: load_rows(state, f * wide + i + d)
+        here_t, here_w, inc_t, inc_p, inc_w = increments(load, tabs, TILE - halo + i, ends)
+        if tile:
+            j = o - new
+            rows = zip(load_rows(state, 2 * wide + j), inc_p, load_rows(defect, 2 * narrow + j))
+            store_rows(out, [(p + RATIO * v) + e for p, v, e in rows], 2 * narrow + j)
+        for f, here, inc in ((0, here_t, inc_t), (1, here_w, inc_w)):
+            rows = zip(here, inc, load_rows(defect, f * narrow + o))
+            store_rows(out, [(v + RATIO * x) + e for v, x, e in rows], f * narrow + o)
         return 0
 
-    if new:
-        lax.fori_loop(0, new, functools.partial(one, kind=0), 0)
-    lax.fori_loop(new, new + TILE, functools.partial(one, kind=1), 0)
-    if new:
-        lax.fori_loop(new + TILE, 2 * new + TILE, functools.partial(one, kind=2), 0)
+    loop(0, new, one)
+    loop(new, new + TILE, functools.partial(one, tile=True))
+    loop(new + TILE, narrow, one)
 
 
 def call(kernel, outs, scratch, n_in, smem_first=True, **kw):
@@ -294,46 +304,64 @@
         5,
     )(flag, relaxed, from_left, from_right, tabs)
 
-    ahead = STEPS_AHEAD
-    left = shifted(defect[:, TILE - ahead:], 0, 1)
-    right = shifted(defect[:, :ahead], 0, -1)
-    zero = jnp.zeros((), F32)
-    held = jnp.where(t == 0, jnp.stack([relaxed[0], relaxed[2]]), zero)
-    held_p = jnp.where(t == 0, relaxed[1], zero)
-
-    state = jnp.concatenate([left, defect, right], axis=1)
-    total = strain
-    for k in range(1, nt):
-        since = (k - 1) % ahead
-        if since == 0 and 1 < k < nt - 1:
-            tile = state
-            state = jnp.concatenate(
-                [
-                    shifted(tile[:, TILE - ahead:], 1, 1, [k - 1]),
-                    shifted(tile, 1, 0, [k - 1]),
-                    shifted(tile[:, :ahead], 1, -1, [k - 1]),
-                ],
-                axis=1,
-            )
+    around = AROUND
+    left = shifted(defect[:, TILE - around:], 0, 1)
+    right = shifted(defect[:, :around], 0, -1)
+    widened = jnp.concatenate([left, defect, right], axis=1)
+
+    def with_halo(h):
+        sides = widened[:, around - h:around + TILE + h]
+        return jnp.concatenate([sides.reshape(-1, *LAYER), strain])
+
+    def step(halo, state, term):
+        (out,) = call(
+            functools.partial(coarse_kernel, halo), [(2 * (TILE + 2 * halo - 2) + TILE, *LAYER)], [], 3, smem_first=False
+        )(state, tabs, term)
+        return out
+
+    def tile_of(state, h):
+        layers = TILE + 2 * h
+        return jnp.stack([state[h:h + TILE], state[2 * layers:], state[layers + h:layers + h + TILE]])
+
+    state, holder = with_halo(PHASE_END[2] - 1), 0
+    results = {}
+    for worker, steps in BLOCKS:
+        first = steps[0]
+        halo = PHASE_END[first] - first + 1
+        hop = worker - holder
+        if PHASE_END[first] == PHASE_END[first - 1]:
+            state = shifted(state, hop, 0, [holder])
         else:
-            state = shifted(state, 1, 0, [k - 1])
-        halo = ahead - since
-        got = shifted(total, 1, 0, [k - 1])
-        held_p = held_p + got
-        if k == nt - 1:
-            held = held + state
-            break
-        out, grown, held = call(
-            functools.partial(coarse_kernel, halo),
-            [(2, TILE + 2 * halo - 2, *LAYER), (TILE, *LAYER), (2, TILE, *LAYER)],
-            [],
-            7,
-            smem_first=False,
-            input_output_aliases={6: 2},
-        )(state, tabs, left, defect, right, strain, held)
-        total = got + grown
-        state = out
-    corrected = jnp.stack([held[0], held_p, held[1]])
+            tile = state[:2 * TILE]
+            before = shifted(tile, hop, 1, [holder])
+            after = shifted(tile, hop, -1, [holder])
+            state = shifted(state, hop, 0, [holder])
+            parts = []
+            for f in range(2):
+                own = slice(f * TILE, (f + 1) * TILE)
+                parts += [before[own][TILE - halo:], state[own], after[own][:halo]]
+            state = jnp.concatenate([*parts, state[2 * TILE:]])
+        if first == 2:
+            results[1] = tile_of(state, halo)
+        terms = {}
+        for k in steps:
+            mine = with_halo(PHASE_END[k] - k)
+            terms[k] = mine if k - 1 == worker else shifted(mine, worker - k + 1, 0, [k - 1])
+        for k in steps:
+            state = step(PHASE_END[k] - k + 1, state, terms[k])
+            results[k] = tile_of(state, PHASE_END[k] - k)
+        holder = worker
+
+    corrected = jnp.where(t == 0, relaxed, 0.0)
+    for sends in ROUNDS:
+        payload = results[sends[0][1]]
+        pairs = []
+        for source, k, target in sends:
+            payload = jnp.where(t == source, results[k], payload)
+            pairs += [(source * ns + b, target * ns + b) for b in range(ns)]
+        corrected = corrected + lax.ppermute(payload, both, pairs)
+    for device, k in KEPT:
+        corrected = jnp.where(t == device, results[k], corrected)
     return corrected[None], relaxed[None]
 
 

time: 196 us -> 156 us (0.80)
  the two profiles are of different devices: /device:TPU:127 before, /device:TPU:47 now
where the time goes in v2:
time: 156 us
  waiting for transfers between devices  84.9 us (54%)
  starting transfers between devices  43.6 us (28%)
  Pallas kernels  15 us (10%)
  local copies, waits for them, and re-layouts  5.69 us (4%)
  other arithmetic  4.94 us (3%)
    ppermute x4, waiting for transfers between devices, on_device(): corrected = corrected + lax.ppermute(payload, both, pairs)  62.3 us
    ppermute x25, starting transfers between devices, shifted(): return lax.ppermute(x, both, pairs)  40.3 us
    ppermute x25, waiting for transfers between devices, shifted(): return lax.ppermute(x, both, pairs)  22.6 us
    pallas_call x14, Pallas kernels, step(): call(functools.partial(coarse_kernel, halo), [(2 * (TILE + 2 * halo - 2)...  6.11 us
    pallas_call x1, Pallas kernels, on_device(): call(relax_kernel, [(3, TILE, *LAYER), (5, EXT * 4, *REGS)], [(2, EXT * 4...  5.01 us
    pallas_call x1, Pallas kernels, on_device(): call(defect_kernel, [(2, TILE, *LAYER), (TILE, *LAYER)], [(2, EXT * 4, *R...  3.88 us
    ppermute x4, starting transfers between devices, on_device(): corrected = corrected + lax.ppermute(payload, both, pairs)  3.35 us
  transfers between devices with their start and end apart: 29, of which 7 were waited for; matrix products, arithmetic and copies ran while one was open for 2% of the time, Pallas kernels for 4%

profile of v2, /device:TPU:47, one launch (start us, length us, event | category | flops | bytes accessed | tf_op | source)
XLA Modules:
  0.0 155.6 jit_solution(7242353368705299095)
XLA Ops:
  0.6 1.0 convert_bitcast_fusion
  1.6 1.1 bitcast_select_fusion
  2.8 11.6 %collective-permute-start.3 = (f32[3,8,32,128]{3,2,1,0:T(8,128)S(1)}, f32[3,8,32,128]{3,2,1,0:T(8,128)S(1)}, u32[]{:S(2)}, u32[]{:S(2)}) collective-permute-start(f32[3,8,32,128]{3,2,1,0:T(8,128)S(1)} %pad_maximum_fusion.7), channel_id=1, source_target_pairs={{1,32},{2,33},{3,34},{4,35},{5,36},{6,37},{7,38},{8,39},{9,40},{10... | collective-permute-start | bytes 1179656 | tf_op jit(solution)/shard_map/ppermute | solution.py:281
  14.4 1.9 %collective-permute-start.2 = (f32[3,8,32,128]{3,2,1,0:T(8,128)S(1)}, f32[3,8,32,128]{3,2,1,0:T(8,128)S(1)}, u32[]{:S(2)}, u32[]{:S(2)}) collective-permute-start(f32[3,8,32,128]{3,2,1,0:T(8,128)S(1)} %pad_maximum_fusion.7), channel_id=1, source_target_pairs={{0,33},{1,34},{2,35},{3,36},{4,37},{5,38},{6,39},{7,40},{8,41},{9,... | collective-permute-start | bytes 1179656 | tf_op jit(solution)/shard_map/ppermute | solution.py:281
  16.4 0.8 collective-permute-start.1
  17.2 10.4 %collective-permute-done.1.pressure = f32[8,32,128]{2,1,0:T(8,128)S(1)} collective-permute-done((f32[8,32,128]{2,1,0:T(8,128)S(1)}, f32[8,32,128]{2,1,0:T(8,128)S(1)}, u32[]{:S(2)}, u32[]{:S(2)}) %collective-permute-start.1) | collective-permute-done | bytes 131104 | tf_op jit(solution)/shard_map/ppermute | solution.py:281
  27.6 2.1 %collective-permute-done.2.left = f32[3,8,32,128]{3,2,1,0:T(8,128)S(1)} collective-permute-done((f32[3,8,32,128]{3,2,1,0:T(8,128)S(1)}, f32[3,8,32,128]{3,2,1,0:T(8,128)S(1)}, u32[]{:S(2)}, u32[]{:S(2)}) %collective-permute-start.2) | collective-permute-done | bytes 393248 | tf_op jit(solution)/shard_map/ppermute | solution.py:281
  29.7 5.0 %shard_map.50 = (f32[3,8,32,128]{3,2,1,0:T(8,128)}, f32[5,96,8,128]{3,2,1,0:T(8,128)S(1)}) custom-call(f32[3]{0:T(128)S(1)} %add_convert_fusion.flag, f32[2,8,32,128]{3,2,1,0:T(8,128)S(1)} %collective-permute-done.centre, f32[8,32,128]{2,1,0:T(8,128)S(1)} %collective-permute-done.1.pressure, f32[3,8,32,128]{3,2,1,0:T(8,128)S(1)} %collective-permute-done.2.left, ...), custom_call_target="tpu_custom_call" | custom-call | tf_op jit(solution)/shard_map/pallas_call | solution.py:290
  34.7 1.0 fusion.1
  35.8 1.9 %collective-permute-start.5 = (f32[2,8,32,128]{3,2,1,0:T(8,128)S(1)}, f32[2,8,32,128]{3,2,1,0:T(8,128)S(1)}, u32[]{:S(2)}, u32[]{:S(2)}) collective-permute-start(f32[2,8,32,128]{3,2,1,0:T(8,128)S(1)} %pad_maximum_fusion.10), channel_id=1, source_target_pairs={{1,0},{2,1},{3,2},{4,3},{5,4},{6,5},{7,6},{8,7},{9,8},{10,9},{11,1... | collective-permute-start | bytes 786440 | tf_op jit(solution)/shard_map/ppermute | solution.py:281
  37.7 3.4 %collective-permute-start.4 = (f32[2,8,32,128]{3,2,1,0:T(8,128)S(1)}, f32[2,8,32,128]{3,2,1,0:T(8,128)S(1)}, u32[]{:S(2)}, u32[]{:S(2)}) collective-permute-start(f32[2,8,32,128]{3,2,1,0:T(8,128)S(1)} %pad_maximum_fusion.10), channel_id=1, source_target_pairs={{0,1},{1,2},{2,3},{3,4},{4,5},{5,6},{6,7},{7,8},{8,9},{9,10},{10,1... | collective-permute-start | bytes 786440 | tf_op jit(solution)/shard_map/ppermute | solution.py:281
  41.1 4.5 %collective-permute-done.5.right = f32[2,8,32,128]{3,2,1,0:T(8,128)S(1)} collective-permute-done((f32[2,8,32,128]{3,2,1,0:T(8,128)S(1)}, f32[2,8,32,128]{3,2,1,0:T(8,128)S(1)}, u32[]{:S(2)}, u32[]{:S(2)}) %collective-permute-start.5) | collective-permute-done | bytes 262176 | tf_op jit(solution)/shard_map/ppermute | solution.py:281
  45.5 2.7 %collective-permute-done.4.left = f32[2,8,32,128]{3,2,1,0:T(8,128)S(1)} collective-permute-done((f32[2,8,32,128]{3,2,1,0:T(8,128)S(1)}, f32[2,8,32,128]{3,2,1,0:T(8,128)S(1)}, u32[]{:S(2)}, u32[]{:S(2)}) %collective-permute-start.4) | collective-permute-done | bytes 262176 | tf_op jit(solution)/shard_map/ppermute | solution.py:281
  48.2 1.0 copy-done
  49.2 3.9 %shard_map.51 = (f32[2,8,32,128]{3,2,1,0:T(8,128)S(1)}, f32[8,32,128]{2,1,0:T(8,128)S(1)}) custom-call(f32[3]{0:T(128)S(1)} %add_convert_fusion.flag, f32[3,8,32,128]{3,2,1,0:T(8,128)S(1)} %copy-done, f32[2,8,32,128]{3,2,1,0:T(8,128)S(1)} %collective-permute-done.4.left, f32[2,8,32,128]{3,2,1,0:T(8,128)S(1)} %collective-permute-done.5.right, ...), custom_call_target="tpu_custom_call" | custom-call | tf_op jit(solution)/shard_map/pallas_call | solution.py:300
  53.1 2.3 %collective-permute-start.6 = (f32[2,7,32,128]{3,2,1,0:T(8,128)S(1)}, f32[2,7,32,128]{3,2,1,0:T(8,128)S(1)}, u32[]{:S(2)}, u32[]{:S(2)}) collective-permute-start(f32[2,7,32,128]{3,2,1,0:T(8,128)S(1)} %get-tuple-element.61), channel_id=1, source_target_pairs={{0,1},{1,2},{2,3},{3,4},{4,5},{5,6},{6,7},{7,8},{8,9},{9,10},{10,1... | collective-permute-start | bytes 688136 | tf_op jit(solution)/shard_map/ppermute | solution.py:281
  55.4 5.1 %collective-permute-start.7 = (f32[2,7,32,128]{3,2,1,0:T(8,128)S(1)}, f32[2,7,32,128]{3,2,1,0:T(8,128)S(1)}, u32[]{:S(2)}, u32[]{:S(2)}) collective-permute-start(f32[2,7,32,128]{3,2,1,0:T(8,128)S(1)} %get-tuple-element.60), channel_id=1, source_target_pairs={{1,0},{2,1},{3,2},{4,3},{5,4},{6,5},{7,6},{8,7},{9,8},{10,9},{11,1... | collective-permute-start | bytes 688136 | tf_op jit(solution)/shard_map/ppermute | solution.py:281
  60.5 1.5 collective-permute-done.6
  62.0 1.4 collective-permute-done.7
  63.5 0.9 copy-done.3
  64.4 0.9 pad_maximum_fusion.1
  66.1 0.8 collective-permute-start.24
  67.0 1.0 slice.278
  68.0 1.0 slice.277
  70.6 0.7 collective-permute-start.9
  73.6 1.8 %collective-permute-start.20 = (f32[36,32,128]{2,1,0:T(8,128)S(1)}, f32[36,32,128]{2,1,0:T(8,128)S(1)}, u32[]{:S(2)}, u32[]{:S(2)}) collective-permute-start(f32[36,32,128]{2,1,0:T(8,128)S(1)} %pad_maximum_fusion.4.defect), channel_id=1, source_target_pairs={{352,288},{353,289},{354,290},{355,291},{356,292},{357,293},{358,2... | collective-permute-start | bytes 1769480 | tf_op jit(solution)/shard_map/ppermute | solution.py:281
  76.4 0.9 collective-permute-start.19
  80.6 0.7 collective-permute-start.18
  81.3 0.7 collective-permute-start.17
  90.5 1.3 collective-permute-start.26
  92.2 62.3 %collective-permute-done.26 = f32[3,8,32,128]{3,2,1,0:T(8,128)S(1)} collective-permute-done((f32[3,8,32,128]{3,2,1,0:T(8,128)S(1)}, f32[3,8,32,128]{3,2,1,0:T(8,128)S(1)}, u32[]{:S(2)}, u32[]{:S(2)}) %collective-permute-start.26) | collective-permute-done | bytes 393248 | tf_op jit(solution)/shard_map/ppermute | solution.py:362
  154.5 1.1 fusion
  (106 shorter events, 17.5 us)
Async XLA Ops:
  0.6 29.1 %copy-start.2 = (s32[8,32,128]{2,1,0:T(8,128)S(1)}, s32[8,32,128]{2,1,0:T(8,128)}, u32[]{:S(2)}) copy-start(s32[8,32,128]{2,1,0:T(8,128)} %soil.1) | copy-start | bytes 393220
  2.8 24.8 %collective-permute-start.3 = (f32[3,8,32,128]{3,2,1,0:T(8,128)S(1)}, f32[3,8,32,128]{3,2,1,0:T(8,128)S(1)}, u32[]{:S(2)}, u32[]{:S(2)}) collective-permute-start(f32[3,8,32,128]{3,2,1,0:T(8,128)S(1)} %pad_maximum_fusion.7), channel_id=1, source_target_pairs={{1,32},{2,33},{3,34},{4,35},{5,36},{6,37},{7,38},{8,39},{9,40},{10... | collective-permute-start | bytes 1179656 | tf_op jit(solution)/shard_map/ppermute | solution.py:281
  14.4 15.3 %collective-permute-start.2 = (f32[3,8,32,128]{3,2,1,0:T(8,128)S(1)}, f32[3,8,32,128]{3,2,1,0:T(8,128)S(1)}, u32[]{:S(2)}, u32[]{:S(2)}) collective-permute-start(f32[3,8,32,128]{3,2,1,0:T(8,128)S(1)} %pad_maximum_fusion.7), channel_id=1, source_target_pairs={{0,33},{1,34},{2,35},{3,36},{4,37},{5,38},{6,39},{7,40},{8,41},{9,... | collective-permute-start | bytes 1179656 | tf_op jit(solution)/shard_map/ppermute | solution.py:281
  16.3 11.3 %collective-permute-start = (f32[2,8,32,128]{3,2,1,0:T(8,128)S(1)}, f32[2,8,32,128]{3,2,1,0:T(8,128)S(1)}, u32[]{:S(2)}, u32[]{:S(2)}) collective-permute-start(f32[2,8,32,128]{3,2,1,0:T(8,128)S(1)} %pad_maximum_fusion.9), channel_id=1, source_target_pairs={{0,32},{1,33},{2,34},{3,35},{4,36},{5,37},{6,38},{7,39},{8,40},{9,... | collective-permute-start | bytes 786440 | tf_op jit(solution)/shard_map/ppermute | solution.py:281
  16.4 11.2 %collective-permute-start.1 = (f32[8,32,128]{2,1,0:T(8,128)S(1)}, f32[8,32,128]{2,1,0:T(8,128)S(1)}, u32[]{:S(2)}, u32[]{:S(2)}) collective-permute-start(f32[8,32,128]{2,1,0:T(8,128)S(1)} %get-tuple-element.57), channel_id=1, source_target_pairs={{0,32},{1,33},{2,34},{3,35},{4,36},{5,37},{6,38},{7,39},{8,40},{9,... | collective-permute-start | bytes 393224 | tf_op jit(solution)/shard_map/ppermute | solution.py:281
  35.8 9.8 %collective-permute-start.5 = (f32[2,8,32,128]{3,2,1,0:T(8,128)S(1)}, f32[2,8,32,128]{3,2,1,0:T(8,128)S(1)}, u32[]{:S(2)}, u32[]{:S(2)}) collective-permute-start(f32[2,8,32,128]{3,2,1,0:T(8,128)S(1)} %pad_maximum_fusion.10), channel_id=1, source_target_pairs={{1,0},{2,1},{3,2},{4,3},{5,4},{6,5},{7,6},{8,7},{9,8},{10,9},{11,1... | collective-permute-start | bytes 786440 | tf_op jit(solution)/shard_map/ppermute | solution.py:281
  37.7 10.5 %collective-permute-start.4 = (f32[2,8,32,128]{3,2,1,0:T(8,128)S(1)}, f32[2,8,32,128]{3,2,1,0:T(8,128)S(1)}, u32[]{:S(2)}, u32[]{:S(2)}) collective-permute-start(f32[2,8,32,128]{3,2,1,0:T(8,128)S(1)} %pad_maximum_fusion.10), channel_id=1, source_target_pairs={{0,1},{1,2},{2,3},{3,4},{4,5},{5,6},{6,7},{7,8},{8,9},{9,10},{10,1... | collective-permute-start | bytes 786440 | tf_op jit(solution)/shard_map/ppermute | solution.py:281
  53.1 8.9 %collective-permute-start.6 = (f32[2,7,32,128]{3,2,1,0:T(8,128)S(1)}, f32[2,7,32,128]{3,2,1,0:T(8,128)S(1)}, u32[]{:S(2)}, u32[]{:S(2)}) collective-permute-start(f32[2,7,32,128]{3,2,1,0:T(8,128)S(1)} %get-tuple-element.61), channel_id=1, source_target_pairs={{0,1},{1,2},{2,3},{3,4},{4,5},{5,6},{6,7},{7,8},{8,9},{9,10},{10,1... | collective-permute-start | bytes 688136 | tf_op jit(solution)/shard_map/ppermute | solution.py:281
  55.4 8.0 %collective-permute-start.7 = (f32[2,7,32,128]{3,2,1,0:T(8,128)S(1)}, f32[2,7,32,128]{3,2,1,0:T(8,128)S(1)}, u32[]{:S(2)}, u32[]{:S(2)}) collective-permute-start(f32[2,7,32,128]{3,2,1,0:T(8,128)S(1)} %get-tuple-element.60), channel_id=1, source_target_pairs={{1,0},{2,1},{3,2},{4,3},{5,4},{6,5},{7,6},{8,7},{9,8},{10,9},{11,1... | collective-permute-start | bytes 688136 | tf_op jit(solution)/shard_map/ppermute | solution.py:281
  65.4 4.7 %collective-permute-start.8 = (f32[48,32,128]{2,1,0:T(8,128)}, f32[48,32,128]{2,1,0:T(8,128)S(1)}, u32[]{:S(2)}, u32[]{:S(2)}) collective-permute-start(f32[48,32,128]{2,1,0:T(8,128)} %pad_maximum_fusion.1), channel_id=1, source_target_pairs={{0,32},{1,33},{2,34},{3,35},{4,36},{5,37},{6,38},{7,39},{8,40},{9,... | collective-permute-start | bytes 2359304 | tf_op jit(solution)/shard_map/ppermute | solution.py:281
  66.1 2.9 %copy-start.4 = (f32[2,22,32,128]{3,2,1,0:T(8,128)S(1)}, f32[2,22,32,128]{3,2,1,0:T(8,128)}, u32[]{:S(2)}) copy-start(f32[2,22,32,128]{3,2,1,0:T(8,128)} %copy-done.3) | copy-start | bytes 2162692
  66.1 25.7 %collective-permute-start.24 = (f32[24,32,128]{2,1,0:T(8,128)S(1)}, f32[24,32,128]{2,1,0:T(8,128)S(1)}, u32[]{:S(2)}, u32[]{:S(2)}) collective-permute-start(f32[24,32,128]{2,1,0:T(8,128)S(1)} %pad_maximum_fusion.8), channel_id=1, source_target_pairs={{448,480},{449,481},{450,482},{451,483},{452,484},{453,485},{454,4... | collective-permute-start | bytes 1179656 | tf_op jit(solution)/shard_map/ppermute | solution.py:281
  69.2 3.7 %collective-permute-start.10 = (f32[40,32,128]{2,1,0:T(8,128)S(1)}, f32[40,32,128]{2,1,0:T(8,128)S(1)}, u32[]{:S(2)}, u32[]{:S(2)}) collective-permute-start(f32[40,32,128]{2,1,0:T(8,128)S(1)} %pad_maximum_fusion.3), channel_id=1, source_target_pairs={{64,96},{65,97},{66,98},{67,99},{68,100},{69,101},{70,102},{71,103... | collective-permute-start | bytes 1966088 | tf_op jit(solution)/shard_map/ppermute | solution.py:281
  70.6 3.0 %collective-permute-start.9 = (f32[44,32,128]{2,1,0:T(8,128)S(1)}, f32[44,32,128]{2,1,0:T(8,128)S(1)}, u32[]{:S(2)}, u32[]{:S(2)}) collective-permute-start(f32[44,32,128]{2,1,0:T(8,128)S(1)} %shard_map.52), channel_id=1, source_target_pairs={{32,96},{33,97},{34,98},{35,99},{36,100},{37,101},{38,102},{39,103... | collective-permute-start | bytes 2162696 | tf_op jit(solution)/shard_map/ppermute | solution.py:281
  71.4 6.3 %collective-permute-start.12 = (f32[28,32,128]{2,1,0:T(8,128)S(1)}, f32[28,32,128]{2,1,0:T(8,128)S(1)}, u32[]{:S(2)}, u32[]{:S(2)}) collective-permute-start(f32[28,32,128]{2,1,0:T(8,128)S(1)} %pad_maximum_fusion.6), channel_id=1, source_target_pairs={{160,96},{161,97},{162,98},{163,99},{164,100},{165,101},{166,102},... | collective-permute-start | bytes 1376264 | tf_op jit(solution)/shard_map/ppermute | solution.py:281
  72.1 4.3 %collective-permute-start.11 = (f32[32,32,128]{2,1,0:T(8,128)S(1)}, f32[32,32,128]{2,1,0:T(8,128)S(1)}, u32[]{:S(2)}, u32[]{:S(2)}) collective-permute-start(f32[32,32,128]{2,1,0:T(8,128)S(1)} %pad_maximum_fusion.5), channel_id=1, source_target_pairs={{128,96},{129,97},{130,98},{131,99},{132,100},{133,101},{134,102},... | collective-permute-start | bytes 1572872 | tf_op jit(solution)/shard_map/ppermute | solution.py:281
  72.9 5.2 %collective-permute-start.13 = (f32[24,32,128]{2,1,0:T(8,128)S(1)}, f32[24,32,128]{2,1,0:T(8,128)S(1)}, u32[]{:S(2)}, u32[]{:S(2)}) collective-permute-start(f32[24,32,128]{2,1,0:T(8,128)S(1)} %pad_maximum_fusion.8), channel_id=1, source_target_pairs={{192,96},{193,97},{194,98},{195,99},{196,100},{197,101},{198,102},... | collective-permute-start | bytes 1179656 | tf_op jit(solution)/shard_map/ppermute | solution.py:281
  73.6 12.3 %collective-permute-start.20 = (f32[36,32,128]{2,1,0:T(8,128)S(1)}, f32[36,32,128]{2,1,0:T(8,128)S(1)}, u32[]{:S(2)}, u32[]{:S(2)}) collective-permute-start(f32[36,32,128]{2,1,0:T(8,128)S(1)} %pad_maximum_fusion.4.defect), channel_id=1, source_target_pairs={{352,288},{353,289},{354,290},{355,291},{356,292},{357,293},{358,2... | collective-permute-start | bytes 1769480 | tf_op jit(solution)/shard_map/ppermute | solution.py:281
  76.4 9.0 %collective-permute-start.19 = (f32[40,32,128]{2,1,0:T(8,128)S(1)}, f32[40,32,128]{2,1,0:T(8,128)S(1)}, u32[]{:S(2)}, u32[]{:S(2)}) collective-permute-start(f32[40,32,128]{2,1,0:T(8,128)S(1)} %pad_maximum_fusion.3), channel_id=1, source_target_pairs={{320,288},{321,289},{322,290},{323,291},{324,292},{325,293},{326,2... | collective-permute-start | bytes 1966088 | tf_op jit(solution)/shard_map/ppermute | solution.py:281
  78.4 1.5 collective-permute-start.14
  79.1 1.4 collective-permute-start.15
  79.9 1.5 collective-permute-start.16
  80.6 3.0 %collective-permute-start.18 = (f32[48,32,128]{2,1,0:T(8,128)}, f32[48,32,128]{2,1,0:T(8,128)S(1)}, u32[]{:S(2)}, u32[]{:S(2)}) collective-permute-start(f32[48,32,128]{2,1,0:T(8,128)} %pad_maximum_fusion.1), channel_id=1, source_target_pairs={{256,288},{257,289},{258,290},{259,291},{260,292},{261,293},{262,2... | collective-permute-start | bytes 2359304 | tf_op jit(solution)/shard_map/ppermute | solution.py:281
  81.3 0.8 collective-permute-start.17
  82.1 7.0 %collective-permute-start.23 = (f32[28,32,128]{2,1,0:T(8,128)S(1)}, f32[28,32,128]{2,1,0:T(8,128)S(1)}, u32[]{:S(2)}, u32[]{:S(2)}) collective-permute-start(f32[28,32,128]{2,1,0:T(8,128)S(1)} %pad_maximum_fusion.6), channel_id=1, source_target_pairs={{416,480},{417,481},{418,482},{419,483},{420,484},{421,485},{422,4... | collective-permute-start | bytes 1376264 | tf_op jit(solution)/shard_map/ppermute | solution.py:281
  83.5 4.5 %collective-permute-start.22 = (f32[32,32,128]{2,1,0:T(8,128)S(1)}, f32[32,32,128]{2,1,0:T(8,128)S(1)}, u32[]{:S(2)}, u32[]{:S(2)}) collective-permute-start(f32[32,32,128]{2,1,0:T(8,128)S(1)} %pad_maximum_fusion.5), channel_id=1, source_target_pairs={{384,480},{385,481},{386,482},{387,483},{388,484},{389,485},{390,4... | collective-permute-start | bytes 1572872 | tf_op jit(solution)/shard_map/ppermute | solution.py:281
  86.4 2.3 %collective-permute-start.21 = (f32[36,32,128]{2,1,0:T(8,128)S(1)}, f32[36,32,128]{2,1,0:T(8,128)S(1)}, u32[]{:S(2)}, u32[]{:S(2)}) collective-permute-start(f32[36,32,128]{2,1,0:T(8,128)S(1)} %shard_map.62), channel_id=1, source_target_pairs={{288,480},{289,481},{290,482},{291,483},{292,484},{293,485},{294,4... | collective-permute-start | bytes 1769480 | tf_op jit(solution)/shard_map/ppermute | solution.py:281
  87.2 5.0 %collective-permute-start.27 = (f32[3,8,32,128]{3,2,1,0:T(8,128)S(1)}, f32[3,8,32,128]{3,2,1,0:T(8,128)S(1)}, u32[]{:S(2)}, u32[]{:S(2)}) collective-permute-start(f32[3,8,32,128]{3,2,1,0:T(8,128)S(1)} %maximum_select_fusion.9), channel_id=1, source_target_pairs={{288,384},{289,385},{290,386},{291,387},{292,388},{293,389},{294,3... | collective-permute-start | bytes 1179656 | tf_op jit(solution)/shard_map/ppermute | solution.py:362
  88.0 4.1 %collective-permute-start.28 = (f32[3,8,32,128]{3,2,1,0:T(8,128)S(1)}, f32[3,8,32,128]{3,2,1,0:T(8,128)S(1)}, u32[]{:S(2)}, u32[]{:S(2)}) collective-permute-start(f32[3,8,32,128]{3,2,1,0:T(8,128)S(1)} %maximum_select_fusion.10), channel_id=1, source_target_pairs={{288,256},{289,257},{290,258},{291,259},{292,260},{293,261},{294,2... | collective-permute-start | bytes 1179656 | tf_op jit(solution)/shard_map/ppermute | solution.py:362
  89.7 2.5 %collective-permute-start.25 = (f32[3,8,32,128]{3,2,1,0:T(8,128)S(1)}, f32[3,8,32,128]{3,2,1,0:T(8,128)S(1)}, u32[]{:S(2)}, u32[]{:S(2)}) collective-permute-start(f32[3,8,32,128]{3,2,1,0:T(8,128)S(1)} %maximum_select_fusion.4), channel_id=1, source_target_pairs={{480,416},{481,417},{482,418},{483,419},{484,420},{485,421},{486,4... | collective-permute-start | bytes 1179656 | tf_op jit(solution)/shard_map/ppermute | solution.py:362
  90.5 64.0 %collective-permute-start.26 = (f32[3,8,32,128]{3,2,1,0:T(8,128)S(1)}, f32[3,8,32,128]{3,2,1,0:T(8,128)S(1)}, u32[]{:S(2)}, u32[]{:S(2)}) collective-permute-start(f32[3,8,32,128]{3,2,1,0:T(8,128)S(1)} %maximum_select_fusion.7), channel_id=1, source_target_pairs={{480,448},{481,449},{482,450},{483,451},{484,452},{485,453},{486,4... | collective-permute-start | bytes 1179656 | tf_op jit(solution)/shard_map/ppermute | solution.py:362
  91.8 62.6 %copy-start.1 = (f32[3,8,32,128]{3,2,1,0:T(8,128)S(1)}, f32[3,8,32,128]{3,2,1,0:T(8,128)}, u32[]{:S(2)}) copy-start(f32[3,8,32,128]{3,2,1,0:T(8,128)} %get-tuple-element.6.centre) | copy-start | bytes 1179652
  (2 other events, 1.9 us)

commit v3 on v2

--- a/solution.py
+++ b/solution.py
@@ -26,6 +26,14 @@
 
 BLOCKS = ((1, range(2, 3)), (3, range(3, 8)), (9, range(8, 13)), (15, range(13, 16)))
 PHASE_END = {k: 7 if k < 8 else 15 for k in range(1, 16)}
+GATHERS = (
+    (6, ((0, 1), (8, 9))),
+    (7, ((2, 3), (7, 9), (14, 15))),
+    (3, ((4, 3), (11, 9), (12, 15))),
+    (1, ((5, 3), (13, 15))),
+    (0, ((6, 3),)),
+)
+GATHER_WITH_STATE = (5, ((1, 3), (10, 9)))
 ROUNDS = (
     ((15, 13, 13), (9, 10, 10), (3, 4, 4), (1, 2, 2)),
     ((15, 14, 14), (9, 11, 11), (3, 5, 5)),
@@ -134,10 +142,11 @@
             for k in range(5):
                 store4(tabs, out[k], k, part * TILE + i)
             return 0
-        lax.fori_loop(0, TILE, one, 0)
-
-
-def fine_steps(bufs, tabs, ps, finish, ends, first_extra=None):
+        loop(0, TILE, one)
+
+
+def fine_steps(bufs, tabs, strain, finish, ends, first_extra=None):
+    load_strain, store_strain = strain
     for t in range(RATIO):
         src, dst = bufs[t % 2], bufs[(t + 1) % 2]
 
@@ -148,11 +157,11 @@
             if tile:
                 i = l - TILE
                 if t == 0:
-                    store4(ps, inc_p, i)
                     if first_extra is not None:
-                        first_extra(i, here_t, here_w, inc_t, inc_p, inc_w)
+                        inc_p = first_extra(i, here_t, here_w, inc_t, inc_p, inc_w)
+                    store_strain(inc_p, i)
                 else:
-                    store4(ps, plus(load4(ps, i), inc_p), i)
+                    store_strain(plus(load_strain(i), inc_p), i)
             if t == RATIO - 1:
                 finish(l - TILE, new_t, new_w)
             else:
@@ -177,7 +186,7 @@
     lax.fori_loop(0, TILE, one, 0)
 
 
-def relax_kernel(flag, centre, pressure, left, right, soil, out, tabs, a, b, ps):
+def relax_kernel(flag, centre, left, right, soil, out, ps, tabs, a, b):
     ends = edges()
     make_tables(
         flag,
@@ -192,43 +201,57 @@
 
     def finish(i, theta, w):
         store_rows(out, theta, 0, i)
-        store_rows(out, w, 2, i)
-
-    fine_steps((a, b), tabs, ps, finish, ends)
-
-    def strain(i, _):
-        store_rows(out, plus(load_rows(pressure, i), load4(ps, i)), 1, i)
-        return 0
-    lax.fori_loop(0, TILE, strain, 0)
-
-
-def defect_kernel(flag, centre, left, right, tabs, out, out_p, a, b, ps, coarse):
+        store_rows(out, w, 1, i)
+
+    strain = (lambda i: load4(ps, i), lambda rows, i: store4(ps, rows, i))
+    fine_steps((a, b), tabs, strain, finish, ends)
+
+
+def defect_kernel(flag, centre, left, right, tabs, start_p, first_ps, out, ps, a, b, coarse):
     ends = edges()
-    gather_ext(a, left, centre, right, ((0, 0, 0), (1, 2, 1)))
+    gather_ext(a, left, centre, right, ((0, 0, 0), (1, 1, 1)))
     later = 1.0 - flag[2]
 
     def first_extra(i, here_t, here_w, inc_t, inc_p, inc_w):
         store4(coarse, [later * (v + RATIO * d) for v, d in zip(here_t, inc_t)], 0, i)
-        store4(coarse, [(later * RATIO) * d for d in inc_p], 1, i)
-        store4(coarse, [later * (v + RATIO * d) for v, d in zip(here_w, inc_w)], 2, i)
+        store4(coarse, [later * (v + RATIO * d) for v, d in zip(here_w, inc_w)], 1, i)
+        rows = zip(inc_p, load_rows(start_p, 1, i), load4(first_ps, i))
+        return [(1.0 - RATIO * later) * d + flag[2] * (p + q) for d, p, q in rows]
 
     def finish(i, theta, w):
         store_rows(out, [v - g for v, g in zip(theta, load4(coarse, 0, i))], 0, i)
-        store_rows(out, [v - g for v, g in zip(w, load4(coarse, 2, i))], 1, i)
-
-    fine_steps((a, b), tabs, ps, finish, ends, first_extra)
-
-    def strain(i, _):
-        rows = zip(load_rows(centre, 1, i), load4(ps, i), load4(coarse, 1, i))
-        store_rows(out_p, [flag[2] * p + (s - g) for p, s, g in rows], i)
-        return 0
-    lax.fori_loop(0, TILE, strain, 0)
-
-
-def coarse_kernel(halo, state, tabs, defect, out):
+        store_rows(out, [v - g for v, g in zip(w, load4(coarse, 1, i))], 1, i)
+
+    strain = (lambda i: load_rows(ps, i), lambda rows, i: store_rows(ps, rows, i))
+    fine_steps((a, b), tabs, strain, finish, ends, first_extra)
+
+
+def pack_kernel(halos, left, centre, right, strain, *outs):
+    for h, out in zip(halos, outs):
+        wide = TILE + 2 * h
+        for f in range(2):
+            if h:
+                out[f * wide:f * wide + h] = left[f, AROUND - h:]
+                out[f * wide + h + TILE:(f + 1) * wide] = right[f, :h]
+            out[f * wide + h:f * wide + h + TILE] = centre[f]
+        out[2 * wide:] = strain[...]
+
+
+def copy_kernel(*refs):
+    n = len(refs) // 2
+    for source, target in zip(refs[:n], refs[n + 1:]):
+        target[...] = source[...]
+
+
+def strain_kernel(start_p, ps, out):
+    for i in range(TILE):
+        store_rows(out, plus(load_rows(start_p, i), load4(ps, i)), i)
+
+
+def coarse_kernel(halo, sent, state, tabs, defect, out):
     ends = edges()
     new = halo - 1
-    wide, narrow = TILE + 2 * halo, TILE + 2 * new
+    wide, narrow, other = TILE + 2 * halo, TILE + 2 * new, TILE + 2 * sent
 
     def one(o, _, tile=False):
         i = o + 1
@@ -236,10 +259,10 @@
         here_t, here_w, inc_t, inc_p, inc_w = increments(load, tabs, TILE - halo + i, ends)
         if tile:
             j = o - new
-            rows = zip(load_rows(state, 2 * wide + j), inc_p, load_rows(defect, 2 * narrow + j))
+            rows = zip(load_rows(state, 2 * wide + j), inc_p, load_rows(defect, 2 * other + j))
             store_rows(out, [(p + RATIO * v) + e for p, v, e in rows], 2 * narrow + j)
         for f, here, inc in ((0, here_t, inc_t), (1, here_w, inc_w)):
-            rows = zip(here, inc, load_rows(defect, f * narrow + o))
+            rows = zip(here, inc, load_rows(defect, f * other + sent - new + o))
             store_rows(out, [(v + RATIO * x) + e for v, x, e in rows], f * narrow + o)
         return 0
 
@@ -248,19 +271,20 @@
     loop(new + TILE, narrow, one)
 
 
-def call(kernel, outs, scratch, n_in, smem_first=True, **kw):
-    specs = [VMEM() for _ in range(n_in)]
-    if smem_first:
-        specs[0] = SMEM()
+def call(kernel, outs, scratch, specs):
     return pl.pallas_call(
         kernel,
         out_shape=[jax.ShapeDtypeStruct(s, F32) for s in outs],
         in_specs=specs,
         out_specs=[VMEM() for _ in outs],
         scratch_shapes=[pltpu.VMEM(s, F32) for s in scratch],
-        compiler_params=pltpu.CompilerParams(vmem_limit_bytes=24 * 2**20),
-        **kw,
+        compiler_params=pltpu.CompilerParams(vmem_limit_bytes=12 * 2**20),
     )
+
+
+def after(arrays, wait):
+    specs = [VMEM() for _ in arrays] + [pl.BlockSpec(memory_space=pl.ANY)]
+    return call(copy_kernel, [a.shape for a in arrays], [], specs)(*arrays, wait)
 
 
 LAYER = (32, 128)
@@ -286,72 +310,91 @@
     from_left = shifted(packed, 1, 1)
     from_right = shifted(packed, 1, -1)
     centre = shifted(heat_stress, 1, 0)
-    pressure = shifted(mine[1], 1, 0)
-    relaxed, tabs = call(
+    kept, grown, tabs = call(
         relax_kernel,
-        [(3, TILE, *LAYER), (5, EXT * 4, *REGS)],
-        [(2, EXT * 4, *REGS), (2, EXT * 4, *REGS), (TILE * 4, *REGS)],
-        6,
-    )(flag, centre, pressure, from_left, from_right, soil)
-
-    heat_stress = jnp.stack([relaxed[0], relaxed[2]])
-    from_left = shifted(heat_stress, 0, 1)
-    from_right = shifted(heat_stress, 0, -1)
+        [(2, TILE, *LAYER), (TILE * 4, *REGS), (5, EXT * 4, *REGS)],
+        [(2, EXT * 4, *REGS), (2, EXT * 4, *REGS)],
+        [SMEM(), *[VMEM() for _ in range(4)]],
+    )(flag, centre, from_left, from_right, soil)
+
+    from_left = shifted(kept, 0, 1)
+    from_right = shifted(kept, 0, -1)
     defect, strain = call(
         defect_kernel,
         [(2, TILE, *LAYER), (TILE, *LAYER)],
-        [(2, EXT * 4, *REGS), (2, EXT * 4, *REGS), (TILE * 4, *REGS), (3, TILE * 4, *REGS)],
-        5,
-    )(flag, relaxed, from_left, from_right, tabs)
+        [(2, EXT * 4, *REGS), (2, EXT * 4, *REGS), (2, TILE * 4, *REGS)],
+        [SMEM(), *[VMEM() for _ in range(6)]],
+    )(flag, kept, from_left, from_right, tabs, initial_state, grown)
 
     around = AROUND
     left = shifted(defect[:, TILE - around:], 0, 1)
     right = shifted(defect[:, :around], 0, -1)
-    widened = jnp.concatenate([left, defect, right], axis=1)
-
-    def with_halo(h):
-        sides = widened[:, around - h:around + TILE + h]
-        return jnp.concatenate([sides.reshape(-1, *LAYER), strain])
-
-    def step(halo, state, term):
-        (out,) = call(
-            functools.partial(coarse_kernel, halo), [(2 * (TILE + 2 * halo - 2) + TILE, *LAYER)], [], 3, smem_first=False
-        )(state, tabs, term)
-        return out
+    halos = [h for h, _ in GATHERS] + [GATHER_WITH_STATE[0]]
+    packs = call(
+        functools.partial(pack_kernel, halos),
+        [(2 * (TILE + 2 * h) + TILE, *LAYER) for h in halos],
+        [],
+        [VMEM() for _ in range(4)],
+    )(left, defect, right, strain)
+    with_halo = dict(zip(halos, packs)).get
 
     def tile_of(state, h):
         layers = TILE + 2 * h
         return jnp.stack([state[h:h + TILE], state[2 * layers:], state[layers + h:layers + h + TILE]])
 
-    state, holder = with_halo(PHASE_END[2] - 1), 0
-    results = {}
+    terms = {}
+
+    def gather(payload, h, sends):
+        got = lax.ppermute(payload, both, [(a * ns + b, c * ns + b) for a, c in sends for b in range(ns)])
+        for a, _ in sends:
+            terms[a + 1] = (h, got)
+        return got
+
+    def step(k, state):
+        halo = PHASE_END[k] - k + 1
+        sent, term = terms.get(k) or (halo - 1, with_halo(halo - 1))
+        (out,) = call(
+            functools.partial(coarse_kernel, halo, sent),
+            [(2 * (TILE + 2 * halo - 2) + TILE, *LAYER)],
+            [],
+            [VMEM() for _ in range(3)],
+        )(state, tabs, term)
+        return out
+
+    state = [gather(with_halo(h), h, sends) for h, sends in GATHERS][0]
+    del terms[1]
+    results = {1: tile_of(state, GATHERS[0][0])}
+    holder = None
     for worker, steps in BLOCKS:
         first = steps[0]
         halo = PHASE_END[first] - first + 1
-        hop = worker - holder
-        if PHASE_END[first] == PHASE_END[first - 1]:
-            state = shifted(state, hop, 0, [holder])
+        if holder is None:
+            pass
+        elif holder == BLOCKS[0][0]:
+            h, sends = GATHER_WITH_STATE
+            state = gather(jnp.where(t == holder, state, with_halo(h)), h, sends)
+            del terms[holder + 1]
+        elif PHASE_END[first] == PHASE_END[first - 1]:
+            state = shifted(state, worker - holder, 0, [holder])
         else:
+            hop = worker - holder
             tile = state[:2 * TILE]
             before = shifted(tile, hop, 1, [holder])
-            after = shifted(tile, hop, -1, [holder])
+            following = shifted(tile, hop, -1, [holder])
             state = shifted(state, hop, 0, [holder])
             parts = []
             for f in range(2):
                 own = slice(f * TILE, (f + 1) * TILE)
-                parts += [before[own][TILE - halo:], state[own], after[own][:halo]]
+                parts += [before[own][TILE - halo:], state[own], following[own][:halo]]
             state = jnp.concatenate([*parts, state[2 * TILE:]])
-        if first == 2:
-            results[1] = tile_of(state, halo)
-        terms = {}
         for k in steps:
-            mine = with_halo(PHASE_END[k] - k)
-            terms[k] = mine if k - 1 == worker else shifted(mine, worker - k + 1, 0, [k - 1])
-        for k in steps:
-            state = step(PHASE_END[k] - k + 1, state, terms[k])
+            state = step(k, state)
             results[k] = tile_of(state, PHASE_END[k] - k)
         holder = worker
 
+    (start_p,) = after([mine[1]], results[8])
+    (relaxed_p,) = call(strain_kernel, [(TILE, *LAYER)], [], [VMEM(), VMEM()])(shifted(start_p, 1, 0), grown)
+    relaxed = jnp.stack([kept[0], relaxed_p, kept[1]])
     corrected = jnp.where(t == 0, relaxed, 0.0)
     for sends in ROUNDS:
         payload = results[sends[0][1]]

time: 156 us -> 148 us (0.949)
  waiting for transfers between devices: 84.9 us -> 69.8 us
  Pallas kernels: 15 us -> 19.8 us
  local copies, waits for them, and re-layouts: 5.69 us -> 10.2 us
  starting transfers between devices: 43.6 us -> 40.7 us
    ppermute x4, waiting for transfers between devices: 62.3 us -> 35 us  [on_device(): corrected = corrected + lax.ppermute(payload, both, pairs)]
    ppermute x25 -> x12, starting transfers between devices: 40.3 us -> 27 us  [shifted(): return lax.ppermute(x, both, pairs)]
    ppermute x0 -> x6, starting transfers between devices: none -> 10.3 us  [gather(): lax.ppermute(payload, both, [(a * ns + b, c * ns + b) for a, c in sends f...]
    ppermute x0 -> x6, waiting for transfers between devices: none -> 6.55 us  [gather(): lax.ppermute(payload, both, [(a * ns + b, c * ns + b) for a, c in sends f...]
    ppermute x25 -> x12, waiting for transfers between devices: 22.6 us -> 28.3 us  [shifted(): return lax.ppermute(x, both, pairs)]
    pallas_call x15 -> x18, Pallas kernels: 11.1 us -> 16 us  [the longest x14 10.6 us: step(): call(functools.partial(coarse_kernel, halo, sent), [(2 * (TILE + 2 * halo...]
    unnamed x18 -> x34, local copies, waits for them, and re-layouts: 1.99 us -> 5.98 us
    slice x7 -> x1, local copies, waits for them, and re-layouts: 3.16 us -> 0.99 us  [on_device(): relaxed = jnp.stack([kept[0], relaxed_p, kept[1]])]
  transfers between devices with their start and end apart: 29 -> 22, of which waited for: 7 -> 8; matrix products, arithmetic and copies ran while one was open for 2% -> 4% of each run, Pallas kernels for 4% -> 4%
where the time goes in v3:
time: 148 us; the launch traced here: 147 us
  waiting for transfers between devices  69.8 us (47%)
  starting transfers between devices  40.7 us (28%)
  Pallas kernels  19.8 us (13%)
  local copies, waits for them, and re-layouts  10.2 us (7%)
  other arithmetic  5.52 us (4%)
    ppermute x4, waiting for transfers between devices, on_device(): corrected = corrected + lax.ppermute(payload, both, pairs)  35 us
    ppermute x12, waiting for transfers between devices, shifted(): return lax.ppermute(x, both, pairs)  28.3 us
    ppermute x12, starting transfers between devices, shifted(): return lax.ppermute(x, both, pairs)  27 us
    pallas_call x14, Pallas kernels, step(): call(functools.partial(coarse_kernel, halo, sent), [(2 * (TILE + 2 * halo...  10.6 us
    ppermute x6, starting transfers between devices, gather(): lax.ppermute(payload, both, [(a * ns + b, c * ns + b) for a, c in sends f...  10.3 us
    ppermute x6, waiting for transfers between devices, gather(): lax.ppermute(payload, both, [(a * ns + b, c * ns + b) for a, c in sends f...  6.55 us
    unnamed x34, local copies, waits for them, and re-layouts  5.98 us
    pallas_call x1, Pallas kernels, on_device(): call(relax_kernel, [(2, TILE, *LAYER), (TILE * 4, *REGS), (5, EXT * 4, *R...  4.15 us
  transfers between devices with their start and end apart: 22, of which 8 were waited for; matrix products, arithmetic and copies ran while one was open for 4% of the time, Pallas kernels for 4%

profile of v3, /device:TPU:47, one launch (start us, length us, event | category | flops | bytes accessed | tf_op | source)
XLA Modules:
  0.0 147.4 jit_solution(16578485308389513756)
XLA Ops:
  1.6 1.1 bitcast_select_fusion
  3.5 11.6 %collective-permute-start.2 = (f32[3,8,32,128]{3,2,1,0:T(8,128)S(1)}, f32[3,8,32,128]{3,2,1,0:T(8,128)S(1)}, u32[]{:S(2)}, u32[]{:S(2)}) collective-permute-start(f32[3,8,32,128]{3,2,1,0:T(8,128)S(1)} %pad_maximum_fusion), channel_id=1, source_target_pairs={{1,32},{2,33},{3,34},{4,35},{5,36},{6,37},{7,38},{8,39},{9,40},{10... | collective-permute-start | bytes 1179656 | tf_op jit(solution)/shard_map/ppermute | solution.py:305
  15.1 1.9 %collective-permute-start.1 = (f32[3,8,32,128]{3,2,1,0:T(8,128)S(1)}, f32[3,8,32,128]{3,2,1,0:T(8,128)S(1)}, u32[]{:S(2)}, u32[]{:S(2)}) collective-permute-start(f32[3,8,32,128]{3,2,1,0:T(8,128)S(1)} %pad_maximum_fusion), channel_id=1, source_target_pairs={{0,33},{1,34},{2,35},{3,36},{4,37},{5,38},{6,39},{7,40},{8,41},{9,... | collective-permute-start | bytes 1179656 | tf_op jit(solution)/shard_map/ppermute | solution.py:305
  17.2 9.7 %collective-permute-done.centre = f32[2,8,32,128]{3,2,1,0:T(8,128)S(1)} collective-permute-done((f32[2,8,32,128]{3,2,1,0:T(8,128)S(1)}, f32[2,8,32,128]{3,2,1,0:T(8,128)S(1)}, u32[]{:S(2)}, u32[]{:S(2)}) %collective-permute-start) | collective-permute-done | bytes 262176 | tf_op jit(solution)/shard_map/ppermute | solution.py:305
  26.9 3.5 %collective-permute-done.1.left = f32[3,8,32,128]{3,2,1,0:T(8,128)S(1)} collective-permute-done((f32[3,8,32,128]{3,2,1,0:T(8,128)S(1)}, f32[3,8,32,128]{3,2,1,0:T(8,128)S(1)}, u32[]{:S(2)}, u32[]{:S(2)}) %collective-permute-start.1) | collective-permute-done | bytes 393248 | tf_op jit(solution)/shard_map/ppermute | solution.py:305
  31.2 1.0 copy-done.10
  32.2 4.1 %shard_map.50 = (f32[2,8,32,128]{3,2,1,0:T(8,128)S(1)}, f32[32,8,128]{2,1,0:T(8,128)S(1)}, f32[5,96,8,128]{3,2,1,0:T(8,128)S(1)}) custom-call(f32[3]{0:T(128)S(1)} %add_convert_fusion.flag, f32[2,8,32,128]{3,2,1,0:T(8,128)S(1)} %collective-permute-done.centre, f32[3,8,32,128]{3,2,1,0:T(8,128)S(1)} %copy-done.10, ...), custom_call_target="tpu_custom_call" | custom-call | tf_op jit(solution)/shard_map/pallas_call | solution.py:313
  36.3 1.9 %collective-permute-start.4 = (f32[2,8,32,128]{3,2,1,0:T(8,128)S(1)}, f32[2,8,32,128]{3,2,1,0:T(8,128)S(1)}, u32[]{:S(2)}, u32[]{:S(2)}) collective-permute-start(f32[2,8,32,128]{3,2,1,0:T(8,128)S(1)} %get-tuple-element.13.centre), channel_id=1, source_target_pairs={{1,0},{2,1},{3,2},{4,3},{5,4},{6,5},{7,6},{8,7},{9,8},{10,9},{11,1... | collective-permute-start | bytes 786440 | tf_op jit(solution)/shard_map/ppermute | solution.py:305
  38.3 3.4 %collective-permute-start.3 = (f32[2,8,32,128]{3,2,1,0:T(8,128)S(1)}, f32[2,8,32,128]{3,2,1,0:T(8,128)S(1)}, u32[]{:S(2)}, u32[]{:S(2)}) collective-permute-start(f32[2,8,32,128]{3,2,1,0:T(8,128)S(1)} %get-tuple-element.13.centre), channel_id=1, source_target_pairs={{0,1},{1,2},{2,3},{3,4},{4,5},{5,6},{6,7},{7,8},{8,9},{9,10},{10,1... | collective-permute-start | bytes 786440 | tf_op jit(solution)/shard_map/ppermute | solution.py:305
  41.6 4.1 %collective-permute-done.4.right = f32[2,8,32,128]{3,2,1,0:T(8,128)S(1)} collective-permute-done((f32[2,8,32,128]{3,2,1,0:T(8,128)S(1)}, f32[2,8,32,128]{3,2,1,0:T(8,128)S(1)}, u32[]{:S(2)}, u32[]{:S(2)}) %collective-permute-start.4) | collective-permute-done | bytes 262176 | tf_op jit(solution)/shard_map/ppermute | solution.py:305
  45.7 4.3 %collective-permute-done.3.left = f32[2,8,32,128]{3,2,1,0:T(8,128)S(1)} collective-permute-done((f32[2,8,32,128]{3,2,1,0:T(8,128)S(1)}, f32[2,8,32,128]{3,2,1,0:T(8,128)S(1)}, u32[]{:S(2)}, u32[]{:S(2)}) %collective-permute-start.3) | collective-permute-done | bytes 262176 | tf_op jit(solution)/shard_map/ppermute | solution.py:305
  50.0 3.8 %shard_map.51 = (f32[2,8,32,128]{3,2,1,0:T(8,128)S(1)}, f32[8,32,128]{2,1,0:T(8,128)S(1)}) custom-call(f32[3]{0:T(128)S(1)} %add_convert_fusion.flag, f32[2,8,32,128]{3,2,1,0:T(8,128)S(1)} %get-tuple-element.13.centre, f32[2,8,32,128]{3,2,1,0:T(8,128)S(1)} %collective-permute-done.3.left, f32[2,8,32,128]{3,2,1,0:T(8,128)S(1)} %collective-permute-done.4.right, ...), custom_call_target="tpu_custom_call" | custom-call | tf_op jit(solution)/shard_map/pallas_call | solution.py:322
  53.9 1.9 %collective-permute-start.6 = (f32[2,7,32,128]{3,2,1,0:T(8,128)S(1)}, f32[2,7,32,128]{3,2,1,0:T(8,128)S(1)}, u32[]{:S(2)}, u32[]{:S(2)}) collective-permute-start(f32[2,7,32,128]{3,2,1,0:T(8,128)S(1)} %get-tuple-element.76), channel_id=1, source_target_pairs={{1,0},{2,1},{3,2},{4,3},{5,4},{6,5},{7,6},{8,7},{9,8},{10,9},{11,1... | collective-permute-start | bytes 688136 | tf_op jit(solution)/shard_map/ppermute | solution.py:305
  55.8 3.4 %collective-permute-start.5 = (f32[2,7,32,128]{3,2,1,0:T(8,128)S(1)}, f32[2,7,32,128]{3,2,1,0:T(8,128)S(1)}, u32[]{:S(2)}, u32[]{:S(2)}) collective-permute-start(f32[2,7,32,128]{3,2,1,0:T(8,128)S(1)} %get-tuple-element.77), channel_id=1, source_target_pairs={{0,1},{1,2},{2,3},{3,4},{4,5},{5,6},{6,7},{7,8},{8,9},{9,10},{10,1... | collective-permute-start | bytes 688136 | tf_op jit(solution)/shard_map/ppermute | solution.py:305
  59.2 2.7 %collective-permute-done.6.right = f32[2,7,32,128]{3,2,1,0:T(8,128)S(1)} collective-permute-done((f32[2,7,32,128]{3,2,1,0:T(8,128)S(1)}, f32[2,7,32,128]{3,2,1,0:T(8,128)S(1)}, u32[]{:S(2)}, u32[]{:S(2)}) %collective-permute-start.6) | collective-permute-done | bytes 229408 | tf_op jit(solution)/shard_map/ppermute | solution.py:305
  61.8 4.0 %collective-permute-done.5.left = f32[2,7,32,128]{3,2,1,0:T(8,128)S(1)} collective-permute-done((f32[2,7,32,128]{3,2,1,0:T(8,128)S(1)}, f32[2,7,32,128]{3,2,1,0:T(8,128)S(1)}, u32[]{:S(2)}, u32[]{:S(2)}) %collective-permute-start.5) | collective-permute-done | bytes 229408 | tf_op jit(solution)/shard_map/ppermute | solution.py:305
  65.9 1.1 shard_map.52
  70.3 1.5 %collective-permute-start.7 = (f32[48,32,128]{2,1,0:T(8,128)}, f32[48,32,128]{2,1,0:T(8,128)}, u32[]{:S(2)}, u32[]{:S(2)}) collective-permute-start(f32[48,32,128]{2,1,0:T(8,128)} %get-tuple-element.18), channel_id=1, source_target_pairs={{0,32},{1,33},{2,34},{3,35},{4,36},{5,37},{6,38},{7,39},{8,40},{9,... | collective-permute-start | bytes 2359304 | tf_op jit(solution)/shard_map/ppermute | solution.py:348
  72.6 1.7 %shard_map.53 = f32[44,32,128]{2,1,0:T(8,128)S(1)} custom-call(f32[48,32,128]{2,1,0:T(8,128)} %collective-permute-done.7.state.defect, f32[5,96,8,128]{3,2,1,0:T(8,128)S(1)} %get-tuple-element.14.tabs, f32[44,32,128]{2,1,0:T(8,128)S(1)} %get-tuple-element.19.defect), custom_call_target="tpu_custom_call" | custom-call | tf_op jit(solution)/shard_map/pallas_call | solution.py:356
  75.1 1.0 broadcast_select_fusion
  76.1 1.5 %collective-permute-start.8 = (f32[44,32,128]{2,1,0:T(8,128)}, f32[44,32,128]{2,1,0:T(8,128)}, u32[]{:S(2)}, u32[]{:S(2)}) collective-permute-start(f32[44,32,128]{2,1,0:T(8,128)} %broadcast_select_fusion), channel_id=1, source_target_pairs={{32,96},{33,97},{34,98},{35,99},{36,100},{37,101},{38,102},{39,103... | collective-permute-start | bytes 2162696 | tf_op jit(solution)/shard_map/ppermute | solution.py:348
  77.6 5.0 %collective-permute-start.10 = (f32[36,32,128]{2,1,0:T(8,128)}, f32[36,32,128]{2,1,0:T(8,128)S(1)}, u32[]{:S(2)}, u32[]{:S(2)}) collective-permute-start(f32[36,32,128]{2,1,0:T(8,128)} %copy-done.3), channel_id=1, source_target_pairs={{128,96},{129,97},{130,98},{131,99},{132,100},{133,101},{134,102},... | collective-permute-start | bytes 1769480 | tf_op jit(solution)/shard_map/ppermute | solution.py:348
  82.6 1.0 fusion.2
  85.2 1.1 slice_bitcast_fusion.29
  86.2 1.1 slice_bitcast_fusion.36
  87.3 1.7 %shard_map.54.state = f32[40,32,128]{2,1,0:T(8,128)S(1)} custom-call(f32[44,32,128]{2,1,0:T(8,128)} %collective-permute-done.8.state.defect, f32[5,96,8,128]{3,2,1,0:T(8,128)S(1)} %get-tuple-element.14.tabs, f32[52,32,128]{2,1,0:T(8,128)S(1)} %collective-permute-done.9.defect), custom_call_target="tpu_custom_call" | custom-call | tf_op jit(solution)/shard_map/pallas_call | solution.py:356
  89.4 6.5 %collective-permute-done.10.defect = f32[36,32,128]{2,1,0:T(8,128)S(1)} collective-permute-done((f32[36,32,128]{2,1,0:T(8,128)}, f32[36,32,128]{2,1,0:T(8,128)S(1)}, u32[]{:S(2)}, u32[]{:S(2)}) %collective-permute-start.10) | collective-permute-done | bytes 589856 | tf_op jit(solution)/shard_map/ppermute | solution.py:348
  100.1 1.7 %shard_map.60.state = f32[48,32,128]{2,1,0:T(8,128)S(1)} custom-call(f32[52,32,128]{2,1,0:T(8,128)S(1)} %shard_map.59.state, f32[5,96,8,128]{3,2,1,0:T(8,128)S(1)} %get-tuple-element.14.tabs, f32[48,32,128]{2,1,0:T(8,128)} %collective-permute-done.7.state.defect), custom_call_target="tpu_custom_call" | custom-call | tf_op jit(solution)/shard_map/pallas_call | solution.py:356
  102.4 1.6 %shard_map.62.state = f32[40,32,128]{2,1,0:T(8,128)S(1)} custom-call(f32[44,32,128]{2,1,0:T(8,128)S(1)} %shard_map.61.state, f32[5,96,8,128]{3,2,1,0:T(8,128)S(1)} %get-tuple-element.14.tabs, f32[44,32,128]{2,1,0:T(8,128)} %collective-permute-done.8.state.defect), custom_call_target="tpu_custom_call" | custom-call | tf_op jit(solution)/shard_map/pallas_call | solution.py:356
  108.7 1.3 collective-permute-start.19
  111.3 35.0 %collective-permute-done.19 = f32[3,8,32,128]{3,2,1,0:T(8,128)S(1)} collective-permute-done((f32[3,8,32,128]{3,2,1,0:T(8,128)S(1)}, f32[3,8,32,128]{3,2,1,0:T(8,128)S(1)}, u32[]{:S(2)}, u32[]{:S(2)}) %collective-permute-start.19) | collective-permute-done | bytes 393248 | tf_op jit(solution)/shard_map/ppermute | solution.py:405
  146.2 1.2 fusion
  (96 shorter events, 19.7 us)
Async XLA Ops:
  0.6 30.6 %copy-start.7 = (s32[8,32,128]{2,1,0:T(8,128)S(1)}, s32[8,32,128]{2,1,0:T(8,128)}, u32[]{:S(2)}) copy-start(s32[8,32,128]{2,1,0:T(8,128)} %soil.1) | copy-start | bytes 393220
  1.6 48.3 %copy-start.1 = (f32[3,8,32,128]{3,2,1,0:T(8,128)S(1)}, f32[3,8,32,128]{3,2,1,0:T(8,128)}, u32[]{:S(2)}) copy-start(f32[3,8,32,128]{3,2,1,0:T(8,128)} %start_p.1) | copy-start | bytes 1179652
  3.5 23.4 %collective-permute-start.2 = (f32[3,8,32,128]{3,2,1,0:T(8,128)S(1)}, f32[3,8,32,128]{3,2,1,0:T(8,128)S(1)}, u32[]{:S(2)}, u32[]{:S(2)}) collective-permute-start(f32[3,8,32,128]{3,2,1,0:T(8,128)S(1)} %pad_maximum_fusion), channel_id=1, source_target_pairs={{1,32},{2,33},{3,34},{4,35},{5,36},{6,37},{7,38},{8,39},{9,40},{10... | collective-permute-start | bytes 1179656 | tf_op jit(solution)/shard_map/ppermute | solution.py:305
  15.1 15.3 %collective-permute-start.1 = (f32[3,8,32,128]{3,2,1,0:T(8,128)S(1)}, f32[3,8,32,128]{3,2,1,0:T(8,128)S(1)}, u32[]{:S(2)}, u32[]{:S(2)}) collective-permute-start(f32[3,8,32,128]{3,2,1,0:T(8,128)S(1)} %pad_maximum_fusion), channel_id=1, source_target_pairs={{0,33},{1,34},{2,35},{3,36},{4,37},{5,38},{6,39},{7,40},{8,41},{9,... | collective-permute-start | bytes 1179656 | tf_op jit(solution)/shard_map/ppermute | solution.py:305
  17.0 9.9 %collective-permute-start = (f32[2,8,32,128]{3,2,1,0:T(8,128)S(1)}, f32[2,8,32,128]{3,2,1,0:T(8,128)S(1)}, u32[]{:S(2)}, u32[]{:S(2)}) collective-permute-start(f32[2,8,32,128]{3,2,1,0:T(8,128)S(1)} %pad_maximum_fusion.3), channel_id=1, source_target_pairs={{0,32},{1,33},{2,34},{3,35},{4,36},{5,37},{6,38},{7,39},{8,40},{9,... | collective-permute-start | bytes 786440 | tf_op jit(solution)/shard_map/ppermute | solution.py:305
  31.2 1.0 copy-start.10
  36.3 17.5 %copy-start.2 = (f32[2,8,32,128]{3,2,1,0:T(8,128)}, f32[2,8,32,128]{3,2,1,0:T(8,128)S(1)}, u32[]{:S(2)}) copy-start(f32[2,8,32,128]{3,2,1,0:T(8,128)S(1)} %get-tuple-element.13.centre) | copy-start | bytes 786436
  36.3 17.5 %copy-start.5 = (f32[32,8,128]{2,1,0:T(8,128)}, f32[32,8,128]{2,1,0:T(8,128)S(1)}, u32[]{:S(2)}) copy-start(f32[32,8,128]{2,1,0:T(8,128)S(1)} %get-tuple-element.15.first_ps.ps) | copy-start | bytes 393220
  36.3 9.4 %collective-permute-start.4 = (f32[2,8,32,128]{3,2,1,0:T(8,128)S(1)}, f32[2,8,32,128]{3,2,1,0:T(8,128)S(1)}, u32[]{:S(2)}, u32[]{:S(2)}) collective-permute-start(f32[2,8,32,128]{3,2,1,0:T(8,128)S(1)} %get-tuple-element.13.centre), channel_id=1, source_target_pairs={{1,0},{2,1},{3,2},{4,3},{5,4},{6,5},{7,6},{8,7},{9,8},{10,9},{11,1... | collective-permute-start | bytes 786440 | tf_op jit(solution)/shard_map/ppermute | solution.py:305
  38.3 11.7 %collective-permute-start.3 = (f32[2,8,32,128]{3,2,1,0:T(8,128)S(1)}, f32[2,8,32,128]{3,2,1,0:T(8,128)S(1)}, u32[]{:S(2)}, u32[]{:S(2)}) collective-permute-start(f32[2,8,32,128]{3,2,1,0:T(8,128)S(1)} %get-tuple-element.13.centre), channel_id=1, source_target_pairs={{0,1},{1,2},{2,3},{3,4},{4,5},{5,6},{6,7},{7,8},{8,9},{9,10},{10,1... | collective-permute-start | bytes 786440 | tf_op jit(solution)/shard_map/ppermute | solution.py:305
  53.9 8.0 %collective-permute-start.6 = (f32[2,7,32,128]{3,2,1,0:T(8,128)S(1)}, f32[2,7,32,128]{3,2,1,0:T(8,128)S(1)}, u32[]{:S(2)}, u32[]{:S(2)}) collective-permute-start(f32[2,7,32,128]{3,2,1,0:T(8,128)S(1)} %get-tuple-element.76), channel_id=1, source_target_pairs={{1,0},{2,1},{3,2},{4,3},{5,4},{6,5},{7,6},{8,7},{9,8},{10,9},{11,1... | collective-permute-start | bytes 688136 | tf_op jit(solution)/shard_map/ppermute | solution.py:305
  55.8 10.1 %collective-permute-start.5 = (f32[2,7,32,128]{3,2,1,0:T(8,128)S(1)}, f32[2,7,32,128]{3,2,1,0:T(8,128)S(1)}, u32[]{:S(2)}, u32[]{:S(2)}) collective-permute-start(f32[2,7,32,128]{3,2,1,0:T(8,128)S(1)} %get-tuple-element.77), channel_id=1, source_target_pairs={{0,1},{1,2},{2,3},{3,4},{4,5},{5,6},{6,7},{7,8},{8,9},{9,10},{10,1... | collective-permute-start | bytes 688136 | tf_op jit(solution)/shard_map/ppermute | solution.py:305
  67.8 0.9 copy-start.11
  70.3 2.3 %collective-permute-start.7 = (f32[48,32,128]{2,1,0:T(8,128)}, f32[48,32,128]{2,1,0:T(8,128)}, u32[]{:S(2)}, u32[]{:S(2)}) collective-permute-start(f32[48,32,128]{2,1,0:T(8,128)} %get-tuple-element.18), channel_id=1, source_target_pairs={{0,32},{1,33},{2,34},{3,35},{4,36},{5,37},{6,38},{7,39},{8,40},{9,... | collective-permute-start | bytes 2359304 | tf_op jit(solution)/shard_map/ppermute | solution.py:348
  71.8 15.5 %collective-permute-start.9 = (f32[52,32,128]{2,1,0:T(8,128)}, f32[52,32,128]{2,1,0:T(8,128)S(1)}, u32[]{:S(2)}, u32[]{:S(2)}) collective-permute-start(f32[52,32,128]{2,1,0:T(8,128)} %copy-done.11), channel_id=1, source_target_pairs={{64,96},{65,97},{66,98},{67,99},{68,100},{69,101},{70,102},{71,103... | collective-permute-start | bytes 2555912 | tf_op jit(solution)/shard_map/ppermute | solution.py:348
  74.2 0.9 copy-start
  76.1 11.3 %collective-permute-start.8 = (f32[44,32,128]{2,1,0:T(8,128)}, f32[44,32,128]{2,1,0:T(8,128)}, u32[]{:S(2)}, u32[]{:S(2)}) collective-permute-start(f32[44,32,128]{2,1,0:T(8,128)} %broadcast_select_fusion), channel_id=1, source_target_pairs={{32,96},{33,97},{34,98},{35,99},{36,100},{37,101},{38,102},{39,103... | collective-permute-start | bytes 2162696 | tf_op jit(solution)/shard_map/ppermute | solution.py:348
  77.6 18.4 %collective-permute-start.10 = (f32[36,32,128]{2,1,0:T(8,128)}, f32[36,32,128]{2,1,0:T(8,128)S(1)}, u32[]{:S(2)}, u32[]{:S(2)}) collective-permute-start(f32[36,32,128]{2,1,0:T(8,128)} %copy-done.3), channel_id=1, source_target_pairs={{128,96},{129,97},{130,98},{131,99},{132,100},{133,101},{134,102},... | collective-permute-start | bytes 1769480 | tf_op jit(solution)/shard_map/ppermute | solution.py:348
  83.6 13.2 %collective-permute-start.12 = (f32[24,32,128]{2,1,0:T(8,128)}, f32[24,32,128]{2,1,0:T(8,128)S(1)}, u32[]{:S(2)}, u32[]{:S(2)}) collective-permute-start(f32[24,32,128]{2,1,0:T(8,128)} %copy-done.13), channel_id=1, source_target_pairs={{192,96},{193,97},{194,98},{195,99},{196,100},{197,101},{198,102},... | collective-permute-start | bytes 1179656 | tf_op jit(solution)/shard_map/ppermute | solution.py:348
  84.3 12.1 %collective-permute-start.11 = (f32[28,32,128]{2,1,0:T(8,128)}, f32[28,32,128]{2,1,0:T(8,128)S(1)}, u32[]{:S(2)}, u32[]{:S(2)}) collective-permute-start(f32[28,32,128]{2,1,0:T(8,128)} %copy-done.12), channel_id=1, source_target_pairs={{160,96},{161,97},{162,98},{163,99},{164,100},{165,101},{166,102},... | collective-permute-start | bytes 1376264 | tf_op jit(solution)/shard_map/ppermute | solution.py:348
  87.3 1.7 %copy-start.4 = (f32[36,32,128]{2,1,0:T(8,128)S(1)}, f32[36,32,128]{2,1,0:T(8,128)}, u32[]{:S(2)}) copy-start(f32[36,32,128]{2,1,0:T(8,128)} %copy-done.3) | copy-start | bytes 1769476
  97.1 2.1 %collective-permute-start.13 = (f32[16,32,128]{2,1,0:T(8,128)S(1)}, f32[16,32,128]{2,1,0:T(8,128)S(1)}, u32[]{:S(2)}, u32[]{:S(2)}) collective-permute-start(f32[16,32,128]{2,1,0:T(8,128)S(1)} %slice.242), channel_id=1, source_target_pairs={{96,289},{97,290},{98,291},{99,292},{100,293},{101,294},{102,295},... | collective-permute-start | bytes 786440 | tf_op jit(solution)/shard_map/ppermute | solution.py:305
  97.8 1.5 %collective-permute-start.15 = (f32[16,32,128]{2,1,0:T(8,128)S(1)}, f32[16,32,128]{2,1,0:T(8,128)S(1)}, u32[]{:S(2)}, u32[]{:S(2)}) collective-permute-start(f32[16,32,128]{2,1,0:T(8,128)S(1)} %slice.242), channel_id=1, source_target_pairs={{97,288},{98,289},{99,290},{100,291},{101,292},{102,293},{103,294}... | collective-permute-start | bytes 786440 | tf_op jit(solution)/shard_map/ppermute | solution.py:305
  98.5 0.8 collective-permute-start.14
  104.4 1.0 copy-start.8
  104.5 2.5 %collective-permute-start.16 = (f32[36,32,128]{2,1,0:T(8,128)S(1)}, f32[36,32,128]{2,1,0:T(8,128)S(1)}, u32[]{:S(2)}, u32[]{:S(2)}) collective-permute-start(f32[36,32,128]{2,1,0:T(8,128)S(1)} %shard_map.63), channel_id=1, source_target_pairs={{288,480},{289,481},{290,482},{291,483},{292,484},{293,485},{294,4... | collective-permute-start | bytes 1769480 | tf_op jit(solution)/shard_map/ppermute | solution.py:305
  105.4 4.7 %collective-permute-start.17 = (f32[8,32,128]{2,1,0:T(8,128)S(1)}, f32[8,32,128]{2,1,0:T(8,128)S(1)}, u32[]{:S(2)}, u32[]{:S(2)}) collective-permute-start(f32[8,32,128]{2,1,0:T(8,128)S(1)} %shard_map.67), channel_id=1, source_target_pairs={{0,32},{1,33},{2,34},{3,35},{4,36},{5,37},{6,38},{7,39},{8,40},{9,... | collective-permute-start | bytes 393224 | tf_op jit(solution)/shard_map/ppermute | solution.py:305
  105.5 5.7 %collective-permute-start.20 = (f32[3,8,32,128]{3,2,1,0:T(8,128)S(1)}, f32[3,8,32,128]{3,2,1,0:T(8,128)S(1)}, u32[]{:S(2)}, u32[]{:S(2)}) collective-permute-start(f32[3,8,32,128]{3,2,1,0:T(8,128)S(1)} %maximum_select_fusion.9), channel_id=1, source_target_pairs={{288,384},{289,385},{290,386},{291,387},{292,388},{293,389},{294,3... | collective-permute-start | bytes 1179656 | tf_op jit(solution)/shard_map/ppermute | solution.py:405
  106.2 5.1 %collective-permute-start.21 = (f32[3,8,32,128]{3,2,1,0:T(8,128)S(1)}, f32[3,8,32,128]{3,2,1,0:T(8,128)S(1)}, u32[]{:S(2)}, u32[]{:S(2)}) collective-permute-start(f32[3,8,32,128]{3,2,1,0:T(8,128)S(1)} %get-tuple-element.64), channel_id=1, source_target_pairs={{288,256},{289,257},{290,258},{291,259},{292,260},{293,261},{294,2... | collective-permute-start | bytes 1179656 | tf_op jit(solution)/shard_map/ppermute | solution.py:405
  107.7 2.3 %copy-start.6 = (f32[32,8,128]{2,1,0:T(8,128)S(1)}, f32[32,8,128]{2,1,0:T(8,128)}, u32[]{:S(2)}) copy-start(f32[32,8,128]{2,1,0:T(8,128)} %copy-done.5) | copy-start | bytes 393220
  107.9 3.3 %collective-permute-start.18 = (f32[3,8,32,128]{3,2,1,0:T(8,128)S(1)}, f32[3,8,32,128]{3,2,1,0:T(8,128)S(1)}, u32[]{:S(2)}, u32[]{:S(2)}) collective-permute-start(f32[3,8,32,128]{3,2,1,0:T(8,128)S(1)} %maximum_select_fusion.4), channel_id=1, source_target_pairs={{480,416},{481,417},{482,418},{483,419},{484,420},{485,421},{486,4... | collective-permute-start | bytes 1179656 | tf_op jit(solution)/shard_map/ppermute | solution.py:405
  108.7 37.5 %collective-permute-start.19 = (f32[3,8,32,128]{3,2,1,0:T(8,128)S(1)}, f32[3,8,32,128]{3,2,1,0:T(8,128)S(1)}, u32[]{:S(2)}, u32[]{:S(2)}) collective-permute-start(f32[3,8,32,128]{3,2,1,0:T(8,128)S(1)} %maximum_select_fusion.7), channel_id=1, source_target_pairs={{480,448},{481,449},{482,450},{483,451},{484,452},{485,453},{486,4... | collective-permute-start | bytes 1179656 | tf_op jit(solution)/shard_map/ppermute | solution.py:405
  (4 other events, 3.1 us)

commit v4 on v3

--- a/solution.py
+++ b/solution.py
@@ -24,23 +24,24 @@
 TILE = 8
 EXT = 3 * TILE
 
-BLOCKS = ((1, range(2, 3)), (3, range(3, 8)), (9, range(8, 13)), (15, range(13, 16)))
+BLOCKS = ((3, range(2, 8)), (9, range(8, 13)), (15, range(13, 16)))
 PHASE_END = {k: 7 if k < 8 else 15 for k in range(1, 16)}
 GATHERS = (
-    (6, ((0, 1), (8, 9))),
+    (6, ((0, 3), (8, 9))),
+    (5, ((1, 3), (10, 9))),
+    (3, ((4, 3), (11, 9), (12, 15))),
     (7, ((2, 3), (7, 9), (14, 15))),
-    (3, ((4, 3), (11, 9), (12, 15))),
     (1, ((5, 3), (13, 15))),
     (0, ((6, 3),)),
 )
-GATHER_WITH_STATE = (5, ((1, 3), (10, 9)))
 ROUNDS = (
-    ((15, 13, 13), (9, 10, 10), (3, 4, 4), (1, 2, 2)),
-    ((15, 14, 14), (9, 11, 11), (3, 5, 5)),
-    ((9, 12, 12), (3, 6, 6)),
-    ((9, 8, 8), (3, 7, 7)),
+    ((9, 12, 12), (3, 7, 7)),
+    ((9, 11, 11), (3, 6, 6)),
+    ((9, 8, 8), (3, 2, 2)),
+    ((15, 13, 13), (9, 10, 10), (3, 4, 4), (0, 1, 1)),
+    ((15, 14, 14), (3, 5, 5)),
 )
-KEPT = ((1, 1), (3, 3), (9, 9), (15, 15))
+KEPT = ((3, 3), (9, 9), (15, 15))
 AROUND = 7
 VMEM = functools.partial(pl.BlockSpec, memory_space=pltpu.VMEM)
 SMEM = functools.partial(pl.BlockSpec, memory_space=pltpu.SMEM)
@@ -115,7 +116,7 @@
     return [x + y for x, y in zip(a, b)]
 
 
-def make_tables(flag, soils, tabs):
+def make_tables(place, last, soils, tabs):
     for part, load in enumerate(soils):
         def one(i, _):
             kinds = load(i)
@@ -134,9 +135,8 @@
                     pick(STRENGTH),
                 ]
                 if part != 1:
-                    inside = flag[0 if part == 0 else 1]
-                    rows[0], rows[1], rows[3] = rows[0] * inside, rows[1] * inside, rows[3] * inside
-                    rows[2] = rows[2] - 1000.0 * (1.0 - inside)
+                    inside = (place[1] > 0) if part == 0 else (place[1] < last)
+                    rows = [jnp.where(inside, v, other) for v, other in zip(rows, (0.0, 0.0, -1000.0, 0.0, 0.0))]
                 for o, v in zip(out, rows):
                     o.append(v)
             for k in range(5):
@@ -186,13 +186,14 @@
     lax.fori_loop(0, TILE, one, 0)
 
 
-def relax_kernel(flag, centre, left, right, soil, out, ps, tabs, a, b):
+def relax_kernel(last, place, centre, left, right, soil, out, ps, tabs, a, b):
     ends = edges()
     make_tables(
-        flag,
+        place,
+        last,
         (
             lambda i: load_rows(left, 2, i),
-            lambda i: [k.astype(F32) for k in load_rows(soil, i)],
+            lambda i: load_rows(soil, 2, i),
             lambda i: load_rows(right, 2, i),
         ),
         tabs,
@@ -207,20 +208,26 @@
     fine_steps((a, b), tabs, strain, finish, ends)
 
 
-def defect_kernel(flag, centre, left, right, tabs, start_p, first_ps, out, ps, a, b, coarse):
+def defect_kernel(place, centre, left, right, tabs, start_p, first_ps, out, up, down, ps, a, b, coarse):
     ends = edges()
     gather_ext(a, left, centre, right, ((0, 0, 0), (1, 1, 1)))
-    later = 1.0 - flag[2]
+    first = jnp.where(place[0] == 0, 1.0, 0.0)
+    later = 1.0 - first
 
     def first_extra(i, here_t, here_w, inc_t, inc_p, inc_w):
         store4(coarse, [later * (v + RATIO * d) for v, d in zip(here_t, inc_t)], 0, i)
         store4(coarse, [later * (v + RATIO * d) for v, d in zip(here_w, inc_w)], 1, i)
         rows = zip(inc_p, load_rows(start_p, 1, i), load4(first_ps, i))
-        return [(1.0 - RATIO * later) * d + flag[2] * (p + q) for d, p, q in rows]
+        return [(1.0 - RATIO * later) * d + first * (p + q) for d, p, q in rows]
 
     def finish(i, theta, w):
-        store_rows(out, [v - g for v, g in zip(theta, load4(coarse, 0, i))], 0, i)
-        store_rows(out, [v - g for v, g in zip(w, load4(coarse, 1, i))], 1, i)
+        for f, rows in enumerate((theta, w)):
+            rows = [v - g for v, g in zip(rows, load4(coarse, f, i))]
+            store_rows(out, rows, f, i)
+            if i >= TILE - AROUND:
+                store_rows(up, rows, f, i - (TILE - AROUND))
+            if i < AROUND:
+                store_rows(down, rows, f, i)
 
     strain = (lambda i: load_rows(ps, i), lambda rows, i: store_rows(ps, rows, i))
     fine_steps((a, b), tabs, strain, finish, ends, first_extra)
@@ -237,18 +244,60 @@
         out[2 * wide:] = strain[...]
 
 
-def copy_kernel(*refs):
-    n = len(refs) // 2
-    for source, target in zip(refs[:n], refs[n + 1:]):
-        target[...] = source[...]
-
-
-def strain_kernel(start_p, ps, out):
-    for i in range(TILE):
-        store_rows(out, plus(load_rows(start_p, i), load4(ps, i)), i)
-
-
-def coarse_kernel(halo, sent, state, tabs, defect, out):
+def join_kernel(before, state, after, out):
+    for f in range(2):
+        for part, (ref, at) in enumerate(((before, f * TILE), (state, f * TILE), (after, f * TILE))):
+            out[f * EXT + part * TILE:f * EXT + (part + 1) * TILE] = ref[at:at + TILE]
+    out[2 * EXT:] = state[2 * TILE:]
+
+
+def copy_tile(out, state, h):
+    layers = TILE + 2 * h
+    out[0] = state[h:h + TILE]
+    out[1] = state[2 * layers:]
+    out[2] = state[layers + h:layers + h + TILE]
+
+
+def send_kernel(plan, place, *refs):
+    *states, out = refs
+    for (sender, h), state in zip(plan, states):
+        pl.when(place[0] == sender)(functools.partial(copy_tile, out, state, h))
+
+
+def corrected_kernel(kept, sent, place, relaxed, *refs):
+    *results, out = refs
+
+    @pl.when(place[0] == 0)
+    def _():
+        out[...] = relaxed[...]
+
+    for (device, h), state in zip(kept, results):
+        pl.when(place[0] == device)(functools.partial(copy_tile, out, state, h))
+    for devices, got in zip(sent, results[len(kept):]):
+        for device in devices:
+            @pl.when(place[0] == device)
+            def _(got=got):
+                out[...] = got[...]
+
+
+def late_kernel(start_p, wait, out):
+    out[...] = start_p[...]
+
+
+def relaxed_kernel(place, start_p, first_p, kept, ps, *outs):
+    is_first = place[0] == 0
+    rows = [
+        [jnp.where(is_first, a, b) for a, b in zip(load_rows(first_p, 1, i), load_rows(start_p, i))] for i in range(TILE)
+    ]
+    for out in outs:
+        out[0], out[2] = kept[0], kept[1]
+        for i in range(TILE):
+            store_rows(out, plus(rows[i], load4(ps, i)), 1, i)
+
+
+def coarse_kernel(halo, sent, waits, state, tabs, defect, *rest):
+    out, *tile_out = rest[waits:]
+    tile_out = tile_out[0] if tile_out else None
     ends = edges()
     new = halo - 1
     wide, narrow, other = TILE + 2 * halo, TILE + 2 * new, TILE + 2 * sent
@@ -263,7 +312,10 @@
             store_rows(out, [(p + RATIO * v) + e for p, v, e in rows], 2 * narrow + j)
         for f, here, inc in ((0, here_t, inc_t), (1, here_w, inc_w)):
             rows = zip(here, inc, load_rows(defect, f * other + sent - new + o))
-            store_rows(out, [(v + RATIO * x) + e for v, x, e in rows], f * narrow + o)
+            rows = [(v + RATIO * x) + e for v, x, e in rows]
+            store_rows(out, rows, f * narrow + o)
+            if tile_out is not None:
+                store_rows(tile_out, rows, f * narrow + o)
         return 0
 
     loop(0, new, one)
@@ -271,20 +323,20 @@
     loop(new + TILE, narrow, one)
 
 
-def call(kernel, outs, scratch, specs):
+def call(kernel, outs, scratch, operands, place=None, waits=()):
+    specs = [VMEM() for _ in operands] + [pl.BlockSpec(memory_space=pltpu.HBM if x.size > 2 * TILE * 32 * 128 else pl.ANY) for x in waits]
+    operands = [*operands, *waits]
+    if place is not None:
+        operands, specs = [place, *operands], [SMEM(), *specs]
     return pl.pallas_call(
         kernel,
         out_shape=[jax.ShapeDtypeStruct(s, F32) for s in outs],
         in_specs=specs,
         out_specs=[VMEM() for _ in outs],
-        scratch_shapes=[pltpu.VMEM(s, F32) for s in scratch],
+        scratch_shapes=[pltpu.VMEM(s, F32) if isinstance(s, tuple) else s for s in scratch],
         compiler_params=pltpu.CompilerParams(vmem_limit_bytes=12 * 2**20),
-    )
-
-
-def after(arrays, wait):
-    specs = [VMEM() for _ in arrays] + [pl.BlockSpec(memory_space=pl.ANY)]
-    return call(copy_kernel, [a.shape for a in arrays], [], specs)(*arrays, wait)
+        cost_estimate=pl.CostEstimate(flops=1, bytes_accessed=1, transcendentals=0),
+    )(*operands)
 
 
 LAYER = (32, 128)
@@ -292,119 +344,108 @@
 
 
 def on_device(nt, ns, initial_state, guess, soil):
-    t, s = lax.axis_index("tm"), lax.axis_index("space")
-    flag = jnp.stack([s > 0, s < ns - 1, t == 0]).astype(F32)
+    place = jnp.stack([lax.axis_index("tm"), lax.axis_index("space")]).astype(jnp.int32)
     both = ("tm", "space")
-
-    def shifted(x, dt, ds, only=None):
-        pairs = []
-        for a in range(nt) if only is None else only:
-            for b in range(ns):
-                if 0 <= b + ds < ns:
-                    pairs.append((a * ns + b, (a + dt) % nt * ns + b + ds))
+    tile, whole = (2, TILE, *LAYER), (3, TILE, *LAYER)
+
+    def sent(x, moves, ds=0):
+        pairs = [(a * ns + b, c * ns + b + ds) for a, c in moves for b in range(ns) if 0 <= b + ds < ns]
         return lax.ppermute(x, both, pairs)
 
-    mine = jnp.where(t == nt - 1, initial_state, guess[0])
-    heat_stress = jnp.stack([mine[0], mine[2]])
+    stay = [(a, a) for a in range(nt)]
+    ahead = [(a, (a + 1) % nt) for a in range(nt)]
+
+    mine = jnp.where(lax.axis_index("tm") == nt - 1, initial_state, guess[0])
+    mine_p, heat_stress = mine[1], jnp.stack([mine[0], mine[2]])
     packed = jnp.concatenate([heat_stress, soil.astype(F32)[None]])
-    from_left = shifted(packed, 1, 1)
-    from_right = shifted(packed, 1, -1)
-    centre = shifted(heat_stress, 1, 0)
+    from_left = sent(packed, ahead, 1)
+    from_right = sent(packed, ahead, -1)
+    centre = sent(heat_stress, ahead)
     kept, grown, tabs = call(
-        relax_kernel,
-        [(2, TILE, *LAYER), (TILE * 4, *REGS), (5, EXT * 4, *REGS)],
+        functools.partial(relax_kernel, ns - 1),
+        [tile, (TILE * 4, *REGS), (5, EXT * 4, *REGS)],
         [(2, EXT * 4, *REGS), (2, EXT * 4, *REGS)],
-        [SMEM(), *[VMEM() for _ in range(4)]],
-    )(flag, centre, from_left, from_right, soil)
-
-    from_left = shifted(kept, 0, 1)
-    from_right = shifted(kept, 0, -1)
-    defect, strain = call(
+        [centre, from_left, from_right, packed],
+        place,
+    )
+
+    from_left = sent(kept, stay, 1)
+    from_right = sent(kept, stay, -1)
+    around = (2, AROUND, *LAYER)
+    defect, up, down, strain = call(
         defect_kernel,
-        [(2, TILE, *LAYER), (TILE, *LAYER)],
+        [tile, around, around, (TILE, *LAYER)],
         [(2, EXT * 4, *REGS), (2, EXT * 4, *REGS), (2, TILE * 4, *REGS)],
-        [SMEM(), *[VMEM() for _ in range(6)]],
-    )(flag, kept, from_left, from_right, tabs, initial_state, grown)
-
-    around = AROUND
-    left = shifted(defect[:, TILE - around:], 0, 1)
-    right = shifted(defect[:, :around], 0, -1)
-    halos = [h for h, _ in GATHERS] + [GATHER_WITH_STATE[0]]
+        [kept, from_left, from_right, tabs, initial_state, grown],
+        place,
+    )
+    left, right = sent(up, stay, 1), sent(down, stay, -1)
+    halos = [h for h, _ in GATHERS]
     packs = call(
         functools.partial(pack_kernel, halos),
         [(2 * (TILE + 2 * h) + TILE, *LAYER) for h in halos],
         [],
-        [VMEM() for _ in range(4)],
-    )(left, defect, right, strain)
-    with_halo = dict(zip(halos, packs)).get
-
-    def tile_of(state, h):
-        layers = TILE + 2 * h
-        return jnp.stack([state[h:h + TILE], state[2 * layers:], state[layers + h:layers + h + TILE]])
+        [left, defect, right, strain],
+    )
+    with_halo = dict(zip(halos, packs))
 
     terms = {}
-
-    def gather(payload, h, sends):
-        got = lax.ppermute(payload, both, [(a * ns + b, c * ns + b) for a, c in sends for b in range(ns)])
-        for a, _ in sends:
+    for h, moves in GATHERS:
+        got = sent(with_halo[h], moves)
+        for a, _ in moves:
             terms[a + 1] = (h, got)
-        return got
-
-    def step(k, state):
-        halo = PHASE_END[k] - k + 1
-        sent, term = terms.get(k) or (halo - 1, with_halo(halo - 1))
-        (out,) = call(
-            functools.partial(coarse_kernel, halo, sent),
-            [(2 * (TILE + 2 * halo - 2) + TILE, *LAYER)],
-            [],
-            [VMEM() for _ in range(3)],
-        )(state, tabs, term)
-        return out
-
-    state = [gather(with_halo(h), h, sends) for h, sends in GATHERS][0]
-    del terms[1]
-    results = {1: tile_of(state, GATHERS[0][0])}
-    holder = None
+    results = {1: terms.pop(1)}
+    state, holder, late = results[1][1], None, 3
     for worker, steps in BLOCKS:
         first = steps[0]
         halo = PHASE_END[first] - first + 1
         if holder is None:
             pass
-        elif holder == BLOCKS[0][0]:
-            h, sends = GATHER_WITH_STATE
-            state = gather(jnp.where(t == holder, state, with_halo(h)), h, sends)
-            del terms[holder + 1]
         elif PHASE_END[first] == PHASE_END[first - 1]:
-            state = shifted(state, worker - holder, 0, [holder])
+            state = sent(state, [(holder, worker)])
         else:
-            hop = worker - holder
-            tile = state[:2 * TILE]
-            before = shifted(tile, hop, 1, [holder])
-            following = shifted(tile, hop, -1, [holder])
-            state = shifted(state, hop, 0, [holder])
-            parts = []
-            for f in range(2):
-                own = slice(f * TILE, (f + 1) * TILE)
-                parts += [before[own][TILE - halo:], state[own], following[own][:halo]]
-            state = jnp.concatenate([*parts, state[2 * TILE:]])
+            move = [(holder, worker)]
+            parts = sent(edge, move, 1), sent(state, move), sent(edge, move, -1)
+            (state,) = call(join_kernel, [(2 * EXT + TILE, *LAYER)], [], parts)
+        waits = [held] if late in results and first == PHASE_END[late] + 1 else []
         for k in steps:
-            state = step(k, state)
-            results[k] = tile_of(state, PHASE_END[k] - k)
+            halo = PHASE_END[k] - k + 1
+            given, term = terms.get(k) or (halo - 1, with_halo[halo - 1])
+            shapes = [(2 * (TILE + 2 * halo - 2) + TILE, *LAYER)]
+            if halo == 1 and k < nt - 1:
+                shapes.append((2 * TILE, *LAYER))
+            state, *edge = call(
+                functools.partial(coarse_kernel, halo, given, len(waits)), shapes, [], [state, tabs, term], waits=waits
+            )
+            edge = edge[0] if edge else None
+            results[k] = (halo - 1, state)
+            waits = []
+            if k == late:
+                (late_p,) = call(late_kernel, [(TILE, *LAYER)], [], [mine_p], waits=[state])
+                relaxed, held = call(
+                    relaxed_kernel, [whole, whole], [], [sent(late_p, ahead[:-1]), initial_state, kept, grown], place
+                )
         holder = worker
 
-    (start_p,) = after([mine[1]], results[8])
-    (relaxed_p,) = call(strain_kernel, [(TILE, *LAYER)], [], [VMEM(), VMEM()])(shifted(start_p, 1, 0), grown)
-    relaxed = jnp.stack([kept[0], relaxed_p, kept[1]])
-    corrected = jnp.where(t == 0, relaxed, 0.0)
+    results[1] = (0, with_halo[0])
+    received = []
     for sends in ROUNDS:
-        payload = results[sends[0][1]]
-        pairs = []
-        for source, k, target in sends:
-            payload = jnp.where(t == source, results[k], payload)
-            pairs += [(source * ns + b, target * ns + b) for b in range(ns)]
-        corrected = corrected + lax.ppermute(payload, both, pairs)
-    for device, k in KEPT:
-        corrected = jnp.where(t == device, results[k], corrected)
+        plan = [(source, results[k][0]) for source, k, _ in sends]
+        (payload,) = call(
+            functools.partial(send_kernel, plan), [whole], [], [results[k][1] for _, k, _ in sends], place
+        )
+        received.append(sent(payload, [(source, target) for source, _, target in sends]))
+    (corrected,) = call(
+        functools.partial(
+            corrected_kernel,
+            [(device, results[k][0]) for device, k in KEPT],
+            [[target for _, _, target in sends] for sends in ROUNDS],
+        ),
+        [whole],
+        [],
+        [held, *[results[k][1] for _, k in KEPT], *received],
+        place,
+    )
     return corrected[None], relaxed[None]
 
 

time: 148 us -> 134 us (0.905)
  the two profiles are of different devices: /device:TPU:47 before, /device:TPU:55 now
where the time goes in v4:
time: 134 us; the launch traced here: 133 us
  waiting for transfers between devices  69.6 us (52%)
  starting transfers between devices  40.2 us (30%)
  Pallas kernels  20 us (15%)
  other arithmetic  2.1 us (2%)
    ppermute x23, waiting for transfers between devices, sent(): return lax.ppermute(x, both, pairs)  69.6 us
    ppermute x23, starting transfers between devices, sent(): return lax.ppermute(x, both, pairs)  40.2 us
    pallas_call x26, Pallas kernels, call(): pl.pallas_call(kernel, out_shape=[jax.ShapeDtypeStruct(s, F32) for s in o...  20 us
  transfers between devices with their start and end apart: 23, of which 9 were waited for; matrix products, arithmetic and copies ran while one was open for 0% of the time, Pallas kernels for 5%

profile of v4, /device:TPU:55, one launch (start us, length us, event | category | flops | bytes accessed | tf_op | source)
XLA Modules:
  0.0 133.0 jit_solution(13911064966060044422)
XLA Ops:
  0.6 0.9 convert_bitcast_fusion
  1.6 1.1 bitcast_select_fusion
  2.7 11.7 %collective-permute-start.2 = (f32[3,8,32,128]{3,2,1,0:T(8,128)S(1)}, f32[3,8,32,128]{3,2,1,0:T(8,128)S(1)}, u32[]{:S(2)}, u32[]{:S(2)}) collective-permute-start(f32[3,8,32,128]{3,2,1,0:T(8,128)S(1)} %pad_maximum_fusion.soil), channel_id=1, source_target_pairs={{1,32},{2,33},{3,34},{4,35},{5,36},{6,37},{7,38},{8,39},{9,40},{10... | collective-permute-start | bytes 1179656 | tf_op jit(solution)/shard_map/ppermute | solution.py:353
  14.5 1.9 %collective-permute-start.1 = (f32[3,8,32,128]{3,2,1,0:T(8,128)S(1)}, f32[3,8,32,128]{3,2,1,0:T(8,128)S(1)}, u32[]{:S(2)}, u32[]{:S(2)}) collective-permute-start(f32[3,8,32,128]{3,2,1,0:T(8,128)S(1)} %pad_maximum_fusion.soil), channel_id=1, source_target_pairs={{0,33},{1,34},{2,35},{3,36},{4,37},{5,38},{6,39},{7,40},{8,41},{9,... | collective-permute-start | bytes 1179656 | tf_op jit(solution)/shard_map/ppermute | solution.py:353
  16.6 9.7 %collective-permute-done.centre = f32[2,8,32,128]{3,2,1,0:T(8,128)S(1)} collective-permute-done((f32[2,8,32,128]{3,2,1,0:T(8,128)S(1)}, f32[2,8,32,128]{3,2,1,0:T(8,128)S(1)}, u32[]{:S(2)}, u32[]{:S(2)}) %collective-permute-start) | collective-permute-done | bytes 262176 | tf_op jit(solution)/shard_map/ppermute | solution.py:353
  26.3 3.5 %collective-permute-done.1.left = f32[3,8,32,128]{3,2,1,0:T(8,128)S(1)} collective-permute-done((f32[3,8,32,128]{3,2,1,0:T(8,128)S(1)}, f32[3,8,32,128]{3,2,1,0:T(8,128)S(1)}, u32[]{:S(2)}, u32[]{:S(2)}) %collective-permute-start.1) | collective-permute-done | bytes 393248 | tf_op jit(solution)/shard_map/ppermute | solution.py:353
  29.8 4.2 %shard_map.50 = (f32[2,8,32,128]{3,2,1,0:T(8,128)S(1)}, f32[32,8,128]{2,1,0:T(8,128)S(1)}, f32[5,96,8,128]{3,2,1,0:T(8,128)S(1)}) custom-call(s32[2]{0:T(128)S(1)} %pad_add_fusion.place, f32[2,8,32,128]{3,2,1,0:T(8,128)S(1)} %collective-permute-done.centre, f32[3,8,32,128]{3,2,1,0:T(8,128)S(1)} %collective-permute-done.1.left, ...), custom_call_target="tpu_custom_call" | custom-call | flops 1 | bytes 1 | tf_op jit(solution)/shard_map/pallas_call | solution.py:331
  34.0 1.9 %collective-permute-start.4 = (f32[2,8,32,128]{3,2,1,0:T(8,128)S(1)}, f32[2,8,32,128]{3,2,1,0:T(8,128)S(1)}, u32[]{:S(2)}, u32[]{:S(2)}) collective-permute-start(f32[2,8,32,128]{3,2,1,0:T(8,128)S(1)} %get-tuple-element.19.centre.kept), channel_id=1, source_target_pairs={{1,0},{2,1},{3,2},{4,3},{5,4},{6,5},{7,6},{8,7},{9,8},{10,9},{11,1... | collective-permute-start | bytes 786440 | tf_op jit(solution)/shard_map/ppermute | solution.py:353
  35.9 3.4 %collective-permute-start.3 = (f32[2,8,32,128]{3,2,1,0:T(8,128)S(1)}, f32[2,8,32,128]{3,2,1,0:T(8,128)S(1)}, u32[]{:S(2)}, u32[]{:S(2)}) collective-permute-start(f32[2,8,32,128]{3,2,1,0:T(8,128)S(1)} %get-tuple-element.19.centre.kept), channel_id=1, source_target_pairs={{0,1},{1,2},{2,3},{3,4},{4,5},{5,6},{6,7},{7,8},{8,9},{9,10},{10,1... | collective-permute-start | bytes 786440 | tf_op jit(solution)/shard_map/ppermute | solution.py:353
  39.3 4.1 %collective-permute-done.4.right = f32[2,8,32,128]{3,2,1,0:T(8,128)S(1)} collective-permute-done((f32[2,8,32,128]{3,2,1,0:T(8,128)S(1)}, f32[2,8,32,128]{3,2,1,0:T(8,128)S(1)}, u32[]{:S(2)}, u32[]{:S(2)}) %collective-permute-start.4) | collective-permute-done | bytes 262176 | tf_op jit(solution)/shard_map/ppermute | solution.py:353
  43.3 4.3 %collective-permute-done.3.left = f32[2,8,32,128]{3,2,1,0:T(8,128)S(1)} collective-permute-done((f32[2,8,32,128]{3,2,1,0:T(8,128)S(1)}, f32[2,8,32,128]{3,2,1,0:T(8,128)S(1)}, u32[]{:S(2)}, u32[]{:S(2)}) %collective-permute-start.3) | collective-permute-done | bytes 262176 | tf_op jit(solution)/shard_map/ppermute | solution.py:353
  47.6 3.8 %shard_map.51 = (f32[2,8,32,128]{3,2,1,0:T(8,128)S(1)}, f32[2,7,32,128]{3,2,1,0:T(8,128)S(1)}, f32[2,7,32,128]{3,2,1,0:T(8,128)S(1)}, f32[8,32,128]{2,1,0:T(8,128)S(1)}) custom-call(s32[2]{0:T(128)S(1)} %pad_add_fusion.place, f32[2,8,32,128]{3,2,1,0:T(8,128)S(1)} %get-tuple-element.19.centre.kept, f32[2,8,32,128]{3,2,1,0:T(8,128)S(1)} %collective-permute-done.3.left, ...), custom_call_target="tpu_custom_call" | custom-call | flops 1 | bytes 1 | tf_op jit(solution)/shard_map/pallas_call | solution.py:331
  51.4 1.9 %collective-permute-start.5 = (f32[2,7,32,128]{3,2,1,0:T(8,128)S(1)}, f32[2,7,32,128]{3,2,1,0:T(8,128)S(1)}, u32[]{:S(2)}, u32[]{:S(2)}) collective-permute-start(f32[2,7,32,128]{3,2,1,0:T(8,128)S(1)} %get-tuple-element.22), channel_id=1, source_target_pairs={{0,1},{1,2},{2,3},{3,4},{4,5},{5,6},{6,7},{7,8},{8,9},{9,10},{10,1... | collective-permute-start | bytes 688136 | tf_op jit(solution)/shard_map/ppermute | solution.py:353
  53.4 5.5 %collective-permute-start.6 = (f32[2,7,32,128]{3,2,1,0:T(8,128)S(1)}, f32[2,7,32,128]{3,2,1,0:T(8,128)S(1)}, u32[]{:S(2)}, u32[]{:S(2)}) collective-permute-start(f32[2,7,32,128]{3,2,1,0:T(8,128)S(1)} %get-tuple-element.24), channel_id=1, source_target_pairs={{1,0},{2,1},{3,2},{4,3},{5,4},{6,5},{7,6},{8,7},{9,8},{10,9},{11,1... | collective-permute-start | bytes 688136 | tf_op jit(solution)/shard_map/ppermute | solution.py:353
  58.8 2.7 %collective-permute-done.5.left = f32[2,7,32,128]{3,2,1,0:T(8,128)S(1)} collective-permute-done((f32[2,7,32,128]{3,2,1,0:T(8,128)S(1)}, f32[2,7,32,128]{3,2,1,0:T(8,128)S(1)}, u32[]{:S(2)}, u32[]{:S(2)}) %collective-permute-start.5) | collective-permute-done | bytes 229408 | tf_op jit(solution)/shard_map/ppermute | solution.py:353
  61.5 0.9 collective-permute-done.6.right
  62.6 0.7 collective-permute-start.8
  63.4 0.7 collective-permute-start.9
  64.1 0.7 collective-permute-start.7
  64.8 0.7 collective-permute-start.11
  65.5 1.3 collective-permute-start.12
  66.9 0.7 collective-permute-start.13
  69.5 5.9 %collective-permute-done.12.defect = f32[28,32,128]{2,1,0:T(8,128)S(1)} collective-permute-done((f32[28,32,128]{2,1,0:T(8,128)S(1)}, f32[28,32,128]{2,1,0:T(8,128)S(1)}, u32[]{:S(2)}, u32[]{:S(2)}) %collective-permute-start.12) | collective-permute-done | bytes 458784 | tf_op jit(solution)/shard_map/ppermute | solution.py:353
  76.0 0.7 collective-permute-start.15
  76.7 0.9 collective-permute-start.16
  78.2 1.9 %collective-permute-start.10 = (f32[8,32,128]{2,1,0:T(8,128)S(1)}, f32[8,32,128]{2,1,0:T(8,128)S(1)}, u32[]{:S(2)}, u32[]{:S(2)}) collective-permute-start(f32[8,32,128]{2,1,0:T(8,128)S(1)} %shard_map.55), channel_id=1, source_target_pairs={{0,32},{1,33},{2,34},{3,35},{4,36},{5,37},{6,38},{7,39},{8,40},{9,... | collective-permute-start | bytes 393224 | tf_op jit(solution)/shard_map/ppermute | solution.py:353
  80.2 4.8 %collective-permute-done.10.start_p = f32[8,32,128]{2,1,0:T(8,128)S(1)} collective-permute-done((f32[8,32,128]{2,1,0:T(8,128)S(1)}, f32[8,32,128]{2,1,0:T(8,128)S(1)}, u32[]{:S(2)}, u32[]{:S(2)}) %collective-permute-start.10) | collective-permute-done | bytes 131104 | tf_op jit(solution)/shard_map/ppermute | solution.py:353
  84.9 1.3 %shard_map.56 = (f32[3,8,32,128]{3,2,1,0:T(8,128)}, f32[3,8,32,128]{3,2,1,0:T(8,128)S(1)}) custom-call(s32[2]{0:T(128)S(1)} %pad_add_fusion.place, f32[8,32,128]{2,1,0:T(8,128)S(1)} %collective-permute-done.10.start_p, f32[3,8,32,128]{3,2,1,0:T(8,128)S(1)} %copy-done, f32[2,8,32,128]{3,2,1,0:T(8,128)S(1)} %get-tuple-element.19.centre.kept, ...), custom_call_target="tpu_custom_call" | custom-call | flops 1 | bytes 1 | tf_op jit(solution)/shard_map/pallas_call | solution.py:331
  89.1 0.7 collective-permute-start.17
  96.2 1.3 collective-permute-start.21
  97.8 33.8 %collective-permute-done.21.refs_6_ = f32[3,8,32,128]{3,2,1,0:T(8,128)S(1)} collective-permute-done((f32[3,8,32,128]{3,2,1,0:T(8,128)S(1)}, f32[3,8,32,128]{3,2,1,0:T(8,128)S(1)}, u32[]{:S(2)}, u32[]{:S(2)}) %collective-permute-start.21) | collective-permute-done | bytes 393248 | tf_op jit(solution)/shard_map/ppermute | solution.py:353
  131.6 1.4 %shard_map.75 = f32[3,8,32,128]{3,2,1,0:T(8,128)} custom-call(s32[2]{0:T(128)S(1)} %pad_add_fusion.place, f32[3,8,32,128]{3,2,1,0:T(8,128)S(1)} %get-tuple-element.29.rest_0_.relaxed, f32[40,32,128]{2,1,0:T(8,128)S(1)} %shard_map.54.wait.state.refs_0_, f32[48,32,128]{2,1,0:T(8,128)S(1)} %shard_map.63.state.refs_1_, f32[24,32,128]{2,1,0:T(8,128)S(1)} %shard_map.69.refs_2_, ...), custom_call_target="tpu_custom_call" | custom-call | flops 1 | bytes 1 | tf_op jit(solution)/shard_map/pallas_call | solution.py:331
  (48 shorter events, 13.0 us)
Async XLA Ops:
  2.6 45.0 %copy-start = (f32[3,8,32,128]{3,2,1,0:T(8,128)S(1)}, f32[3,8,32,128]{3,2,1,0:T(8,128)}, u32[]{:S(2)}) copy-start(f32[3,8,32,128]{3,2,1,0:T(8,128)} %first_p.1) | copy-start | bytes 1179652
  2.7 23.6 %collective-permute-start.2 = (f32[3,8,32,128]{3,2,1,0:T(8,128)S(1)}, f32[3,8,32,128]{3,2,1,0:T(8,128)S(1)}, u32[]{:S(2)}, u32[]{:S(2)}) collective-permute-start(f32[3,8,32,128]{3,2,1,0:T(8,128)S(1)} %pad_maximum_fusion.soil), channel_id=1, source_target_pairs={{1,32},{2,33},{3,34},{4,35},{5,36},{6,37},{7,38},{8,39},{9,40},{10... | collective-permute-start | bytes 1179656 | tf_op jit(solution)/shard_map/ppermute | solution.py:353
  14.5 15.3 %collective-permute-start.1 = (f32[3,8,32,128]{3,2,1,0:T(8,128)S(1)}, f32[3,8,32,128]{3,2,1,0:T(8,128)S(1)}, u32[]{:S(2)}, u32[]{:S(2)}) collective-permute-start(f32[3,8,32,128]{3,2,1,0:T(8,128)S(1)} %pad_maximum_fusion.soil), channel_id=1, source_target_pairs={{0,33},{1,34},{2,35},{3,36},{4,37},{5,38},{6,39},{7,40},{8,41},{9,... | collective-permute-start | bytes 1179656 | tf_op jit(solution)/shard_map/ppermute | solution.py:353
  16.4 9.9 %collective-permute-start = (f32[2,8,32,128]{3,2,1,0:T(8,128)S(1)}, f32[2,8,32,128]{3,2,1,0:T(8,128)S(1)}, u32[]{:S(2)}, u32[]{:S(2)}) collective-permute-start(f32[2,8,32,128]{3,2,1,0:T(8,128)S(1)} %pad_maximum_fusion.1), channel_id=1, source_target_pairs={{0,32},{1,33},{2,34},{3,35},{4,36},{5,37},{6,38},{7,39},{8,40},{9,... | collective-permute-start | bytes 786440 | tf_op jit(solution)/shard_map/ppermute | solution.py:353
  34.0 9.4 %collective-permute-start.4 = (f32[2,8,32,128]{3,2,1,0:T(8,128)S(1)}, f32[2,8,32,128]{3,2,1,0:T(8,128)S(1)}, u32[]{:S(2)}, u32[]{:S(2)}) collective-permute-start(f32[2,8,32,128]{3,2,1,0:T(8,128)S(1)} %get-tuple-element.19.centre.kept), channel_id=1, source_target_pairs={{1,0},{2,1},{3,2},{4,3},{5,4},{6,5},{7,6},{8,7},{9,8},{10,9},{11,1... | collective-permute-start | bytes 786440 | tf_op jit(solution)/shard_map/ppermute | solution.py:353
  35.9 11.7 %collective-permute-start.3 = (f32[2,8,32,128]{3,2,1,0:T(8,128)S(1)}, f32[2,8,32,128]{3,2,1,0:T(8,128)S(1)}, u32[]{:S(2)}, u32[]{:S(2)}) collective-permute-start(f32[2,8,32,128]{3,2,1,0:T(8,128)S(1)} %get-tuple-element.19.centre.kept), channel_id=1, source_target_pairs={{0,1},{1,2},{2,3},{3,4},{4,5},{5,6},{6,7},{7,8},{8,9},{9,10},{10,1... | collective-permute-start | bytes 786440 | tf_op jit(solution)/shard_map/ppermute | solution.py:353
  51.4 10.1 %collective-permute-start.5 = (f32[2,7,32,128]{3,2,1,0:T(8,128)S(1)}, f32[2,7,32,128]{3,2,1,0:T(8,128)S(1)}, u32[]{:S(2)}, u32[]{:S(2)}) collective-permute-start(f32[2,7,32,128]{3,2,1,0:T(8,128)S(1)} %get-tuple-element.22), channel_id=1, source_target_pairs={{0,1},{1,2},{2,3},{3,4},{4,5},{5,6},{6,7},{7,8},{8,9},{9,10},{10,1... | collective-permute-start | bytes 688136 | tf_op jit(solution)/shard_map/ppermute | solution.py:353
  53.4 9.0 %collective-permute-start.6 = (f32[2,7,32,128]{3,2,1,0:T(8,128)S(1)}, f32[2,7,32,128]{3,2,1,0:T(8,128)S(1)}, u32[]{:S(2)}, u32[]{:S(2)}) collective-permute-start(f32[2,7,32,128]{3,2,1,0:T(8,128)S(1)} %get-tuple-element.24), channel_id=1, source_target_pairs={{1,0},{2,1},{3,2},{4,3},{5,4},{6,5},{7,6},{8,7},{9,8},{10,9},{11,1... | collective-permute-start | bytes 688136 | tf_op jit(solution)/shard_map/ppermute | solution.py:353
  62.6 4.2 %collective-permute-start.8 = (f32[44,32,128]{2,1,0:T(8,128)S(1)}, f32[44,32,128]{2,1,0:T(8,128)S(1)}, u32[]{:S(2)}, u32[]{:S(2)}) collective-permute-start(f32[44,32,128]{2,1,0:T(8,128)S(1)} %get-tuple-element.27.defect), channel_id=1, source_target_pairs={{32,96},{33,97},{34,98},{35,99},{36,100},{37,101},{38,102},{39,103... | collective-permute-start | bytes 2162696 | tf_op jit(solution)/shard_map/ppermute | solution.py:353
  63.4 4.8 %collective-permute-start.9 = (f32[52,32,128]{2,1,0:T(8,128)S(1)}, f32[52,32,128]{2,1,0:T(8,128)S(1)}, u32[]{:S(2)}, u32[]{:S(2)}) collective-permute-start(f32[52,32,128]{2,1,0:T(8,128)S(1)} %get-tuple-element.28), channel_id=1, source_target_pairs={{64,96},{65,97},{66,98},{67,99},{68,100},{69,101},{70,102},{71,103... | collective-permute-start | bytes 2555912 | tf_op jit(solution)/shard_map/ppermute | solution.py:353
  64.1 3.5 %collective-permute-start.7 = (f32[48,32,128]{2,1,0:T(8,128)S(1)}, f32[48,32,128]{2,1,0:T(8,128)S(1)}, u32[]{:S(2)}, u32[]{:S(2)}) collective-permute-start(f32[48,32,128]{2,1,0:T(8,128)S(1)} %get-tuple-element.26), channel_id=1, source_target_pairs={{0,96},{1,97},{2,98},{3,99},{4,100},{5,101},{6,102},{7,103},{8,104... | collective-permute-start | bytes 2359304 | tf_op jit(solution)/shard_map/ppermute | solution.py:353
  64.8 4.3 %collective-permute-start.11 = (f32[36,32,128]{2,1,0:T(8,128)S(1)}, f32[36,32,128]{2,1,0:T(8,128)S(1)}, u32[]{:S(2)}, u32[]{:S(2)}) collective-permute-start(f32[36,32,128]{2,1,0:T(8,128)S(1)} %get-tuple-element.30.defect), channel_id=1, source_target_pairs={{128,96},{129,97},{130,98},{131,99},{132,100},{133,101},{134,102},... | collective-permute-start | bytes 1769480 | tf_op jit(solution)/shard_map/ppermute | solution.py:353
  65.5 9.9 %collective-permute-start.12 = (f32[28,32,128]{2,1,0:T(8,128)S(1)}, f32[28,32,128]{2,1,0:T(8,128)S(1)}, u32[]{:S(2)}, u32[]{:S(2)}) collective-permute-start(f32[28,32,128]{2,1,0:T(8,128)S(1)} %get-tuple-element.31), channel_id=1, source_target_pairs={{160,96},{161,97},{162,98},{163,99},{164,100},{165,101},{166,102},... | collective-permute-start | bytes 1376264 | tf_op jit(solution)/shard_map/ppermute | solution.py:353
  66.9 8.8 %collective-permute-start.13 = (f32[24,32,128]{2,1,0:T(8,128)S(1)}, f32[24,32,128]{2,1,0:T(8,128)S(1)}, u32[]{:S(2)}, u32[]{:S(2)}) collective-permute-start(f32[24,32,128]{2,1,0:T(8,128)S(1)} %get-tuple-element.32.refs_3_), channel_id=1, source_target_pairs={{192,96},{193,97},{194,98},{195,99},{196,100},{197,101},{198,102},... | collective-permute-start | bytes 1179656 | tf_op jit(solution)/shard_map/ppermute | solution.py:353
  76.0 10.3 %collective-permute-start.15 = (f32[24,32,128]{2,1,0:T(8,128)S(1)}, f32[24,32,128]{2,1,0:T(8,128)S(1)}, u32[]{:S(2)}, u32[]{:S(2)}) collective-permute-start(f32[24,32,128]{2,1,0:T(8,128)S(1)} %get-tuple-element.34.refs_1_), channel_id=1, source_target_pairs={{96,288},{97,289},{98,290},{99,291},{100,292},{101,293},{102,294},... | collective-permute-start | bytes 1179656 | tf_op jit(solution)/shard_map/ppermute | solution.py:353
  76.7 9.6 %collective-permute-start.16 = (f32[16,32,128]{2,1,0:T(8,128)S(1)}, f32[16,32,128]{2,1,0:T(8,128)S(1)}, u32[]{:S(2)}, u32[]{:S(2)}) collective-permute-start(f32[16,32,128]{2,1,0:T(8,128)S(1)} %get-tuple-element.33), channel_id=1, source_target_pairs={{97,288},{98,289},{99,290},{100,291},{101,292},{102,293},{103,294}... | collective-permute-start | bytes 786440 | tf_op jit(solution)/shard_map/ppermute | solution.py:353
  77.5 8.8 %collective-permute-start.14 = (f32[16,32,128]{2,1,0:T(8,128)S(1)}, f32[16,32,128]{2,1,0:T(8,128)S(1)}, u32[]{:S(2)}, u32[]{:S(2)}) collective-permute-start(f32[16,32,128]{2,1,0:T(8,128)S(1)} %get-tuple-element.33), channel_id=1, source_target_pairs={{96,289},{97,290},{98,291},{99,292},{100,293},{101,294},{102,295},... | collective-permute-start | bytes 786440 | tf_op jit(solution)/shard_map/ppermute | solution.py:353
  78.2 6.7 %collective-permute-start.10 = (f32[8,32,128]{2,1,0:T(8,128)S(1)}, f32[8,32,128]{2,1,0:T(8,128)S(1)}, u32[]{:S(2)}, u32[]{:S(2)}) collective-permute-start(f32[8,32,128]{2,1,0:T(8,128)S(1)} %shard_map.55), channel_id=1, source_target_pairs={{0,32},{1,33},{2,34},{3,35},{4,36},{5,37},{6,38},{7,39},{8,40},{9,... | collective-permute-start | bytes 393224 | tf_op jit(solution)/shard_map/ppermute | solution.py:353
  89.1 3.1 %collective-permute-start.17 = (f32[36,32,128]{2,1,0:T(8,128)S(1)}, f32[36,32,128]{2,1,0:T(8,128)S(1)}, u32[]{:S(2)}, u32[]{:S(2)}) collective-permute-start(f32[36,32,128]{2,1,0:T(8,128)S(1)} %shard_map.66.refs_0_), channel_id=1, source_target_pairs={{288,480},{289,481},{290,482},{291,483},{292,484},{293,485},{294,4... | collective-permute-start | bytes 1769480 | tf_op jit(solution)/shard_map/ppermute | solution.py:353
  91.5 6.2 %collective-permute-start.18 = (f32[3,8,32,128]{3,2,1,0:T(8,128)S(1)}, f32[3,8,32,128]{3,2,1,0:T(8,128)S(1)}, u32[]{:S(2)}, u32[]{:S(2)}) collective-permute-start(f32[3,8,32,128]{3,2,1,0:T(8,128)S(1)} %shard_map.70), channel_id=1, source_target_pairs={{288,384},{289,385},{290,386},{291,387},{292,388},{293,389},{294,3... | collective-permute-start | bytes 1179656 | tf_op jit(solution)/shard_map/ppermute | solution.py:353
  92.6 5.1 %collective-permute-start.19 = (f32[3,8,32,128]{3,2,1,0:T(8,128)S(1)}, f32[3,8,32,128]{3,2,1,0:T(8,128)S(1)}, u32[]{:S(2)}, u32[]{:S(2)}) collective-permute-start(f32[3,8,32,128]{3,2,1,0:T(8,128)S(1)} %shard_map.71), channel_id=1, source_target_pairs={{288,352},{289,353},{290,354},{291,355},{292,356},{293,357},{294,3... | collective-permute-start | bytes 1179656 | tf_op jit(solution)/shard_map/ppermute | solution.py:353
  93.6 4.1 %collective-permute-start.20 = (f32[3,8,32,128]{3,2,1,0:T(8,128)S(1)}, f32[3,8,32,128]{3,2,1,0:T(8,128)S(1)}, u32[]{:S(2)}, u32[]{:S(2)}) collective-permute-start(f32[3,8,32,128]{3,2,1,0:T(8,128)S(1)} %shard_map.72), channel_id=1, source_target_pairs={{288,256},{289,257},{290,258},{291,259},{292,260},{293,261},{294,2... | collective-permute-start | bytes 1179656 | tf_op jit(solution)/shard_map/ppermute | solution.py:353
  94.9 2.9 %collective-permute-start.22 = (f32[3,8,32,128]{3,2,1,0:T(8,128)S(1)}, f32[3,8,32,128]{3,2,1,0:T(8,128)S(1)}, u32[]{:S(2)}, u32[]{:S(2)}) collective-permute-start(f32[3,8,32,128]{3,2,1,0:T(8,128)S(1)} %shard_map.74), channel_id=1, source_target_pairs={{480,448},{481,449},{482,450},{483,451},{484,452},{485,453},{486,4... | collective-permute-start | bytes 1179656 | tf_op jit(solution)/shard_map/ppermute | solution.py:353
  96.2 35.4 %collective-permute-start.21 = (f32[3,8,32,128]{3,2,1,0:T(8,128)S(1)}, f32[3,8,32,128]{3,2,1,0:T(8,128)S(1)}, u32[]{:S(2)}, u32[]{:S(2)}) collective-permute-start(f32[3,8,32,128]{3,2,1,0:T(8,128)S(1)} %shard_map.73), channel_id=1, source_target_pairs={{480,416},{481,417},{482,418},{483,419},{484,420},{485,421},{486,4... | collective-permute-start | bytes 1179656 | tf_op jit(solution)/shard_map/ppermute | solution.py:353

commit v5 on v4

--- a/solution.py
+++ b/solution.py
@@ -102,7 +102,10 @@
     hk, hc, c0, c1, s = (load4(tabs, i, at) for i in range(5))
     inc_t, inc_p, inc_w = [], [], []
     for r in range(4):
-        warm = 1.0 / (1.5 + jnp.tanh(here_t[r]))
+        base = 1.5 + jnp.tanh(here_t[r])
+        warm = pl.reciprocal(base, approx=True)
+        warm = warm * (2.0 - base * warm)
+        warm = warm * (2.0 - base * warm)
         x = s[r] - 0.5 * here_w[r]
         soft = jnp.maximum(x, 0.0) + LN2 * jnp.log2(1.0 + jnp.exp2(-LOG2E * jnp.abs(x)))
         flow = jnp.exp2(c0[r] - c1[r] * warm) * soft

time: 134 us -> 135 us (level)
  Pallas kernels: 20 us -> 21.6 us
    pallas_call x26, Pallas kernels: 20 us -> 21.6 us  [call(): pl.pallas_call(kernel, out_shape=[jax.ShapeDtypeStruct(s, F32) for s in o...]
  transfers between devices with their start and end apart: 23 -> 23, of which waited for: 9 -> 9; matrix products, arithmetic and copies ran while one was open for 0% -> 0% of each run, Pallas kernels for 5% -> 6%
where the time goes in v5:
time: 135 us
  waiting for transfers between devices  69.8 us (52%)
  starting transfers between devices  40.2 us (30%)
  Pallas kernels  21.6 us (16%)
  other arithmetic  2.1 us (2%)
    ppermute x23, waiting for transfers between devices, sent(): return lax.ppermute(x, both, pairs)  69.8 us
    ppermute x23, starting transfers between devices, sent(): return lax.ppermute(x, both, pairs)  40.2 us
    pallas_call x26, Pallas kernels, call(): pl.pallas_call(kernel, out_shape=[jax.ShapeDtypeStruct(s, F32) for s in o...  21.6 us
  transfers between devices with their start and end apart: 23, of which 9 were waited for; matrix products, arithmetic and copies ran while one was open for 0% of the time, Pallas kernels for 6%

profile of v5, /device:TPU:55, one launch (start us, length us, event | category | flops | bytes accessed | tf_op | source)
XLA Modules:
  0.0 134.8 jit_solution(13868792295295590617)
XLA Ops:
  0.6 0.9 convert_bitcast_fusion
  1.6 1.1 bitcast_select_fusion
  2.7 11.7 %collective-permute-start.2 = (f32[3,8,32,128]{3,2,1,0:T(8,128)S(1)}, f32[3,8,32,128]{3,2,1,0:T(8,128)S(1)}, u32[]{:S(2)}, u32[]{:S(2)}) collective-permute-start(f32[3,8,32,128]{3,2,1,0:T(8,128)S(1)} %pad_maximum_fusion.soil), channel_id=1, source_target_pairs={{1,32},{2,33},{3,34},{4,35},{5,36},{6,37},{7,38},{8,39},{9,40},{10... | collective-permute-start | bytes 1179656 | tf_op jit(solution)/shard_map/ppermute | solution.py:356
  14.5 1.9 %collective-permute-start.1 = (f32[3,8,32,128]{3,2,1,0:T(8,128)S(1)}, f32[3,8,32,128]{3,2,1,0:T(8,128)S(1)}, u32[]{:S(2)}, u32[]{:S(2)}) collective-permute-start(f32[3,8,32,128]{3,2,1,0:T(8,128)S(1)} %pad_maximum_fusion.soil), channel_id=1, source_target_pairs={{0,33},{1,34},{2,35},{3,36},{4,37},{5,38},{6,39},{7,40},{8,41},{9,... | collective-permute-start | bytes 1179656 | tf_op jit(solution)/shard_map/ppermute | solution.py:356
  16.6 9.7 %collective-permute-done.centre = f32[2,8,32,128]{3,2,1,0:T(8,128)S(1)} collective-permute-done((f32[2,8,32,128]{3,2,1,0:T(8,128)S(1)}, f32[2,8,32,128]{3,2,1,0:T(8,128)S(1)}, u32[]{:S(2)}, u32[]{:S(2)}) %collective-permute-start) | collective-permute-done | bytes 262176 | tf_op jit(solution)/shard_map/ppermute | solution.py:356
  26.3 3.5 %collective-permute-done.1.left = f32[3,8,32,128]{3,2,1,0:T(8,128)S(1)} collective-permute-done((f32[3,8,32,128]{3,2,1,0:T(8,128)S(1)}, f32[3,8,32,128]{3,2,1,0:T(8,128)S(1)}, u32[]{:S(2)}, u32[]{:S(2)}) %collective-permute-start.1) | collective-permute-done | bytes 393248 | tf_op jit(solution)/shard_map/ppermute | solution.py:356
  29.8 4.6 %shard_map.50 = (f32[2,8,32,128]{3,2,1,0:T(8,128)S(1)}, f32[32,8,128]{2,1,0:T(8,128)S(1)}, f32[5,96,8,128]{3,2,1,0:T(8,128)S(1)}) custom-call(s32[2]{0:T(128)S(1)} %pad_add_fusion.place, f32[2,8,32,128]{3,2,1,0:T(8,128)S(1)} %collective-permute-done.centre, f32[3,8,32,128]{3,2,1,0:T(8,128)S(1)} %collective-permute-done.1.left, ...), custom_call_target="tpu_custom_call" | custom-call | flops 1 | bytes 1 | tf_op jit(solution)/shard_map/pallas_call | solution.py:334
  34.5 1.9 %collective-permute-start.4 = (f32[2,8,32,128]{3,2,1,0:T(8,128)S(1)}, f32[2,8,32,128]{3,2,1,0:T(8,128)S(1)}, u32[]{:S(2)}, u32[]{:S(2)}) collective-permute-start(f32[2,8,32,128]{3,2,1,0:T(8,128)S(1)} %get-tuple-element.19.centre.kept), channel_id=1, source_target_pairs={{1,0},{2,1},{3,2},{4,3},{5,4},{6,5},{7,6},{8,7},{9,8},{10,9},{11,1... | collective-permute-start | bytes 786440 | tf_op jit(solution)/shard_map/ppermute | solution.py:356
  36.4 3.4 %collective-permute-start.3 = (f32[2,8,32,128]{3,2,1,0:T(8,128)S(1)}, f32[2,8,32,128]{3,2,1,0:T(8,128)S(1)}, u32[]{:S(2)}, u32[]{:S(2)}) collective-permute-start(f32[2,8,32,128]{3,2,1,0:T(8,128)S(1)} %get-tuple-element.19.centre.kept), channel_id=1, source_target_pairs={{0,1},{1,2},{2,3},{3,4},{4,5},{5,6},{6,7},{7,8},{8,9},{9,10},{10,1... | collective-permute-start | bytes 786440 | tf_op jit(solution)/shard_map/ppermute | solution.py:356
  39.8 4.1 %collective-permute-done.4.right = f32[2,8,32,128]{3,2,1,0:T(8,128)S(1)} collective-permute-done((f32[2,8,32,128]{3,2,1,0:T(8,128)S(1)}, f32[2,8,32,128]{3,2,1,0:T(8,128)S(1)}, u32[]{:S(2)}, u32[]{:S(2)}) %collective-permute-start.4) | collective-permute-done | bytes 262176 | tf_op jit(solution)/shard_map/ppermute | solution.py:356
  43.8 4.3 %collective-permute-done.3.left = f32[2,8,32,128]{3,2,1,0:T(8,128)S(1)} collective-permute-done((f32[2,8,32,128]{3,2,1,0:T(8,128)S(1)}, f32[2,8,32,128]{3,2,1,0:T(8,128)S(1)}, u32[]{:S(2)}, u32[]{:S(2)}) %collective-permute-start.3) | collective-permute-done | bytes 262176 | tf_op jit(solution)/shard_map/ppermute | solution.py:356
  48.1 4.3 %shard_map.51 = (f32[2,8,32,128]{3,2,1,0:T(8,128)S(1)}, f32[2,7,32,128]{3,2,1,0:T(8,128)S(1)}, f32[2,7,32,128]{3,2,1,0:T(8,128)S(1)}, f32[8,32,128]{2,1,0:T(8,128)S(1)}) custom-call(s32[2]{0:T(128)S(1)} %pad_add_fusion.place, f32[2,8,32,128]{3,2,1,0:T(8,128)S(1)} %get-tuple-element.19.centre.kept, f32[2,8,32,128]{3,2,1,0:T(8,128)S(1)} %collective-permute-done.3.left, ...), custom_call_target="tpu_custom_call" | custom-call | flops 1 | bytes 1 | tf_op jit(solution)/shard_map/pallas_call | solution.py:334
  52.4 1.9 %collective-permute-start.5 = (f32[2,7,32,128]{3,2,1,0:T(8,128)S(1)}, f32[2,7,32,128]{3,2,1,0:T(8,128)S(1)}, u32[]{:S(2)}, u32[]{:S(2)}) collective-permute-start(f32[2,7,32,128]{3,2,1,0:T(8,128)S(1)} %get-tuple-element.22), channel_id=1, source_target_pairs={{0,1},{1,2},{2,3},{3,4},{4,5},{5,6},{6,7},{7,8},{8,9},{9,10},{10,1... | collective-permute-start | bytes 688136 | tf_op jit(solution)/shard_map/ppermute | solution.py:356
  54.3 5.5 %collective-permute-start.6 = (f32[2,7,32,128]{3,2,1,0:T(8,128)S(1)}, f32[2,7,32,128]{3,2,1,0:T(8,128)S(1)}, u32[]{:S(2)}, u32[]{:S(2)}) collective-permute-start(f32[2,7,32,128]{3,2,1,0:T(8,128)S(1)} %get-tuple-element.24), channel_id=1, source_target_pairs={{1,0},{2,1},{3,2},{4,3},{5,4},{6,5},{7,6},{8,7},{9,8},{10,9},{11,1... | collective-permute-start | bytes 688136 | tf_op jit(solution)/shard_map/ppermute | solution.py:356
  59.8 2.7 %collective-permute-done.5.left = f32[2,7,32,128]{3,2,1,0:T(8,128)S(1)} collective-permute-done((f32[2,7,32,128]{3,2,1,0:T(8,128)S(1)}, f32[2,7,32,128]{3,2,1,0:T(8,128)S(1)}, u32[]{:S(2)}, u32[]{:S(2)}) %collective-permute-start.5) | collective-permute-done | bytes 229408 | tf_op jit(solution)/shard_map/ppermute | solution.py:356
  62.5 0.9 collective-permute-done.6.right
  63.6 0.7 collective-permute-start.8
  64.3 0.7 collective-permute-start.9
  65.0 0.7 collective-permute-start.7
  65.8 0.7 collective-permute-start.11
  66.5 1.3 collective-permute-start.12
  67.8 0.9 collective-permute-start.13
  70.8 5.5 %collective-permute-done.12.defect = f32[28,32,128]{2,1,0:T(8,128)S(1)} collective-permute-done((f32[28,32,128]{2,1,0:T(8,128)S(1)}, f32[28,32,128]{2,1,0:T(8,128)S(1)}, u32[]{:S(2)}, u32[]{:S(2)}) %collective-permute-start.12) | collective-permute-done | bytes 458784 | tf_op jit(solution)/shard_map/ppermute | solution.py:356
  77.0 0.7 collective-permute-start.15
  79.1 1.9 %collective-permute-start.10 = (f32[8,32,128]{2,1,0:T(8,128)S(1)}, f32[8,32,128]{2,1,0:T(8,128)S(1)}, u32[]{:S(2)}, u32[]{:S(2)}) collective-permute-start(f32[8,32,128]{2,1,0:T(8,128)S(1)} %shard_map.55), channel_id=1, source_target_pairs={{0,32},{1,33},{2,34},{3,35},{4,36},{5,37},{6,38},{7,39},{8,40},{9,... | collective-permute-start | bytes 393224 | tf_op jit(solution)/shard_map/ppermute | solution.py:356
  81.0 4.8 %collective-permute-done.10.start_p = f32[8,32,128]{2,1,0:T(8,128)S(1)} collective-permute-done((f32[8,32,128]{2,1,0:T(8,128)S(1)}, f32[8,32,128]{2,1,0:T(8,128)S(1)}, u32[]{:S(2)}, u32[]{:S(2)}) %collective-permute-start.10) | collective-permute-done | bytes 131104 | tf_op jit(solution)/shard_map/ppermute | solution.py:356
  85.8 1.3 shard_map.56
  87.2 0.7 shard_map.62.state.refs_0_
  90.3 0.7 collective-permute-start.17
  97.4 1.3 collective-permute-start.21
  99.1 34.3 %collective-permute-done.21.refs_6_ = f32[3,8,32,128]{3,2,1,0:T(8,128)S(1)} collective-permute-done((f32[3,8,32,128]{3,2,1,0:T(8,128)S(1)}, f32[3,8,32,128]{3,2,1,0:T(8,128)S(1)}, u32[]{:S(2)}, u32[]{:S(2)}) %collective-permute-start.21) | collective-permute-done | bytes 393248 | tf_op jit(solution)/shard_map/ppermute | solution.py:356
  133.4 1.4 %shard_map.75 = f32[3,8,32,128]{3,2,1,0:T(8,128)} custom-call(s32[2]{0:T(128)S(1)} %pad_add_fusion.place, f32[3,8,32,128]{3,2,1,0:T(8,128)S(1)} %get-tuple-element.29.rest_0_.relaxed, f32[40,32,128]{2,1,0:T(8,128)S(1)} %shard_map.54.wait.state.refs_0_, f32[48,32,128]{2,1,0:T(8,128)S(1)} %shard_map.63.state.refs_1_, f32[24,32,128]{2,1,0:T(8,128)S(1)} %shard_map.69.refs_2_, ...), custom_call_target="tpu_custom_call" | custom-call | flops 1 | bytes 1 | tf_op jit(solution)/shard_map/pallas_call | solution.py:334
  (48 shorter events, 13.6 us)
Async XLA Ops:
  2.6 45.5 %copy-start = (f32[3,8,32,128]{3,2,1,0:T(8,128)S(1)}, f32[3,8,32,128]{3,2,1,0:T(8,128)}, u32[]{:S(2)}) copy-start(f32[3,8,32,128]{3,2,1,0:T(8,128)} %first_p.1) | copy-start | bytes 1179652
  2.7 23.6 %collective-permute-start.2 = (f32[3,8,32,128]{3,2,1,0:T(8,128)S(1)}, f32[3,8,32,128]{3,2,1,0:T(8,128)S(1)}, u32[]{:S(2)}, u32[]{:S(2)}) collective-permute-start(f32[3,8,32,128]{3,2,1,0:T(8,128)S(1)} %pad_maximum_fusion.soil), channel_id=1, source_target_pairs={{1,32},{2,33},{3,34},{4,35},{5,36},{6,37},{7,38},{8,39},{9,40},{10... | collective-permute-start | bytes 1179656 | tf_op jit(solution)/shard_map/ppermute | solution.py:356
  14.5 15.3 %collective-permute-start.1 = (f32[3,8,32,128]{3,2,1,0:T(8,128)S(1)}, f32[3,8,32,128]{3,2,1,0:T(8,128)S(1)}, u32[]{:S(2)}, u32[]{:S(2)}) collective-permute-start(f32[3,8,32,128]{3,2,1,0:T(8,128)S(1)} %pad_maximum_fusion.soil), channel_id=1, source_target_pairs={{0,33},{1,34},{2,35},{3,36},{4,37},{5,38},{6,39},{7,40},{8,41},{9,... | collective-permute-start | bytes 1179656 | tf_op jit(solution)/shard_map/ppermute | solution.py:356
  16.4 9.9 %collective-permute-start = (f32[2,8,32,128]{3,2,1,0:T(8,128)S(1)}, f32[2,8,32,128]{3,2,1,0:T(8,128)S(1)}, u32[]{:S(2)}, u32[]{:S(2)}) collective-permute-start(f32[2,8,32,128]{3,2,1,0:T(8,128)S(1)} %pad_maximum_fusion.1), channel_id=1, source_target_pairs={{0,32},{1,33},{2,34},{3,35},{4,36},{5,37},{6,38},{7,39},{8,40},{9,... | collective-permute-start | bytes 786440 | tf_op jit(solution)/shard_map/ppermute | solution.py:356
  34.5 9.4 %collective-permute-start.4 = (f32[2,8,32,128]{3,2,1,0:T(8,128)S(1)}, f32[2,8,32,128]{3,2,1,0:T(8,128)S(1)}, u32[]{:S(2)}, u32[]{:S(2)}) collective-permute-start(f32[2,8,32,128]{3,2,1,0:T(8,128)S(1)} %get-tuple-element.19.centre.kept), channel_id=1, source_target_pairs={{1,0},{2,1},{3,2},{4,3},{5,4},{6,5},{7,6},{8,7},{9,8},{10,9},{11,1... | collective-permute-start | bytes 786440 | tf_op jit(solution)/shard_map/ppermute | solution.py:356
  36.4 11.7 %collective-permute-start.3 = (f32[2,8,32,128]{3,2,1,0:T(8,128)S(1)}, f32[2,8,32,128]{3,2,1,0:T(8,128)S(1)}, u32[]{:S(2)}, u32[]{:S(2)}) collective-permute-start(f32[2,8,32,128]{3,2,1,0:T(8,128)S(1)} %get-tuple-element.19.centre.kept), channel_id=1, source_target_pairs={{0,1},{1,2},{2,3},{3,4},{4,5},{5,6},{6,7},{7,8},{8,9},{9,10},{10,1... | collective-permute-start | bytes 786440 | tf_op jit(solution)/shard_map/ppermute | solution.py:356
  52.4 10.1 %collective-permute-start.5 = (f32[2,7,32,128]{3,2,1,0:T(8,128)S(1)}, f32[2,7,32,128]{3,2,1,0:T(8,128)S(1)}, u32[]{:S(2)}, u32[]{:S(2)}) collective-permute-start(f32[2,7,32,128]{3,2,1,0:T(8,128)S(1)} %get-tuple-element.22), channel_id=1, source_target_pairs={{0,1},{1,2},{2,3},{3,4},{4,5},{5,6},{6,7},{7,8},{8,9},{9,10},{10,1... | collective-permute-start | bytes 688136 | tf_op jit(solution)/shard_map/ppermute | solution.py:356
  54.3 9.0 %collective-permute-start.6 = (f32[2,7,32,128]{3,2,1,0:T(8,128)S(1)}, f32[2,7,32,128]{3,2,1,0:T(8,128)S(1)}, u32[]{:S(2)}, u32[]{:S(2)}) collective-permute-start(f32[2,7,32,128]{3,2,1,0:T(8,128)S(1)} %get-tuple-element.24), channel_id=1, source_target_pairs={{1,0},{2,1},{3,2},{4,3},{5,4},{6,5},{7,6},{8,7},{9,8},{10,9},{11,1... | collective-permute-start | bytes 688136 | tf_op jit(solution)/shard_map/ppermute | solution.py:356
  63.6 4.2 %collective-permute-start.8 = (f32[44,32,128]{2,1,0:T(8,128)S(1)}, f32[44,32,128]{2,1,0:T(8,128)S(1)}, u32[]{:S(2)}, u32[]{:S(2)}) collective-permute-start(f32[44,32,128]{2,1,0:T(8,128)S(1)} %get-tuple-element.27.defect), channel_id=1, source_target_pairs={{32,96},{33,97},{34,98},{35,99},{36,100},{37,101},{38,102},{39,103... | collective-permute-start | bytes 2162696 | tf_op jit(solution)/shard_map/ppermute | solution.py:356
  64.3 5.0 %collective-permute-start.9 = (f32[52,32,128]{2,1,0:T(8,128)S(1)}, f32[52,32,128]{2,1,0:T(8,128)S(1)}, u32[]{:S(2)}, u32[]{:S(2)}) collective-permute-start(f32[52,32,128]{2,1,0:T(8,128)S(1)} %get-tuple-element.28), channel_id=1, source_target_pairs={{64,96},{65,97},{66,98},{67,99},{68,100},{69,101},{70,102},{71,103... | collective-permute-start | bytes 2555912 | tf_op jit(solution)/shard_map/ppermute | solution.py:356
  65.0 3.6 %collective-permute-start.7 = (f32[48,32,128]{2,1,0:T(8,128)S(1)}, f32[48,32,128]{2,1,0:T(8,128)S(1)}, u32[]{:S(2)}, u32[]{:S(2)}) collective-permute-start(f32[48,32,128]{2,1,0:T(8,128)S(1)} %get-tuple-element.26), channel_id=1, source_target_pairs={{0,96},{1,97},{2,98},{3,99},{4,100},{5,101},{6,102},{7,103},{8,104... | collective-permute-start | bytes 2359304 | tf_op jit(solution)/shard_map/ppermute | solution.py:356
  65.8 4.6 %collective-permute-start.11 = (f32[36,32,128]{2,1,0:T(8,128)S(1)}, f32[36,32,128]{2,1,0:T(8,128)S(1)}, u32[]{:S(2)}, u32[]{:S(2)}) collective-permute-start(f32[36,32,128]{2,1,0:T(8,128)S(1)} %get-tuple-element.30.defect), channel_id=1, source_target_pairs={{128,96},{129,97},{130,98},{131,99},{132,100},{133,101},{134,102},... | collective-permute-start | bytes 1769480 | tf_op jit(solution)/shard_map/ppermute | solution.py:356
  66.5 9.9 %collective-permute-start.12 = (f32[28,32,128]{2,1,0:T(8,128)S(1)}, f32[28,32,128]{2,1,0:T(8,128)S(1)}, u32[]{:S(2)}, u32[]{:S(2)}) collective-permute-start(f32[28,32,128]{2,1,0:T(8,128)S(1)} %get-tuple-element.31), channel_id=1, source_target_pairs={{160,96},{161,97},{162,98},{163,99},{164,100},{165,101},{166,102},... | collective-permute-start | bytes 1376264 | tf_op jit(solution)/shard_map/ppermute | solution.py:356
  67.8 8.9 %collective-permute-start.13 = (f32[24,32,128]{2,1,0:T(8,128)S(1)}, f32[24,32,128]{2,1,0:T(8,128)S(1)}, u32[]{:S(2)}, u32[]{:S(2)}) collective-permute-start(f32[24,32,128]{2,1,0:T(8,128)S(1)} %get-tuple-element.32.refs_3_), channel_id=1, source_target_pairs={{192,96},{193,97},{194,98},{195,99},{196,100},{197,101},{198,102},... | collective-permute-start | bytes 1179656 | tf_op jit(solution)/shard_map/ppermute | solution.py:356
  77.0 10.2 %collective-permute-start.15 = (f32[24,32,128]{2,1,0:T(8,128)S(1)}, f32[24,32,128]{2,1,0:T(8,128)S(1)}, u32[]{:S(2)}, u32[]{:S(2)}) collective-permute-start(f32[24,32,128]{2,1,0:T(8,128)S(1)} %get-tuple-element.34.refs_1_), channel_id=1, source_target_pairs={{96,288},{97,289},{98,290},{99,291},{100,292},{101,293},{102,294},... | collective-permute-start | bytes 1179656 | tf_op jit(solution)/shard_map/ppermute | solution.py:356
  77.7 9.5 %collective-permute-start.16 = (f32[16,32,128]{2,1,0:T(8,128)S(1)}, f32[16,32,128]{2,1,0:T(8,128)S(1)}, u32[]{:S(2)}, u32[]{:S(2)}) collective-permute-start(f32[16,32,128]{2,1,0:T(8,128)S(1)} %get-tuple-element.33), channel_id=1, source_target_pairs={{97,288},{98,289},{99,290},{100,291},{101,292},{102,293},{103,294}... | collective-permute-start | bytes 786440 | tf_op jit(solution)/shard_map/ppermute | solution.py:356
  78.4 8.8 %collective-permute-start.14 = (f32[16,32,128]{2,1,0:T(8,128)S(1)}, f32[16,32,128]{2,1,0:T(8,128)S(1)}, u32[]{:S(2)}, u32[]{:S(2)}) collective-permute-start(f32[16,32,128]{2,1,0:T(8,128)S(1)} %get-tuple-element.33), channel_id=1, source_target_pairs={{96,289},{97,290},{98,291},{99,292},{100,293},{101,294},{102,295},... | collective-permute-start | bytes 786440 | tf_op jit(solution)/shard_map/ppermute | solution.py:356
  79.1 6.7 %collective-permute-start.10 = (f32[8,32,128]{2,1,0:T(8,128)S(1)}, f32[8,32,128]{2,1,0:T(8,128)S(1)}, u32[]{:S(2)}, u32[]{:S(2)}) collective-permute-start(f32[8,32,128]{2,1,0:T(8,128)S(1)} %shard_map.55), channel_id=1, source_target_pairs={{0,32},{1,33},{2,34},{3,35},{4,36},{5,37},{6,38},{7,39},{8,40},{9,... | collective-permute-start | bytes 393224 | tf_op jit(solution)/shard_map/ppermute | solution.py:356
  90.3 3.1 %collective-permute-start.17 = (f32[36,32,128]{2,1,0:T(8,128)S(1)}, f32[36,32,128]{2,1,0:T(8,128)S(1)}, u32[]{:S(2)}, u32[]{:S(2)}) collective-permute-start(f32[36,32,128]{2,1,0:T(8,128)S(1)} %shard_map.66.refs_0_), channel_id=1, source_target_pairs={{288,480},{289,481},{290,482},{291,483},{292,484},{293,485},{294,4... | collective-permute-start | bytes 1769480 | tf_op jit(solution)/shard_map/ppermute | solution.py:356
  92.7 6.3 %collective-permute-start.18 = (f32[3,8,32,128]{3,2,1,0:T(8,128)S(1)}, f32[3,8,32,128]{3,2,1,0:T(8,128)S(1)}, u32[]{:S(2)}, u32[]{:S(2)}) collective-permute-start(f32[3,8,32,128]{3,2,1,0:T(8,128)S(1)} %shard_map.70), channel_id=1, source_target_pairs={{288,384},{289,385},{290,386},{291,387},{292,388},{293,389},{294,3... | collective-permute-start | bytes 1179656 | tf_op jit(solution)/shard_map/ppermute | solution.py:356
  93.8 5.2 %collective-permute-start.19 = (f32[3,8,32,128]{3,2,1,0:T(8,128)S(1)}, f32[3,8,32,128]{3,2,1,0:T(8,128)S(1)}, u32[]{:S(2)}, u32[]{:S(2)}) collective-permute-start(f32[3,8,32,128]{3,2,1,0:T(8,128)S(1)} %shard_map.71), channel_id=1, source_target_pairs={{288,352},{289,353},{290,354},{291,355},{292,356},{293,357},{294,3... | collective-permute-start | bytes 1179656 | tf_op jit(solution)/shard_map/ppermute | solution.py:356
  94.9 4.2 %collective-permute-start.20 = (f32[3,8,32,128]{3,2,1,0:T(8,128)S(1)}, f32[3,8,32,128]{3,2,1,0:T(8,128)S(1)}, u32[]{:S(2)}, u32[]{:S(2)}) collective-permute-start(f32[3,8,32,128]{3,2,1,0:T(8,128)S(1)} %shard_map.72), channel_id=1, source_target_pairs={{288,256},{289,257},{290,258},{291,259},{292,260},{293,261},{294,2... | collective-permute-start | bytes 1179656 | tf_op jit(solution)/shard_map/ppermute | solution.py:356
  96.2 2.9 %collective-permute-start.22 = (f32[3,8,32,128]{3,2,1,0:T(8,128)S(1)}, f32[3,8,32,128]{3,2,1,0:T(8,128)S(1)}, u32[]{:S(2)}, u32[]{:S(2)}) collective-permute-start(f32[3,8,32,128]{3,2,1,0:T(8,128)S(1)} %shard_map.74), channel_id=1, source_target_pairs={{480,448},{481,449},{482,450},{483,451},{484,452},{485,453},{486,4... | collective-permute-start | bytes 1179656 | tf_op jit(solution)/shard_map/ppermute | solution.py:356
  97.4 36.0 %collective-permute-start.21 = (f32[3,8,32,128]{3,2,1,0:T(8,128)S(1)}, f32[3,8,32,128]{3,2,1,0:T(8,128)S(1)}, u32[]{:S(2)}, u32[]{:S(2)}) collective-permute-start(f32[3,8,32,128]{3,2,1,0:T(8,128)S(1)} %shard_map.73), channel_id=1, source_target_pairs={{480,416},{481,417},{482,418},{483,419},{484,420},{485,421},{486,4... | collective-permute-start | bytes 1179656 | tf_op jit(solution)/shard_map/ppermute | solution.py:356
